TPU v7x, 1024 devices: a whole 8x8x8 slice. The times are simulated.
1024 devices in a mesh: sec: 4 (over y_lo, core), row: 8 (over x), col: 32 (over y_hi, z).
Axes of the slice: x: 8, y: 8 (y_hi: 4, y_lo: 2; y = y_hi * 2 + y_lo), z: 8, core: 2. Of those that a mesh axis runs over, the one named last changes fastest.
Arguments:
- gas_field: float32 [4, 32, 64, 1024], P('sec', 'row', 'col'), may hold values from -6 to 6
- parcel_state: float32 [4, 1048576], P('sec', ('row', 'col')), may hold values from -6 to 6
- parcel_mass: float32 [1048576], P(('row', 'col')), may hold values from 0.5 to 2
- base_time: float32 [1048576], P(('row', 'col')), may hold values from 0.5 to 4
- evap_rate: float32 [1048576], P(('row', 'col')), may hold values from 0.1 to 1
- slot_blocks: int32 [256, 32, 4], P(('row', 'col')), may hold values from 0 to 63
- parcel_block_slot: int32 [1048576], P(('row', 'col')), may hold values from 0 to 127
- parcel_cell: int32 [1048576], P(('row', 'col')), may hold values from 0 to 127
- parcel_count: int32 [256], P(('row', 'col')), may hold values from 1024 to 4096, as said below
Outputs:
- gas_out: float32 [4, 32, 64, 1024], P('sec', 'row', 'col')
- parcel_out: float32 [4, 1048576], P('sec', ('row', 'col'))
- mass_out: float32 [1048576], P(('row', 'col'))
Inputs may be any that keep to these rules, and one draw needn't show every extreme that they name: `slot_blocks`: local block indices of the owner; repeats allowed. `parcel_count`: some parcel block is full, with exactly 4096 live rows.
All inputs are finite; a program needn't handle non-finite values.
Results may differ from a plain program's by a relative error of at most 0.0015.
Values may be sent and summed in bfloat16 or wider, within the bound.
No kernel may reach another device: no remote copies, remote signals or barrier semaphores. Data moves between devices by JAX's collectives and lax.ppermute only.
A program may use at most 32 MiB of HBM per device.

v0:
```python
import jax
import jax.numpy as jnp
from jax import lax
from jax.sharding import PartitionSpec as P

ITERS = 4


LATENT = 2.0
DEPOSIT_MODE = 0.5
ADVECT = 0.3
DIFFUSE = 0.2


def transport(current_gas):
    left = jnp.concatenate([current_gas[..., :1], current_gas[..., :-1]], axis=-1)
    right = jnp.concatenate([current_gas[..., 1:], current_gas[..., -1:]], axis=-1)
    return (
        current_gas + ADVECT * (left - current_gas) + DIFFUSE * (right - 2.0 * current_gas + left)
    )


def contract_first(left_side, right_side):
    return lax.dot_general(
        left_side,
        right_side,
        (((0,), (0,)), ((), ())),
        precision=lax.Precision.HIGHEST,
        preferred_element_type=jnp.float32,
    )


def shards(
    gas_field,
    parcel_state,
    parcel_mass,
    base_time,
    evap_rate,
    slot_blocks,
    parcel_block_slot,
    parcel_cell,
    parcel_count,
):
    current_gas = gas_field[0]
    cells_x, cells_y, cells_z = current_gas.shape
    blocks = cells_x * cells_y * cells_z // 128
    block_lists = slot_blocks[0]
    peer_total, per_peer = block_lists.shape
    slot_total = peer_total * per_peer
    parcels = parcel_mass.shape[0]
    section = lax.axis_index("sec")
    heat_factor = jnp.where(section == 3, 1.5, 1.0).astype(jnp.float32)
    latent = jnp.where(section == 3, LATENT, 0.0).astype(jnp.float32)
    active = jnp.arange(parcels, dtype=jnp.int32) < parcel_count[0]
    slot_hot = (
        parcel_block_slot[:, None] == jnp.arange(slot_total, dtype=jnp.int32)[None, :]
    ).astype(jnp.float32)
    slot_bf = slot_hot.astype(jnp.bfloat16)
    cell_hot = (parcel_cell[:, None] == jnp.arange(128, dtype=jnp.int32)[None, :]).astype(
        jnp.float32
    )
    wanted = (jnp.arange(peer_total, dtype=jnp.int32)[:, None] * blocks + block_lists).reshape(
        slot_total
    )
    drop_state = parcel_state[0]
    drop_mass = parcel_mass
    for substep in range(ITERS):
        block_vals = current_gas.reshape(blocks, 128).astype(jnp.bfloat16)
        shard_rows = lax.all_gather(block_vals, "col", axis=0, tiled=True)
        rows_here = jnp.arange(shard_rows.shape[0], dtype=jnp.int32)
        one_hot = (wanted[:, None] == rows_here[None, :]).astype(jnp.bfloat16)
        collected = jnp.dot(one_hot, shard_rows, preferred_element_type=jnp.float32)
        slot_vals = collected.astype(jnp.bfloat16)
        values = jnp.dot(slot_bf, slot_vals, preferred_element_type=jnp.float32)
        sampled_draws = jnp.sum(values * cell_hot, axis=1)
        paired = lax.all_gather(
            jnp.stack([sampled_draws, drop_state])[None], "sec", axis=0, tiled=True
        )
        gas_temp = paired[3, 0]
        drop_temp = paired[3, 1]
        evap_now = evap_rate * jax.nn.sigmoid(gas_temp - drop_temp)
        updated_mass = jnp.where(active, drop_mass * jnp.exp(-evap_now), drop_mass)
        response_time = base_time * jnp.exp(jnp.log(drop_mass) * (2.0 / 3.0)) * heat_factor
        relaxed = sampled_draws + (drop_state - sampled_draws) * jnp.exp(-1.0 / response_time)
        new_state = jnp.where(active, relaxed, drop_state)
        source = (
            drop_mass * drop_state - updated_mass * new_state - latent * (drop_mass - updated_mass)
        )
        weighted = cell_hot * source[:, None]
        slot_source = contract_first(slot_hot, weighted)
        advected = transport(current_gas)
        spread_rows_here = jnp.arange(blocks * lax.axis_size("col"), dtype=jnp.int32)
        spread_one_hot = (wanted[:, None] == spread_rows_here[None, :]).astype(jnp.float32)
        cell_source = lax.psum_scatter(
            contract_first(spread_one_hot, slot_source), "col", scatter_dimension=0, tiled=True
        )
        current_gas = advected + DEPOSIT_MODE * cell_source.reshape(cells_x, cells_y, cells_z)
        drop_state = new_state
        drop_mass = updated_mass
    return (current_gas[None], drop_state[None], drop_mass)


def solution(mesh):
    return jax.shard_map(
        shards,
        mesh=mesh,
        in_specs=(
            P("sec", "row", "col", None),
            P("sec", ("row", "col")),
            P(("row", "col")),
            P(("row", "col")),
            P(("row", "col")),
            P(("row", "col"), None, None),
            P(("row", "col")),
            P(("row", "col")),
            P(("row", "col")),
        ),
        out_specs=(P("sec", "row", "col", None), P("sec", ("row", "col")), P(("row", "col"))),
        check_vma=False,
    )
```

profile of v0, /device:TPU:14, one launch (start us, length us, event | category | flops | bytes accessed | tf_op | source)
XLA Modules:
  0.0 1317.8 jit_solution(2320447141013342177)
XLA Ops:
  7.4 0.8 copy.50
  8.3 0.8 reshape_squeeze.3
  9.1 98.7 %all_gather.24 = bf16[2048,128]{1,0:T(8,128)(2,1)S(1)} all-gather(bf16[64,128]{1,0:T(8,128)(2,1)S(1)} %convert_element_type.41), channel_id=1, replica_groups=mesh['sec'=4,'row'=8,'col'=32] {'col'}, dimensions={0}, use_global_device_ids=true | all-gather | bytes 540672 | tf_op jit(solution)/shard_map/all_gather | solution.py:69
  107.9 1.8 fusion.13
  109.7 5.4 all-gather.4
  115.9 2.2 fusion.6
  118.1 2.0 fusion.40
  120.4 224.0 %reduce-scatter.5.cloned.1.call-done = f32[64,128]{1,0:T(8,128)} async-done(((f32[2048,128]{1,0:T(8,128)}), f32[64,128]{1,0:T(8,128)}) %reduce-scatter.5.cloned.1.call-update) | async-done | bytes 32784 | tf_op jit(solution)/shard_map/reduce_scatter | solution.py:94
  344.4 0.8 broadcast_multiply_fusion.3
  345.4 0.8 fusion.78
  346.2 83.0 %all_gather.26 = bf16[2048,128]{1,0:T(8,128)(2,1)S(1)} all-gather(bf16[64,128]{1,0:T(8,128)(2,1)S(1)} %get-tuple-element.25), channel_id=1, replica_groups=mesh['sec'=4,'row'=8,'col'=32] {'col'}, dimensions={0}, use_global_device_ids=true | all-gather | bytes 540672 | tf_op jit(solution)/shard_map/all_gather | solution.py:69
  429.2 1.0 fusion.14
  430.2 5.4 all-gather.5
  435.7 2.2 fusion.4
  437.9 2.0 fusion.39
  440.2 225.1 %reduce-scatter.7.cloned.1.call-done = f32[64,128]{1,0:T(8,128)} async-done(((f32[2048,128]{1,0:T(8,128)}), f32[64,128]{1,0:T(8,128)}) %reduce-scatter.7.cloned.1.call-update) | async-done | bytes 32784 | tf_op jit(solution)/shard_map/reduce_scatter | solution.py:94
  665.3 0.8 broadcast_multiply_fusion.2
  666.3 0.8 fusion.77
  667.1 82.0 %all_gather.28 = bf16[2048,128]{1,0:T(8,128)(2,1)S(1)} all-gather(bf16[64,128]{1,0:T(8,128)(2,1)S(1)} %get-tuple-element.16), channel_id=1, replica_groups=mesh['sec'=4,'row'=8,'col'=32] {'col'}, dimensions={0}, use_global_device_ids=true | all-gather | bytes 540672 | tf_op jit(solution)/shard_map/all_gather | solution.py:69
  749.1 1.0 fusion.15
  750.1 5.6 all-gather.6
  755.8 2.2 fusion.2
  758.0 2.0 fusion.38
  760.3 226.7 %reduce-scatter.9.cloned.1.call-done = f32[64,128]{1,0:T(8,128)} async-done(((f32[2048,128]{1,0:T(8,128)}), f32[64,128]{1,0:T(8,128)}) %reduce-scatter.9.cloned.1.call-update) | async-done | bytes 32784 | tf_op jit(solution)/shard_map/reduce_scatter | solution.py:94
  988.0 0.8 add_convert_fusion
  988.7 82.6 %all_gather.30 = bf16[2048,128]{1,0:T(8,128)(2,1)S(1)} all-gather(bf16[64,128]{1,0:T(8,128)(2,1)S(1)} %add_convert_fusion), channel_id=1, replica_groups=mesh['sec'=4,'row'=8,'col'=32] {'col'}, dimensions={0}, use_global_device_ids=true | all-gather | bytes 540672 | tf_op jit(solution)/shard_map/all_gather | solution.py:69
  1071.4 1.0 fusion.16
  1072.4 5.4 all-gather.7
  1078.5 2.2 fusion
  1080.7 2.0 fusion.37
  1084.6 225.0 %reduce-scatter.11.cloned.1.call-done = f32[64,128]{1,0:T(8,128)} async-done(((f32[2048,128]{1,0:T(8,128)}), f32[64,128]{1,0:T(8,128)}) %reduce-scatter.11.cloned.1.call-update) | async-done | bytes 32784 | tf_op jit(solution)/shard_map/reduce_scatter | solution.py:94
  1310.4 0.9 fusion.68
  (82 shorter events, 6.1 us)
Async XLA Ops:
  7.2 337.3 %reduce-scatter.5.cloned.1.call-start = ((), (), s32[]{:S(2)}) async-start(), calls=%async_computation.4 | async-start | bytes 1081344 | tf_op jit(solution)/shard_map/reduce_scatter | solution.py:94
  107.8 1.8 copy-start.3
  107.8 8.0 copy-start.1
  107.8 8.0 copy-start.2
  107.8 8.0 copy-start.4
  107.8 8.1 copy-start.5
  107.9 8.1 copy-start.6
  118.1 2.1 copy-start
  120.2 545.1 %reduce-scatter.7.cloned.1.call-start = ((), (), s32[]{:S(2)}) async-start(), calls=%async_computation.5 | async-start | bytes 1081344 | tf_op jit(solution)/shard_map/reduce_scatter | solution.py:94
  439.9 547.0 %reduce-scatter.9.cloned.1.call-start = ((), (), s32[]{:S(2)}) async-start(), calls=%async_computation.6 | async-start | bytes 1081344 | tf_op jit(solution)/shard_map/reduce_scatter | solution.py:94
  760.1 549.5 %reduce-scatter.11.cloned.1.call-start = ((), (), s32[]{:S(2)}) async-start(), calls=%async_computation.7 | async-start | bytes 1081344 | tf_op jit(solution)/shard_map/reduce_scatter | solution.py:94
Sparse Core Ops, SparseCore 0:
  120.3 224.1 reduce-scatter.4
  440.1 225.1 reduce-scatter.6
  760.2 226.7 reduce-scatter.8
  1082.9 226.6 reduce-scatter.10
where the time goes:
time: 1320 us
  waiting for transfers between devices  901 us (68%)
  blocking collectives  368 us (28%)
  matrix products  21.5 us (2%)
  between operations  14.8 us (1%)
    reduce_scatter x4, waiting for transfers between devices, shards(): lax.psum_scatter(contract_first(spread_one_hot, slot_source), 'col', scat...  901 us
    all_gather x4, blocking collectives, shards(): shard_rows = lax.all_gather(block_vals, 'col', axis=0, tiled=True)  346 us
  transfers between devices with their start and end apart: 4, of which 4 were waited for; matrix products, arithmetic and copies ran while one was open for 0% of the time, Pallas kernels for 0%

commit v1 on v0

v1 whole, which is shorter than its diff:
```python
import functools

import jax
import jax.numpy as jnp
from jax import lax
from jax.experimental import pallas as pl
from jax.experimental.pallas import tpu as pltpu
from jax.sharding import PartitionSpec as P

ITERS = 4
LATENT = 2.0
DEPOSIT_MODE = 0.5
ADVECT = 0.3
DIFFUSE = 0.2
LANES = 128
HALF = 64
VMEM_LIMIT = 32 * 1024 * 1024

F32 = jnp.float32
BF16 = jnp.bfloat16


def iota(shape, axis):
    return lax.broadcasted_iota(jnp.int32, shape, axis)


def dot(left_side, right_side, left_axis=1, right_axis=0):
    return lax.dot_general(
        left_side,
        right_side,
        (((left_axis,), (right_axis,)), ((), ())),
        preferred_element_type=F32,
    )


def halves(values):
    high = values.astype(BF16)
    return high, (values - high.astype(F32)).astype(BF16)


def split_pair(rows):
    tiles = rows.reshape(rows.shape[0] // 16, 2, 8, LANES)
    even, odd = tiles[:, 0], tiles[:, 1]
    low = iota(even.shape, 1) < 4
    first = jnp.where(low, even, pltpu.roll(odd, 4, 1))
    second = jnp.where(low, pltpu.roll(even, 4, 1), odd)
    flat = (rows.shape[0] // 2, LANES)
    return first.reshape(flat), second.reshape(flat)


def merge_pair(first, second):
    shape = (first.shape[0] // 8, 8, LANES)
    first, second = first.reshape(shape), second.reshape(shape)
    low = iota(shape, 1) < 4
    even = jnp.where(low, first, pltpu.roll(second, 4, 1))
    odd = jnp.where(low, pltpu.roll(first, 4, 1), second)
    return jnp.stack([even, odd], axis=1).reshape(2 * shape[0] * 8, LANES)


def pick_kernel(wanted_ref, gas_ref, pick_ref, place_ref, send_ref):
    wanted = wanted_ref[...].astype(F32).astype(jnp.int32)
    pick = (wanted == iota(wanted.shape, 1)).astype(F32)
    pick_ref[...] = pick.astype(BF16)
    place_ref[...] = pick.T.astype(BF16)
    send_ref[...] = dot(pick.astype(BF16), gas_ref[...].astype(BF16)).astype(BF16)


def gas_kernel(per_pencil, source_ref, gas_ref, pick_ref, place_ref, gas_out, send_ref=None):
    high, low = halves(source_ref[...])
    place = place_ref[...]
    deposit = dot(place, high) + dot(place, low)
    gas = gas_ref[...]
    rows = gas.shape[0]
    block = iota(gas.shape, 0) % per_pencil
    lane = iota(gas.shape, 1)
    to_right = pltpu.roll(gas, 1, 1)
    to_left = pltpu.roll(gas, LANES - 1, 1)
    left = jnp.where(
        lane == 0, jnp.where(block == 0, gas, pltpu.roll(to_right, 1, 0)), to_right
    )
    right = jnp.where(
        lane == LANES - 1,
        jnp.where(block == per_pencil - 1, gas, pltpu.roll(to_left, rows - 1, 0)),
        to_left,
    )
    moved = gas + ADVECT * (left - gas) + DIFFUSE * (right - 2.0 * gas + left)
    new_gas = moved + DEPOSIT_MODE * deposit
    gas_out[...] = new_gas
    if send_ref is not None:
        send_ref[...] = dot(pick_ref[...], new_gas.astype(BF16)).astype(BF16)


def parcel_kernel(
    chunk,
    count_ref,
    coef_ref,
    recv_ref,
    drop_ref,
    mass_ref,
    base_ref,
    evap_ref,
    slot_ref,
    cell_ref,
    drop_out,
    mass_out,
    send_ref,
    seen_ref,
    part_ref,
):
    lines = mass_ref.shape[0]
    slots = recv_ref.shape[0] // 2
    width = chunk * LANES

    def fold(values):
        turned = values.T
        return jnp.concatenate([turned[:HALF], turned[HALF:]], axis=1)

    own, temp = split_pair(recv_ref[...].astype(F32))
    table = jnp.concatenate([fold(own), fold(temp)], axis=0).astype(BF16)
    cell = cell_ref[...]
    upper = cell // HALF
    part_ref[4] = (slot_ref[...] + slots * upper).astype(F32)
    part_ref[5] = (cell - HALF * upper).astype(F32)

    def packed(ref, start):
        row = jnp.concatenate([ref[start + i : start + i + 1, :] for i in range(chunk)], axis=1)
        return jnp.broadcast_to(row, (16, width)).astype(BF16)[None]

    def index(count):
        shape = (count // 16, 16, width)
        return (iota(shape, 0) * 16 + iota(shape, 1)).astype(F32).astype(BF16)

    slot_index, cell_index = index(2 * slots), index(HALF)
    one, zero = jnp.ones((), BF16), jnp.zeros((), BF16)

    def masks(start):
        hot = jnp.where(slot_index == packed(part_ref.at[4], start), one, zero)
        return hot.reshape(2 * slots, width), cell_index == packed(part_ref.at[5], start)

    for start in range(0, lines, chunk):
        hot, here = masks(start)
        values = dot(table, hot).astype(BF16).reshape(2, HALF // 16, 16, width)
        for quantity in range(2):
            kept = jnp.where(here, values[quantity], zero)
            total = kept[0]
            for i in range(1, HALF // 16):
                total = total + kept[i]
            seen = jnp.sum(total.astype(F32), axis=0, keepdims=True)
            for i in range(chunk):
                seen_ref[quantity, start + i : start + i + 1, :] = seen[:, i * LANES : (i + 1) * LANES]

    shape = mass_ref.shape
    active = iota(shape, 0) * LANES + iota(shape, 1) < count_ref[0]
    mass = mass_ref[...]
    evap_now = evap_ref[...] * jax.nn.sigmoid(seen_ref[1] - drop_ref[1])
    new_mass = jnp.where(active, mass * jnp.exp(-evap_now), mass)
    mass_out[...] = new_mass
    unit_time = base_ref[...] * jnp.exp(jnp.log(mass) * (2.0 / 3.0))
    for quantity in range(2):
        heat = coef_ref[0] if quantity == 0 else 1.5
        latent = coef_ref[1] if quantity == 0 else LATENT
        seen, drop = seen_ref[quantity], drop_ref[quantity]
        relaxed = seen + (drop - seen) * jnp.exp(-1.0 / (unit_time * heat))
        new_drop = jnp.where(active, relaxed, drop)
        drop_out[quantity] = new_drop
        source = mass * drop - new_mass * new_drop - latent * (mass - new_mass)
        high = source.astype(BF16).astype(F32)
        part_ref[quantity] = high
        part_ref[2 + quantity] = source - high

    total = jnp.zeros((2 * slots, 4 * HALF), F32)
    for start in range(0, lines, chunk):
        hot, here = masks(start)
        parts = [
            jnp.where(here, packed(part_ref.at[i], start), zero).reshape(HALF, width)
            for i in range(4)
        ]
        total += dot(hot, jnp.concatenate(parts, axis=0), 1, 1)
    total = total[:, :LANES] + total[:, LANES:]
    lower, upper = total[:slots], total[slots:]
    left = iota(lower.shape, 1) < HALF
    first = jnp.where(left, lower, pltpu.roll(upper, HALF, 1))
    second = jnp.where(left, pltpu.roll(lower, HALF, 1), upper)
    send_ref[...] = merge_pair(first, second)


def call(body, out_shape, in_specs, **more):
    return pl.pallas_call(
        body,
        out_shape=out_shape,
        in_specs=in_specs,
        out_specs=jax.tree.map(lambda _: pl.BlockSpec(memory_space=pltpu.VMEM), out_shape),
        compiler_params=pltpu.CompilerParams(vmem_limit_bytes=VMEM_LIMIT),
        **more,
    )


def exchange(rows, peers):
    shape = (peers, rows.shape[0] // peers, LANES)
    return lax.all_to_all(rows.reshape(shape), "col", 0, 0, tiled=True).reshape(rows.shape)


def shards(
    gas_field,
    parcel_state,
    parcel_mass,
    base_time,
    evap_rate,
    slot_blocks,
    parcel_block_slot,
    parcel_cell,
    parcel_count,
):
    cells = gas_field.shape[1:]
    blocks = cells[0] * cells[1] * cells[2] // LANES
    per_pencil = cells[2] // LANES
    peers, per_peer = slot_blocks.shape[1:]
    lines = parcel_mass.shape[0] // LANES
    rows = 2 * peers * per_peer
    section = lax.axis_index("sec")
    coef = jnp.stack(
        [jnp.where(section == 3, 1.5, 1.0), jnp.where(section == 3, LATENT, 0.0)]
    ).astype(F32)

    own_gas = gas_field.reshape(blocks, LANES)
    own_drop = parcel_state.reshape(lines, LANES)
    together = lax.all_gather(jnp.concatenate([own_gas, own_drop], axis=0), "sec")[3]
    gas = jnp.concatenate([own_gas, together[:blocks]], axis=0)
    drop = jnp.stack([own_drop, together[blocks:]])
    mass = parcel_mass.reshape(lines, LANES)
    base = base_time.reshape(lines, LANES)
    evap = evap_rate.reshape(lines, LANES)
    slot = parcel_block_slot.reshape(lines, LANES)
    cell = parcel_cell.reshape(lines, LANES)

    wanted = slot_blocks[0][:, None, :] + blocks * jnp.arange(2, dtype=jnp.int32)[None, :, None]
    wanted = jnp.broadcast_to(wanted.reshape(rows, 1), (rows, LANES)).astype(BF16)
    wanted = exchange(wanted, peers)

    vmem = pl.BlockSpec(memory_space=pltpu.VMEM)
    smem = pl.BlockSpec(memory_space=pltpu.SMEM)

    def shape(dims, kind=F32):
        return jax.ShapeDtypeStruct(dims, kind)

    gas_shape = shape((2 * blocks, LANES))
    send_shape = shape((rows, LANES), BF16)
    pick, place, send = call(
        pick_kernel,
        (shape((rows, 2 * blocks), BF16), shape((2 * blocks, rows), BF16), send_shape),
        [vmem] * 2,
    )(wanted, gas)
    for substep in range(ITERS):
        recv = exchange(send, peers)
        drop, mass, source = call(
            functools.partial(parcel_kernel, 4),
            (shape((2, lines, LANES)), shape((lines, LANES)), shape((rows, LANES))),
            [smem] * 2 + [vmem] * 7,
            scratch_shapes=[pltpu.VMEM((2, lines, LANES), F32), pltpu.VMEM((6, lines, LANES), F32)],
        )(parcel_count, coef, recv, drop, mass, base, evap, slot, cell)
        source = exchange(source, peers)
        last = substep == ITERS - 1
        result = call(
            functools.partial(gas_kernel, per_pencil),
            (gas_shape,) if last else (gas_shape, send_shape),
            [vmem] * 4,
        )(source, gas, pick, place)
        gas = result[0]
        if not last:
            send = result[1]
    return (gas[:blocks].reshape(gas_field.shape), drop[:1].reshape(parcel_state.shape), mass.reshape(parcel_mass.shape))


def solution(mesh):
    return jax.shard_map(
        shards,
        mesh=mesh,
        in_specs=(
            P("sec", "row", "col", None),
            P("sec", ("row", "col")),
            P(("row", "col")),
            P(("row", "col")),
            P(("row", "col")),
            P(("row", "col"), None, None),
            P(("row", "col")),
            P(("row", "col")),
            P(("row", "col")),
        ),
        out_specs=(P("sec", "row", "col", None), P("sec", ("row", "col")), P(("row", "col"))),
        check_vma=False,
    )
```

time: 1320 us -> 178 us (0.13)
  the two profiles are of different devices: /device:TPU:14 before, /device:TPU:6 now
where the time goes in v1:
time: 178 us; the launch traced here: 177 us
  blocking collectives  98.9 us (56%)
  starting transfers between devices  32.9 us (18%)
  waiting for transfers between devices  29.6 us (17%)
  Pallas kernels  10.3 us (6%)
  local copies, waits for them, and re-layouts  3.56 us (2%)
    all_to_all x6, blocking collectives, exchange(): lax.all_to_all(rows.reshape(shape), 'col', 0, 0, tiled=True)  93.3 us
    all_to_all x3, starting transfers between devices, exchange(): lax.all_to_all(rows.reshape(shape), 'col', 0, 0, tiled=True)  32.9 us
    all_to_all x3, waiting for transfers between devices, exchange(): lax.all_to_all(rows.reshape(shape), 'col', 0, 0, tiled=True)  29.6 us
    pallas_call x4, Pallas kernels, shards(): call(functools.partial(parcel_kernel, 4), (shape((2, lines, LANES)), shap...  8.3 us
    all_gather x1, blocking collectives, shards(): lax.all_gather(jnp.concatenate([own_gas, own_drop], axis=0), 'sec')[3]  5.59 us
  transfers between devices with their start and end apart: 3, of which 3 were waited for; matrix products, arithmetic and copies ran while one was open for 0% of the time, Pallas kernels for 0%

profile of v1, /device:TPU:6, one launch (start us, length us, event | category | flops | bytes accessed | tf_op | source)
XLA Modules:
  0.0 176.9 jit_solution(10135469869266719997)
XLA Ops:
  0.6 0.1 add.29
  0.7 0.1 add.30
  0.8 0.6 copy-done.7
  1.4 0.1 add_convert_fusion
  1.5 0.1 copy.13
  1.6 0.7 broadcast_in_dim.2
  2.3 22.9 %all-to-all-start = ((bf16[32,8,128]{2,1,0:T(8,128)(2,1)}), bf16[32,8,128]{2,1,0:T(8,128)(2,1)S(1)}, u32[]{:S(2)}, u32[]{:S(2)}) async-start(bf16[32,8,128]{2,1,0:T(8,128)(2,1)} %broadcast_in_dim.2), calls=%async_computation | async-start | bytes 131072 | tf_op jit(solution)/shard_map/all_to_all | solution.py:200
  25.3 0.7 copy-done.5
  26.0 5.6 %all-gather = f32[384,128]{1,0:T(8,128)S(1)} all-gather(f32[96,128]{1,0:T(8,128)S(1)} %pad_maximum_fusion.1), channel_id=2, replica_groups=mesh['sec'=4,'row'=8,'col'=32] {'sec'}, dimensions={0}, use_global_device_ids=true | all-gather | bytes 245760 | tf_op jit(solution)/shard_map/all_gather | solution.py:227
  31.6 6.0 %all-to-all-done = bf16[32,8,128]{2,1,0:T(8,128)(2,1)S(1)} async-done(((bf16[32,8,128]{2,1,0:T(8,128)(2,1)}), bf16[32,8,128]{2,1,0:T(8,128)(2,1)S(1)}, u32[]{:S(2)}, u32[]{:S(2)}) %all-to-all-start) | async-done | bytes 65568 | tf_op jit(solution)/shard_map/all_to_all | solution.py:200
  37.6 0.8 shard_map.112
  38.4 6.2 %all-to-all-start.1 = ((bf16[32,8,128]{2,1,0:T(8,128)(2,1)}), bf16[32,8,128]{2,1,0:T(8,128)(2,1)S(1)}, u32[]{:S(2)}, u32[]{:S(2)}) async-start(bf16[32,8,128]{2,1,0:T(8,128)(2,1)} %bitcast.8), calls=%async_computation.1 | async-start | bytes 131072 | tf_op jit(solution)/shard_map/all_to_all | solution.py:200
  44.5 0.1 pad_maximum_fusion.3.coef_ref
  45.4 11.6 %all-to-all-done.1 = bf16[32,8,128]{2,1,0:T(8,128)(2,1)S(1)} async-done(((bf16[32,8,128]{2,1,0:T(8,128)(2,1)}), bf16[32,8,128]{2,1,0:T(8,128)(2,1)S(1)}, u32[]{:S(2)}, u32[]{:S(2)}) %all-to-all-start.1) | async-done | bytes 65568 | tf_op jit(solution)/shard_map/all_to_all | solution.py:200
  57.0 1.9 %shard_map.113 = (f32[2,32,128]{2,1,0:T(8,128)S(1)}, f32[32,128]{1,0:T(8,128)S(1)}, f32[256,128]{1,0:T(8,128)S(1)}) custom-call(s32[1]{0:T(128)S(6)} %copy.14.count_ref, f32[2]{0:T(128)S(1)} %pad_maximum_fusion.3.coef_ref, bf16[256,128]{1,0:T(8,128)(2,1)S(1)} %bitcast.38, f32[2,32,128]{2,1,0:T(8,128)S(1)} %pad_maximum_fusion.2.drop_ref, ...), custom_call_target="tpu_custom_call" | custom-call | tf_op jit(solution)/shard_map/pallas_call | solution.py:255
  58.9 15.7 %all_to_all.45 = f32[32,8,128]{2,1,0:T(8,128)S(1)} all-to-all(f32[32,8,128]{2,1,0:T(8,128)S(1)} %bitcast.60), channel_id=1, replica_groups=mesh['sec'=4,'row'=8,'col'=32] {'col'}, dimensions={0} | all-to-all | bytes 262144 | tf_op jit(solution)/shard_map/all_to_all | solution.py:200
  74.5 0.3 shard_map.114
  74.9 15.4 %all_to_all.46 = bf16[32,8,128]{2,1,0:T(8,128)(2,1)S(1)} all-to-all(bf16[32,8,128]{2,1,0:T(8,128)(2,1)S(1)} %bitcast.61), channel_id=1, replica_groups=mesh['sec'=4,'row'=8,'col'=32] {'col'}, dimensions={0} | all-to-all | bytes 131072 | tf_op jit(solution)/shard_map/all_to_all | solution.py:200
  90.3 1.9 %shard_map.115 = (f32[2,32,128]{2,1,0:T(8,128)S(1)}, f32[32,128]{1,0:T(8,128)S(1)}, f32[256,128]{1,0:T(8,128)S(1)}) custom-call(s32[1]{0:T(128)S(6)} %copy.14.count_ref, f32[2]{0:T(128)S(1)} %pad_maximum_fusion.3.coef_ref, bf16[256,128]{1,0:T(8,128)(2,1)S(1)} %bitcast.40, f32[2,32,128]{2,1,0:T(8,128)S(1)} %get-tuple-element.29.drop_ref, ...), custom_call_target="tpu_custom_call" | custom-call | tf_op jit(solution)/shard_map/pallas_call | solution.py:255
  92.2 15.6 %all_to_all.47 = f32[32,8,128]{2,1,0:T(8,128)S(1)} all-to-all(f32[32,8,128]{2,1,0:T(8,128)S(1)} %bitcast.58), channel_id=1, replica_groups=mesh['sec'=4,'row'=8,'col'=32] {'col'}, dimensions={0} | all-to-all | bytes 262144 | tf_op jit(solution)/shard_map/all_to_all | solution.py:200
  107.8 0.3 shard_map.116
  108.2 15.5 %all_to_all.48 = bf16[32,8,128]{2,1,0:T(8,128)(2,1)S(1)} all-to-all(bf16[32,8,128]{2,1,0:T(8,128)(2,1)S(1)} %bitcast.62), channel_id=1, replica_groups=mesh['sec'=4,'row'=8,'col'=32] {'col'}, dimensions={0} | all-to-all | bytes 131072 | tf_op jit(solution)/shard_map/all_to_all | solution.py:200
  123.7 1.9 %shard_map.117 = (f32[2,32,128]{2,1,0:T(8,128)S(1)}, f32[32,128]{1,0:T(8,128)S(1)}, f32[256,128]{1,0:T(8,128)S(1)}) custom-call(s32[1]{0:T(128)S(6)} %copy.14.count_ref, f32[2]{0:T(128)S(1)} %pad_maximum_fusion.3.coef_ref, bf16[256,128]{1,0:T(8,128)(2,1)S(1)} %bitcast.41, f32[2,32,128]{2,1,0:T(8,128)S(1)} %get-tuple-element.34.drop_ref, ...), custom_call_target="tpu_custom_call" | custom-call | tf_op jit(solution)/shard_map/pallas_call | solution.py:255
  125.6 15.6 %all_to_all.49 = f32[32,8,128]{2,1,0:T(8,128)S(1)} all-to-all(f32[32,8,128]{2,1,0:T(8,128)S(1)} %bitcast.59), channel_id=1, replica_groups=mesh['sec'=4,'row'=8,'col'=32] {'col'}, dimensions={0} | all-to-all | bytes 262144 | tf_op jit(solution)/shard_map/all_to_all | solution.py:200
  141.2 0.3 shard_map.118
  141.5 15.5 %all_to_all.50 = bf16[32,8,128]{2,1,0:T(8,128)(2,1)S(1)} all-to-all(bf16[32,8,128]{2,1,0:T(8,128)(2,1)S(1)} %bitcast.63), channel_id=1, replica_groups=mesh['sec'=4,'row'=8,'col'=32] {'col'}, dimensions={0} | all-to-all | bytes 131072 | tf_op jit(solution)/shard_map/all_to_all | solution.py:200
  157.1 2.6 %shard_map.119 = (f32[2,32,128]{2,1,0:T(8,128)S(1)}, f32[32,128]{1,0:T(8,128)}, f32[256,128]{1,0:T(8,128)}) custom-call(s32[1]{0:T(128)S(6)} %copy.14.count_ref, f32[2]{0:T(128)S(1)} %pad_maximum_fusion.3.coef_ref, bf16[256,128]{1,0:T(8,128)(2,1)S(1)} %bitcast.39, f32[2,32,128]{2,1,0:T(8,128)S(1)} %get-tuple-element.39.drop_ref, ...), custom_call_target="tpu_custom_call" | custom-call | tf_op jit(solution)/shard_map/pallas_call | solution.py:255
  159.6 3.8 %all-to-all-start.8 = ((f32[32,8,128]{2,1,0:T(8,128)}), f32[32,8,128]{2,1,0:T(8,128)S(1)}, u32[]{:S(2)}, u32[]{:S(2)}) async-start(f32[32,8,128]{2,1,0:T(8,128)} %bitcast.28), calls=%async_computation.8 | async-start | bytes 262144 | tf_op jit(solution)/shard_map/all_to_all | solution.py:200
  163.5 0.6 slice.23
  164.1 12.0 %all-to-all-done.8 = f32[32,8,128]{2,1,0:T(8,128)S(1)} async-done(((f32[32,8,128]{2,1,0:T(8,128)}), f32[32,8,128]{2,1,0:T(8,128)S(1)}, u32[]{:S(2)}, u32[]{:S(2)}) %all-to-all-start.8) | async-done | bytes 131104 | tf_op jit(solution)/shard_map/all_to_all | solution.py:200
  176.1 0.2 shard_map.120
  176.3 0.6 reshape.142
  (23 shorter events, 0.1 us)
Async XLA Ops:
  0.7 0.7 copy-start.7
  2.3 22.9 %copy-start.6 = (f32[1,4,2,1024]{3,2,1,0:T(2,128)S(1)}, f32[1,4,2,1024]{3,2,1,0:T(2,128)}, u32[]{:S(2)}) copy-start(f32[1,4,2,1024]{3,2,1,0:T(2,128)} %param.9) | copy-start | bytes 98308
  2.3 35.3 %all-to-all-start = ((bf16[32,8,128]{2,1,0:T(8,128)(2,1)}), bf16[32,8,128]{2,1,0:T(8,128)(2,1)S(1)}, u32[]{:S(2)}, u32[]{:S(2)}) async-start(bf16[32,8,128]{2,1,0:T(8,128)(2,1)} %broadcast_in_dim.2), calls=%async_computation | async-start | bytes 131072 | tf_op jit(solution)/shard_map/all_to_all | solution.py:200
  25.2 0.7 copy-start.5
  38.4 18.5 %all-to-all-start.1 = ((bf16[32,8,128]{2,1,0:T(8,128)(2,1)}), bf16[32,8,128]{2,1,0:T(8,128)(2,1)S(1)}, u32[]{:S(2)}, u32[]{:S(2)}) async-start(bf16[32,8,128]{2,1,0:T(8,128)(2,1)} %bitcast.8), calls=%async_computation.1 | async-start | bytes 131072 | tf_op jit(solution)/shard_map/all_to_all | solution.py:200
  44.6 12.3 %copy-start.4 = (f32[4096]{0:T(1024)S(1)}, f32[4096]{0:T(1024)}, u32[]{:S(2)}) copy-start(f32[4096]{0:T(1024)} %param.11) | copy-start | bytes 49156
  45.3 11.6 %copy-start = (f32[4096]{0:T(1024)S(1)}, f32[4096]{0:T(1024)}, u32[]{:S(2)}) copy-start(f32[4096]{0:T(1024)} %param.12) | copy-start | bytes 49156
  45.3 11.6 %copy-start.1 = (f32[4096]{0:T(1024)S(1)}, f32[4096]{0:T(1024)}, u32[]{:S(2)}) copy-start(f32[4096]{0:T(1024)} %param.13) | copy-start | bytes 49156
  45.3 11.6 %copy-start.2 = (s32[4096]{0:T(1024)S(1)}, s32[4096]{0:T(1024)}, u32[]{:S(2)}) copy-start(s32[4096]{0:T(1024)} %param.15) | copy-start | bytes 49156
  45.3 11.6 %copy-start.3 = (s32[4096]{0:T(1024)S(1)}, s32[4096]{0:T(1024)}, u32[]{:S(2)}) copy-start(s32[4096]{0:T(1024)} %param.16) | copy-start | bytes 49156
  159.6 16.4 %all-to-all-start.8 = ((f32[32,8,128]{2,1,0:T(8,128)}), f32[32,8,128]{2,1,0:T(8,128)S(1)}, u32[]{:S(2)}, u32[]{:S(2)}) async-start(f32[32,8,128]{2,1,0:T(8,128)} %bitcast.28), calls=%async_computation.8 | async-start | bytes 262144 | tf_op jit(solution)/shard_map/all_to_all | solution.py:200

commit v2 on v1

--- a/solution.py
+++ b/solution.py
@@ -5,6 +5,7 @@
 from jax import lax
 from jax.experimental import pallas as pl
 from jax.experimental.pallas import tpu as pltpu
+from jax.sharding import Mesh
 from jax.sharding import PartitionSpec as P
 
 ITERS = 4
@@ -14,6 +15,7 @@
 DIFFUSE = 0.2
 LANES = 128
 HALF = 64
+GROUP = ("sec", "near")
 VMEM_LIMIT = 32 * 1024 * 1024
 
 F32 = jnp.float32
@@ -117,11 +119,6 @@
 
     own, temp = split_pair(recv_ref[...].astype(F32))
     table = jnp.concatenate([fold(own), fold(temp)], axis=0).astype(BF16)
-    cell = cell_ref[...]
-    upper = cell // HALF
-    part_ref[4] = (slot_ref[...] + slots * upper).astype(F32)
-    part_ref[5] = (cell - HALF * upper).astype(F32)
-
     def packed(ref, start):
         row = jnp.concatenate([ref[start + i : start + i + 1, :] for i in range(chunk)], axis=1)
         return jnp.broadcast_to(row, (16, width)).astype(BF16)[None]
@@ -134,8 +131,8 @@
     one, zero = jnp.ones((), BF16), jnp.zeros((), BF16)
 
     def masks(start):
-        hot = jnp.where(slot_index == packed(part_ref.at[4], start), one, zero)
-        return hot.reshape(2 * slots, width), cell_index == packed(part_ref.at[5], start)
+        hot = jnp.where(slot_index == packed(slot_ref, start), one, zero)
+        return hot.reshape(2 * slots, width), cell_index == packed(cell_ref, start)
 
     for start in range(0, lines, chunk):
         hot, here = masks(start)
@@ -197,7 +194,13 @@
 
 def exchange(rows, peers):
     shape = (peers, rows.shape[0] // peers, LANES)
-    return lax.all_to_all(rows.reshape(shape), "col", 0, 0, tiled=True).reshape(rows.shape)
+    return lax.all_to_all(rows.reshape(shape), GROUP, 0, 0, tiled=True).reshape(rows.shape)
+
+
+def swap(values):
+    side = lax.axis_size("sec")
+    pairs = [(i * side + j, j * side + i) for i in range(side) for j in range(side)]
+    return lax.ppermute(values, ("sec", "far"), pairs)
 
 
 def shards(
@@ -215,25 +218,40 @@
     blocks = cells[0] * cells[1] * cells[2] // LANES
     per_pencil = cells[2] // LANES
     peers, per_peer = slot_blocks.shape[1:]
+    slots = peers * per_peer
     lines = parcel_mass.shape[0] // LANES
-    rows = 2 * peers * per_peer
-    section = lax.axis_index("sec")
+    rows = 2 * slots
+
+    quantity = lax.axis_index("far")
     coef = jnp.stack(
-        [jnp.where(section == 3, 1.5, 1.0), jnp.where(section == 3, LATENT, 0.0)]
+        [jnp.where(quantity == 3, 1.5, 1.0), jnp.where(quantity == 3, LATENT, 0.0)]
     ).astype(F32)
+
+    small = jnp.concatenate(
+        [slot_blocks.reshape(1, slots), jnp.broadcast_to(parcel_count[:, None], (1, slots))]
+    )
+    small = swap(small.astype(F32)).astype(jnp.int32)
+    block_lists, count = small[0].reshape(peers, per_peer), small[1, :1]
 
     own_gas = gas_field.reshape(blocks, LANES)
     own_drop = parcel_state.reshape(lines, LANES)
     together = lax.all_gather(jnp.concatenate([own_gas, own_drop], axis=0), "sec")[3]
-    gas = jnp.concatenate([own_gas, together[:blocks]], axis=0)
-    drop = jnp.stack([own_drop, together[blocks:]])
-    mass = parcel_mass.reshape(lines, LANES)
-    base = base_time.reshape(lines, LANES)
-    evap = evap_rate.reshape(lines, LANES)
-    slot = parcel_block_slot.reshape(lines, LANES)
-    cell = parcel_cell.reshape(lines, LANES)
-
-    wanted = slot_blocks[0][:, None, :] + blocks * jnp.arange(2, dtype=jnp.int32)[None, :, None]
+    gas = swap(jnp.concatenate([own_gas, together[:blocks]], axis=0))
+    upper = parcel_cell // HALF
+    parcels = [
+        own_drop,
+        together[blocks:],
+        parcel_mass,
+        base_time,
+        evap_rate,
+        (parcel_block_slot + slots * upper).astype(F32),
+        (parcel_cell - HALF * upper).astype(F32),
+    ]
+    parcels = swap(jnp.stack([part.reshape(lines, LANES) for part in parcels]))
+    drop = parcels[:2]
+    mass, base, evap, slot, cell = (parcels[i] for i in range(2, 7))
+
+    wanted = block_lists[:, None, :] + blocks * jnp.arange(2, dtype=jnp.int32)[None, :, None]
     wanted = jnp.broadcast_to(wanted.reshape(rows, 1), (rows, LANES)).astype(BF16)
     wanted = exchange(wanted, peers)
 
@@ -256,8 +274,8 @@
             functools.partial(parcel_kernel, 4),
             (shape((2, lines, LANES)), shape((lines, LANES)), shape((rows, LANES))),
             [smem] * 2 + [vmem] * 7,
-            scratch_shapes=[pltpu.VMEM((2, lines, LANES), F32), pltpu.VMEM((6, lines, LANES), F32)],
-        )(parcel_count, coef, recv, drop, mass, base, evap, slot, cell)
+            scratch_shapes=[pltpu.VMEM((2, lines, LANES), F32), pltpu.VMEM((4, lines, LANES), F32)],
+        )(count, coef, recv, drop, mass, base, evap, slot, cell)
         source = exchange(source, peers)
         last = substep == ITERS - 1
         result = call(
@@ -268,24 +286,37 @@
         gas = result[0]
         if not last:
             send = result[1]
-    return (gas[:blocks].reshape(gas_field.shape), drop[:1].reshape(parcel_state.shape), mass.reshape(parcel_mass.shape))
+    parcels = swap(jnp.stack([drop[0], mass]))
+    gas = swap(gas[:blocks])
+    return (
+        gas.reshape(gas_field.shape),
+        parcels[0].reshape(parcel_state.shape),
+        parcels[1].reshape(parcel_mass.shape),
+    )
 
 
 def solution(mesh):
+    sec, row, col = (mesh.shape[name] for name in ("sec", "row", "col"))
+    split = Mesh(mesh.devices.reshape(sec, row, sec, col // sec), ("sec", "row", "far", "near"))
+    place = P(("row", "far", "near"))
     return jax.shard_map(
         shards,
-        mesh=mesh,
+        mesh=split,
         in_specs=(
-            P("sec", "row", "col", None),
-            P("sec", ("row", "col")),
-            P(("row", "col")),
-            P(("row", "col")),
-            P(("row", "col")),
-            P(("row", "col"), None, None),
-            P(("row", "col")),
-            P(("row", "col")),
-            P(("row", "col")),
+            P("sec", "row", ("far", "near"), None),
+            P("sec", ("row", "far", "near")),
+            place,
+            place,
+            place,
+            P(("row", "far", "near"), None, None),
+            place,
+            place,
+            place,
         ),
-        out_specs=(P("sec", "row", "col", None), P("sec", ("row", "col")), P(("row", "col"))),
+        out_specs=(
+            P("sec", "row", ("far", "near"), None),
+            P("sec", ("row", "far", "near")),
+            place,
+        ),
         check_vma=False,
     )

time: 178 us -> 174 us (0.978)
  the two profiles are of different devices: /device:TPU:6 before, /device:TPU:16 now
where the time goes in v2:
time: 174 us; the launch traced here: 173 us
  blocking collectives  82.3 us (47%)
  starting transfers between devices  49.6 us (29%)
  waiting for transfers between devices  19.7 us (11%)
  Pallas kernels  12.9 us (7%)
  local copies, waits for them, and re-layouts  6.75 us (4%)
    all_to_all x6, blocking collectives, exchange(): lax.all_to_all(rows.reshape(shape), GROUP, 0, 0, tiled=True)  71.8 us
    all_to_all x3, starting transfers between devices, exchange(): lax.all_to_all(rows.reshape(shape), GROUP, 0, 0, tiled=True)  26.2 us
    ppermute x5, starting transfers between devices, swap(): return lax.ppermute(values, ('sec', 'far'), pairs)  23.3 us
    all_to_all x3, waiting for transfers between devices, exchange(): lax.all_to_all(rows.reshape(shape), GROUP, 0, 0, tiled=True)  12.5 us
    pallas_call x4, Pallas kernels, shards(): call(functools.partial(parcel_kernel, 4), (shape((2, lines, LANES)), shap...  10.9 us
    all_gather x1, blocking collectives, shards(): lax.all_gather(jnp.concatenate([own_gas, own_drop], axis=0), 'sec')[3]  10.5 us
    ppermute x5, waiting for transfers between devices, swap(): return lax.ppermute(values, ('sec', 'far'), pairs)  7.2 us
    unnamed x20, local copies, waits for them, and re-layouts  3.66 us
  transfers between devices with their start and end apart: 8, of which 4 were waited for; matrix products, arithmetic and copies ran while one was open for 1% of the time, Pallas kernels for 0%

profile of v2, /device:TPU:16, one launch (start us, length us, event | category | flops | bytes accessed | tf_op | source)
XLA Modules:
  0.0 172.9 jit_solution(7752821768689443856)
XLA Ops:
  1.3 0.8 copy.13
  2.2 7.1 %collective-permute-start = (f32[2,128]{1,0:T(2,128)S(1)}, f32[2,128]{1,0:T(2,128)S(1)}, u32[]{:S(2)}, u32[]{:S(2)}) collective-permute-start(f32[2,128]{1,0:T(2,128)S(1)} %pad_convert_fusion), channel_id=1, source_target_pairs={{0,0},{8,256},{16,512},{24,768},{256,8},{264,264},{272,520},{280,7... | collective-permute-start | bytes 3080 | tf_op jit(solution)/shard_map/ppermute | solution.py:203
  9.3 10.5 %all-gather = f32[384,128]{1,0:T(8,128)S(1)} all-gather(f32[96,128]{1,0:T(8,128)S(1)} %pad_maximum_fusion.1), channel_id=2, replica_groups=mesh['sec'=4,'row'=8,'far'=4,'near'=8] {'sec'}, dimensions={0}, use_global_device_ids=true | all-gather | bytes 245760 | tf_op jit(solution)/shard_map/all_gather | solution.py:238
  19.8 0.7 copy-done.4
  20.5 0.7 copy-done.5
  21.3 0.7 copy-done.6
  22.0 0.7 copy-done
  22.8 1.9 %collective-permute-start.2 = (f32[7,32,128]{2,1,0:T(8,128)S(1)}, f32[7,32,128]{2,1,0:T(8,128)S(1)}, u32[]{:S(2)}, u32[]{:S(2)}) collective-permute-start(f32[7,32,128]{2,1,0:T(8,128)S(1)} %constant_dynamic-update-slice_fusion), channel_id=1, source_target_pairs={{0,0},{8,256},{16,512},{24,768},{256,8},{264,264},{272,520},{280,7... | collective-permute-start | bytes 344072 | tf_op jit(solution)/shard_map/ppermute | solution.py:203
  25.2 0.7 broadcast_in_dim.5
  26.0 13.4 %all-to-all-start = ((bf16[32,8,128]{2,1,0:T(8,128)(2,1)}), bf16[32,8,128]{2,1,0:T(8,128)(2,1)S(1)}, u32[]{:S(2)}, u32[]{:S(2)}) async-start(bf16[32,8,128]{2,1,0:T(8,128)(2,1)} %broadcast_in_dim.5), calls=%async_computation | async-start | bytes 131072 | tf_op jit(solution)/shard_map/all_to_all | solution.py:197
  39.4 5.7 %collective-permute-start.1 = (f32[128,128]{1,0:T(8,128)S(1)}, f32[128,128]{1,0:T(8,128)S(1)}, u32[]{:S(2)}, u32[]{:S(2)}) collective-permute-start(f32[128,128]{1,0:T(8,128)S(1)} %pad_maximum_fusion), channel_id=1, source_target_pairs={{0,0},{8,256},{16,512},{24,768},{256,8},{264,264},{272,520},{280,7... | collective-permute-start | bytes 196616 | tf_op jit(solution)/shard_map/ppermute | solution.py:203
  45.7 3.6 %collective-permute-done.1.gas_ref = f32[128,128]{1,0:T(8,128)S(1)} collective-permute-done((f32[128,128]{1,0:T(8,128)S(1)}, f32[128,128]{1,0:T(8,128)S(1)}, u32[]{:S(2)}, u32[]{:S(2)}) %collective-permute-start.1) | collective-permute-done | bytes 65568 | tf_op jit(solution)/shard_map/ppermute | solution.py:203
  49.3 0.8 shard_map.112
  50.1 8.3 %all-to-all-start.1 = ((bf16[32,8,128]{2,1,0:T(8,128)(2,1)}), bf16[32,8,128]{2,1,0:T(8,128)(2,1)S(1)}, u32[]{:S(2)}, u32[]{:S(2)}) async-start(bf16[32,8,128]{2,1,0:T(8,128)(2,1)} %bitcast.9), calls=%async_computation.1 | async-start | bytes 131072 | tf_op jit(solution)/shard_map/all_to_all | solution.py:197
  58.4 7.7 %all-to-all-done.1 = bf16[32,8,128]{2,1,0:T(8,128)(2,1)S(1)} async-done(((bf16[32,8,128]{2,1,0:T(8,128)(2,1)}), bf16[32,8,128]{2,1,0:T(8,128)(2,1)S(1)}, u32[]{:S(2)}, u32[]{:S(2)}) %all-to-all-start.1) | async-done | bytes 65568 | tf_op jit(solution)/shard_map/all_to_all | solution.py:197
  66.1 2.6 %shard_map.113 = (f32[2,32,128]{2,1,0:T(8,128)S(1)}, f32[32,128]{1,0:T(8,128)S(1)}, f32[256,128]{1,0:T(8,128)S(1)}) custom-call(s32[1]{0:T(128)} %bitcast.1.count_ref, f32[2]{0:T(128)S(1)} %pad_maximum_fusion.3.coef_ref, bf16[256,128]{1,0:T(8,128)(2,1)S(1)} %bitcast.57, f32[2,32,128]{2,1,0:T(8,128)S(1)} %slice.66.drop_ref, ...), custom_call_target="tpu_custom_call" | custom-call | tf_op jit(solution)/shard_map/pallas_call | solution.py:273
  68.7 12.5 %all_to_all.45 = f32[32,8,128]{2,1,0:T(8,128)S(1)} all-to-all(f32[32,8,128]{2,1,0:T(8,128)S(1)} %bitcast.61), channel_id=1, replica_groups=mesh['sec'=4,'row'=8,'far'=4,'near'=8] {'sec','near'}, dimensions={0} | all-to-all | bytes 262144 | tf_op jit(solution)/shard_map/all_to_all | solution.py:197
  81.6 11.4 %all_to_all.46 = bf16[32,8,128]{2,1,0:T(8,128)(2,1)S(1)} all-to-all(bf16[32,8,128]{2,1,0:T(8,128)(2,1)S(1)} %bitcast.64), channel_id=1, replica_groups=mesh['sec'=4,'row'=8,'far'=4,'near'=8] {'sec','near'}, dimensions={0} | all-to-all | bytes 131072 | tf_op jit(solution)/shard_map/all_to_all | solution.py:197
  93.0 2.6 %shard_map.115 = (f32[2,32,128]{2,1,0:T(8,128)S(1)}, f32[32,128]{1,0:T(8,128)S(1)}, f32[256,128]{1,0:T(8,128)S(1)}) custom-call(s32[1]{0:T(128)} %bitcast.1.count_ref, f32[2]{0:T(128)S(1)} %pad_maximum_fusion.3.coef_ref, bf16[256,128]{1,0:T(8,128)(2,1)S(1)} %bitcast.59, f32[2,32,128]{2,1,0:T(8,128)S(1)} %get-tuple-element.29.drop_ref, ...), custom_call_target="tpu_custom_call" | custom-call | tf_op jit(solution)/shard_map/pallas_call | solution.py:273
  95.5 12.5 %all_to_all.47 = f32[32,8,128]{2,1,0:T(8,128)S(1)} all-to-all(f32[32,8,128]{2,1,0:T(8,128)S(1)} %bitcast.62), channel_id=1, replica_groups=mesh['sec'=4,'row'=8,'far'=4,'near'=8] {'sec','near'}, dimensions={0} | all-to-all | bytes 262144 | tf_op jit(solution)/shard_map/all_to_all | solution.py:197
  108.4 11.4 %all_to_all.48 = bf16[32,8,128]{2,1,0:T(8,128)(2,1)S(1)} all-to-all(bf16[32,8,128]{2,1,0:T(8,128)(2,1)S(1)} %bitcast.65), channel_id=1, replica_groups=mesh['sec'=4,'row'=8,'far'=4,'near'=8] {'sec','near'}, dimensions={0} | all-to-all | bytes 131072 | tf_op jit(solution)/shard_map/all_to_all | solution.py:197
  119.8 2.6 %shard_map.117 = (f32[2,32,128]{2,1,0:T(8,128)S(1)}, f32[32,128]{1,0:T(8,128)S(1)}, f32[256,128]{1,0:T(8,128)S(1)}) custom-call(s32[1]{0:T(128)} %bitcast.1.count_ref, f32[2]{0:T(128)S(1)} %pad_maximum_fusion.3.coef_ref, bf16[256,128]{1,0:T(8,128)(2,1)S(1)} %bitcast.60, f32[2,32,128]{2,1,0:T(8,128)S(1)} %get-tuple-element.34.drop_ref, ...), custom_call_target="tpu_custom_call" | custom-call | tf_op jit(solution)/shard_map/pallas_call | solution.py:273
  122.4 12.5 %all_to_all.49 = f32[32,8,128]{2,1,0:T(8,128)S(1)} all-to-all(f32[32,8,128]{2,1,0:T(8,128)S(1)} %bitcast.63), channel_id=1, replica_groups=mesh['sec'=4,'row'=8,'far'=4,'near'=8] {'sec','near'}, dimensions={0} | all-to-all | bytes 262144 | tf_op jit(solution)/shard_map/all_to_all | solution.py:197
  135.3 11.4 %all_to_all.50 = bf16[32,8,128]{2,1,0:T(8,128)(2,1)S(1)} all-to-all(bf16[32,8,128]{2,1,0:T(8,128)(2,1)S(1)} %bitcast.66), channel_id=1, replica_groups=mesh['sec'=4,'row'=8,'far'=4,'near'=8] {'sec','near'}, dimensions={0} | all-to-all | bytes 131072 | tf_op jit(solution)/shard_map/all_to_all | solution.py:197
  146.6 3.2 %shard_map.119 = (f32[2,32,128]{2,1,0:T(8,128)S(1)}, f32[32,128]{1,0:T(8,128)S(1)}, f32[256,128]{1,0:T(8,128)}) custom-call(s32[1]{0:T(128)} %bitcast.1.count_ref, f32[2]{0:T(128)S(1)} %pad_maximum_fusion.3.coef_ref, bf16[256,128]{1,0:T(8,128)(2,1)S(1)} %bitcast.58, f32[2,32,128]{2,1,0:T(8,128)S(1)} %get-tuple-element.39.drop_ref, ...), custom_call_target="tpu_custom_call" | custom-call | tf_op jit(solution)/shard_map/pallas_call | solution.py:273
  149.8 4.5 %all-to-all-start.8 = ((f32[32,8,128]{2,1,0:T(8,128)}), f32[32,8,128]{2,1,0:T(8,128)S(1)}, u32[]{:S(2)}, u32[]{:S(2)}) async-start(f32[32,8,128]{2,1,0:T(8,128)} %bitcast.34), calls=%async_computation.8 | async-start | bytes 262144 | tf_op jit(solution)/shard_map/all_to_all | solution.py:197
  154.4 4.1 %collective-permute-start.4 = (f32[2,32,128]{2,1,0:T(8,128)S(1)}, f32[2,32,128]{2,1,0:T(8,128)S(1)}, u32[]{:S(2)}, u32[]{:S(2)}) collective-permute-start(f32[2,32,128]{2,1,0:T(8,128)S(1)} %pad_maximum_fusion.2), channel_id=1, source_target_pairs={{0,0},{8,256},{16,512},{24,768},{256,8},{264,264},{272,520},{280,7... | collective-permute-start | bytes 98312 | tf_op jit(solution)/shard_map/ppermute | solution.py:203
  158.5 4.8 %all-to-all-done.8 = f32[32,8,128]{2,1,0:T(8,128)S(1)} async-done(((f32[32,8,128]{2,1,0:T(8,128)}), f32[32,8,128]{2,1,0:T(8,128)S(1)}, u32[]{:S(2)}, u32[]{:S(2)}) %all-to-all-start.8) | async-done | bytes 131104 | tf_op jit(solution)/shard_map/all_to_all | solution.py:197
  163.5 4.6 %collective-permute-start.3 = (f32[64,128]{1,0:T(8,128)S(1)}, f32[64,128]{1,0:T(8,128)S(1)}, u32[]{:S(2)}, u32[]{:S(2)}) collective-permute-start(f32[64,128]{1,0:T(8,128)S(1)} %slice.72), channel_id=1, source_target_pairs={{0,0},{8,256},{16,512},{24,768},{256,8},{264,264},{272,520},{280,7... | collective-permute-start | bytes 98312 | tf_op jit(solution)/shard_map/ppermute | solution.py:203
  168.0 0.6 slice_bitcast_fusion.1
  168.7 3.6 %collective-permute-done.3 = f32[64,128]{1,0:T(8,128)S(1)} collective-permute-done((f32[64,128]{1,0:T(8,128)S(1)}, f32[64,128]{1,0:T(8,128)S(1)}, u32[]{:S(2)}, u32[]{:S(2)}) %collective-permute-start.3) | collective-permute-done | bytes 32800 | tf_op jit(solution)/shard_map/ppermute | solution.py:203
  172.3 0.6 reshape.123
  (48 shorter events, 2.6 us)
Async XLA Ops:
  0.6 8.6 %copy-start.2 = (f32[1,4,2,1024]{3,2,1,0:T(2,128)S(1)}, f32[1,4,2,1024]{3,2,1,0:T(2,128)}, u32[]{:S(2)}) copy-start(f32[1,4,2,1024]{3,2,1,0:T(2,128)} %param.9) | copy-start | bytes 98308
  2.2 7.1 %copy-start.1 = (f32[1,4096]{1,0:T(1,128)S(1)}, f32[1,4096]{1,0:T(1,128)}, u32[]{:S(2)}) copy-start(f32[1,4096]{1,0:T(1,128)} %param.10) | copy-start | bytes 49156
  2.2 22.7 %collective-permute-start = (f32[2,128]{1,0:T(2,128)S(1)}, f32[2,128]{1,0:T(2,128)S(1)}, u32[]{:S(2)}, u32[]{:S(2)}) collective-permute-start(f32[2,128]{1,0:T(2,128)S(1)} %pad_convert_fusion), channel_id=1, source_target_pairs={{0,0},{8,256},{16,512},{24,768},{256,8},{264,264},{272,520},{280,7... | collective-permute-start | bytes 3080 | tf_op jit(solution)/shard_map/ppermute | solution.py:203
  19.8 0.7 copy-start.4
  20.5 0.7 copy-start.5
  21.3 0.7 copy-start.6
  22.0 0.7 copy-start
  22.0 0.7 copy-start.3
  22.8 23.0 %collective-permute-start.2 = (f32[7,32,128]{2,1,0:T(8,128)S(1)}, f32[7,32,128]{2,1,0:T(8,128)S(1)}, u32[]{:S(2)}, u32[]{:S(2)}) collective-permute-start(f32[7,32,128]{2,1,0:T(8,128)S(1)} %constant_dynamic-update-slice_fusion), channel_id=1, source_target_pairs={{0,0},{8,256},{16,512},{24,768},{256,8},{264,264},{272,520},{280,7... | collective-permute-start | bytes 344072 | tf_op jit(solution)/shard_map/ppermute | solution.py:203
  26.0 23.3 %all-to-all-start = ((bf16[32,8,128]{2,1,0:T(8,128)(2,1)}), bf16[32,8,128]{2,1,0:T(8,128)(2,1)S(1)}, u32[]{:S(2)}, u32[]{:S(2)}) async-start(bf16[32,8,128]{2,1,0:T(8,128)(2,1)} %broadcast_in_dim.5), calls=%async_computation | async-start | bytes 131072 | tf_op jit(solution)/shard_map/all_to_all | solution.py:197
  39.4 9.9 %collective-permute-start.1 = (f32[128,128]{1,0:T(8,128)S(1)}, f32[128,128]{1,0:T(8,128)S(1)}, u32[]{:S(2)}, u32[]{:S(2)}) collective-permute-start(f32[128,128]{1,0:T(8,128)S(1)} %pad_maximum_fusion), channel_id=1, source_target_pairs={{0,0},{8,256},{16,512},{24,768},{256,8},{264,264},{272,520},{280,7... | collective-permute-start | bytes 196616 | tf_op jit(solution)/shard_map/ppermute | solution.py:203
  50.1 16.0 %all-to-all-start.1 = ((bf16[32,8,128]{2,1,0:T(8,128)(2,1)}), bf16[32,8,128]{2,1,0:T(8,128)(2,1)S(1)}, u32[]{:S(2)}, u32[]{:S(2)}) async-start(bf16[32,8,128]{2,1,0:T(8,128)(2,1)} %bitcast.9), calls=%async_computation.1 | async-start | bytes 131072 | tf_op jit(solution)/shard_map/all_to_all | solution.py:197
  149.8 13.4 %all-to-all-start.8 = ((f32[32,8,128]{2,1,0:T(8,128)}), f32[32,8,128]{2,1,0:T(8,128)S(1)}, u32[]{:S(2)}, u32[]{:S(2)}) async-start(f32[32,8,128]{2,1,0:T(8,128)} %bitcast.34), calls=%async_computation.8 | async-start | bytes 262144 | tf_op jit(solution)/shard_map/all_to_all | solution.py:197
  154.4 13.6 %collective-permute-start.4 = (f32[2,32,128]{2,1,0:T(8,128)S(1)}, f32[2,32,128]{2,1,0:T(8,128)S(1)}, u32[]{:S(2)}, u32[]{:S(2)}) collective-permute-start(f32[2,32,128]{2,1,0:T(8,128)S(1)} %pad_maximum_fusion.2), channel_id=1, source_target_pairs={{0,0},{8,256},{16,512},{24,768},{256,8},{264,264},{272,520},{280,7... | collective-permute-start | bytes 98312 | tf_op jit(solution)/shard_map/ppermute | solution.py:203
  163.5 8.8 %collective-permute-start.3 = (f32[64,128]{1,0:T(8,128)S(1)}, f32[64,128]{1,0:T(8,128)S(1)}, u32[]{:S(2)}, u32[]{:S(2)}) collective-permute-start(f32[64,128]{1,0:T(8,128)S(1)} %slice.72), channel_id=1, source_target_pairs={{0,0},{8,256},{16,512},{24,768},{256,8},{264,264},{272,520},{280,7... | collective-permute-start | bytes 98312 | tf_op jit(solution)/shard_map/ppermute | solution.py:203

commit v3 on v2

v3 whole, which is shorter than its diff:
```python
import functools

import jax
import jax.numpy as jnp
from jax import lax
from jax.experimental import pallas as pl
from jax.experimental.pallas import tpu as pltpu
from jax.sharding import Mesh
from jax.sharding import PartitionSpec as P

ITERS = 4
LATENT = 2.0
DEPOSIT_MODE = 0.5
ADVECT = 0.3
DIFFUSE = 0.2
LANES = 128
HALF = 64
GROUP = ("sec", "near")
OWN, MASS, TEMP, BASE, EVAP, SLOT, CELL = range(7)
VMEM_LIMIT = 32 * 1024 * 1024

F32 = jnp.float32
BF16 = jnp.bfloat16


def iota(shape, axis):
    return lax.broadcasted_iota(jnp.int32, shape, axis)


def dot(left_side, right_side, left_axis=1, right_axis=0):
    return lax.dot_general(
        left_side,
        right_side,
        (((left_axis,), (right_axis,)), ((), ())),
        preferred_element_type=F32,
    )


def halves(values):
    high = values.astype(BF16)
    return high, (values - high.astype(F32)).astype(BF16)


def split_pair(rows):
    tiles = rows.reshape(rows.shape[0] // 16, 2, 8, LANES)
    even, odd = tiles[:, 0], tiles[:, 1]
    low = iota(even.shape, 1) < 4
    first = jnp.where(low, even, pltpu.roll(odd, 4, 1))
    second = jnp.where(low, pltpu.roll(even, 4, 1), odd)
    flat = (rows.shape[0] // 2, LANES)
    return first.reshape(flat), second.reshape(flat)


def merge_pair(first, second):
    shape = (first.shape[0] // 8, 8, LANES)
    first, second = first.reshape(shape), second.reshape(shape)
    low = iota(shape, 1) < 4
    even = jnp.where(low, first, pltpu.roll(second, 4, 1))
    odd = jnp.where(low, pltpu.roll(first, 4, 1), second)
    return jnp.stack([even, odd], axis=1).reshape(2 * shape[0] * 8, LANES)


def order_kernel(per_peer, pencils, per_pencil, blocks, list_ref, rows_ref):
    block = list_ref[0]
    first = block // (pencils * per_pencil)
    rest = block - first * (pencils * per_pencil)
    pencil = rest // per_pencil
    place = first * (pencils * per_pencil) + (rest - pencil * per_pencil) * pencils + pencil
    rows, peers = rows_ref.shape[0], block.shape[0]
    each = rows // peers
    owner = (iota((rows, peers), 0) // each == iota((rows, peers), 1)).astype(BF16)
    spread = dot(owner, place.astype(F32).astype(BF16))
    within = iota(spread.shape, 0) % each
    kept = jnp.where(within % per_peer == iota(spread.shape, 1), spread, 0.0)
    value = jnp.sum(kept, axis=1, keepdims=True)
    value = value + (blocks * (within[:, :1] // per_peer)).astype(F32)
    rows_ref[...] = jnp.broadcast_to(value, rows_ref.shape).astype(BF16)


def pack_kernel(
    slots, count_ref, temp_ref, gas_ref, drop_ref, mass_ref, base_ref, evap_ref, slot_ref, cell_ref, out_ref
):
    blocks, lines = gas_ref.shape[0], mass_ref.shape[0]
    start = temp_ref.shape[0] - blocks - lines
    out_ref[:blocks] = gas_ref[...]
    out_ref[blocks : 2 * blocks] = temp_ref[start : start + blocks]

    def store(which, values):
        at = 2 * blocks + which * lines
        out_ref[at : at + lines] = values

    store(OWN, drop_ref[...])
    store(MASS, mass_ref[...])
    store(TEMP, temp_ref[start + blocks :])
    store(BASE, base_ref[...])
    store(EVAP, evap_ref[...])
    shape = mass_ref.shape
    active = iota(shape, 0) * LANES + iota(shape, 1) < count_ref[0]
    upper = cell_ref[...] // HALF
    store(SLOT, (slot_ref[...] + slots * upper).astype(F32))
    store(CELL, jnp.where(active, cell_ref[...] - HALF * upper, -1).astype(F32))


def pick_kernel(wanted_ref, pack_ref, pick_ref, place_ref, send_ref):
    wanted = wanted_ref[...].astype(F32).astype(jnp.int32)
    pick = (wanted == iota(wanted.shape, 1)).astype(F32)
    pick_ref[...] = pick.astype(BF16)
    place_ref[...] = pick.T.astype(BF16)
    gas = pack_ref[: wanted.shape[1]]
    send_ref[...] = dot(pick.astype(BF16), gas.astype(BF16)).astype(BF16)


def gas_kernel(stride, per_pencil, source_ref, gas_ref, pick_ref, place_ref, gas_out, send_ref=None):
    high, low = halves(source_ref[...])
    place = place_ref[...]
    deposit = dot(place, high) + dot(place, low)
    rows = place.shape[0]
    gas = gas_ref[:rows]
    block = iota(gas.shape, 0) // stride % per_pencil
    lane = iota(gas.shape, 1)
    to_right = pltpu.roll(gas, 1, 1)
    to_left = pltpu.roll(gas, LANES - 1, 1)
    left = jnp.where(
        lane == 0, jnp.where(block == 0, gas, pltpu.roll(to_right, stride, 0)), to_right
    )
    right = jnp.where(
        lane == LANES - 1,
        jnp.where(block == per_pencil - 1, gas, pltpu.roll(to_left, rows - stride, 0)),
        to_left,
    )
    moved = gas + ADVECT * (left - gas) + DIFFUSE * (right - 2.0 * gas + left)
    new_gas = moved + DEPOSIT_MODE * deposit
    gas_out[...] = new_gas[: gas_out.shape[0]]
    if send_ref is not None:
        send_ref[...] = dot(pick_ref[...], new_gas.astype(BF16)).astype(BF16)


def parcel_kernel(chunk, first, recv_ref, pack_ref, *refs):
    state_ref = None if first else refs[0]
    state_out, send_ref, seen_ref, part_ref = refs[-4:]
    lines = state_out.shape[1]
    base_row = pack_ref.shape[0] - 7 * lines
    slots = recv_ref.shape[0] // 2
    width = chunk * LANES

    def given(which):
        return pack_ref[base_row + which * lines : base_row + (which + 1) * lines]

    def held(which):
        return given(which) if first else state_ref[which]

    def fold(values):
        turned = values.T
        return jnp.concatenate([turned[:HALF], turned[HALF:]], axis=1)

    own, temp = split_pair(recv_ref[...].astype(F32))
    table = jnp.concatenate([fold(own), fold(temp)], axis=0).astype(BF16)

    def packed(ref, start):
        row = jnp.concatenate([ref[start + i : start + i + 1, :] for i in range(chunk)], axis=1)
        return jnp.broadcast_to(row, (16, width)).astype(BF16)[None]

    def index(count):
        shape = (count // 16, 16, width)
        return (iota(shape, 0) * 16 + iota(shape, 1)).astype(F32).astype(BF16)

    slot_index, cell_index = index(2 * slots), index(HALF)
    one, zero = jnp.ones((), BF16), jnp.zeros((), BF16)

    def masks(start):
        hot = jnp.where(slot_index == packed(pack_ref, base_row + SLOT * lines + start), one, zero)
        here = cell_index == packed(pack_ref, base_row + CELL * lines + start)
        return hot.reshape(2 * slots, width), here

    for start in range(0, lines, chunk):
        hot, here = masks(start)
        values = dot(table, hot).astype(BF16).reshape(2, HALF // 16, 16, width)
        for quantity in range(2):
            kept = jnp.where(here, values[quantity], zero)
            total = kept[0]
            for i in range(1, HALF // 16):
                total = total + kept[i]
            seen = jnp.sum(total.astype(F32), axis=0, keepdims=True)
            for i in range(chunk):
                seen_ref[quantity, start + i : start + i + 1, :] = seen[:, i * LANES : (i + 1) * LANES]

    hot_quantity = lax.axis_index("far") == 3
    own_heat = jnp.where(hot_quantity, 1.5, 1.0).astype(F32)
    own_latent = jnp.where(hot_quantity, LATENT, 0.0).astype(F32)
    active = given(CELL) >= 0.0
    mass = held(MASS)
    evap_now = given(EVAP) * jax.nn.sigmoid(seen_ref[1] - held(TEMP))
    new_mass = jnp.where(active, mass * jnp.exp(-evap_now), mass)
    state_out[MASS] = new_mass
    unit_time = given(BASE) * jnp.exp(jnp.log(mass) * (2.0 / 3.0))
    work = ((OWN, own_heat, own_latent), (TEMP, 1.5, LATENT))
    for quantity, (which, heat, latent) in enumerate(work):
        seen, drop = seen_ref[quantity], held(which)
        relaxed = seen + (drop - seen) * jnp.exp(-1.0 / (unit_time * heat))
        new_drop = jnp.where(active, relaxed, drop)
        if which < state_out.shape[0]:
            state_out[which] = new_drop
        source = mass * drop - new_mass * new_drop - latent * (mass - new_mass)
        high = source.astype(BF16).astype(F32)
        part_ref[quantity] = high
        part_ref[2 + quantity] = source - high

    total = jnp.zeros((2 * slots, 4 * HALF), F32)
    for start in range(0, lines, chunk):
        hot, here = masks(start)
        parts = [
            jnp.where(here, packed(part_ref.at[i], start), zero).reshape(HALF, width)
            for i in range(4)
        ]
        total += dot(hot, jnp.concatenate(parts, axis=0), 1, 1)
    total = total[:, :LANES] + total[:, LANES:]
    lower, upper = total[:slots], total[slots:]
    left = iota(lower.shape, 1) < HALF
    first_rows = jnp.where(left, lower, pltpu.roll(upper, HALF, 1))
    second_rows = jnp.where(left, pltpu.roll(lower, HALF, 1), upper)
    send_ref[...] = merge_pair(first_rows, second_rows)


def call(body, out_shape, *operands, scalars=0, scratch=()):
    vmem = pl.BlockSpec(memory_space=pltpu.VMEM)
    smem = pl.BlockSpec(memory_space=pltpu.SMEM)
    return pl.pallas_call(
        body,
        out_shape=out_shape,
        in_specs=[smem] * scalars + [vmem] * (len(operands) - scalars),
        out_specs=jax.tree.map(lambda _: vmem, out_shape),
        scratch_shapes=list(scratch),
        compiler_params=pltpu.CompilerParams(vmem_limit_bytes=VMEM_LIMIT),
    )(*operands)


def exchange(rows, peers):
    shape = (peers, rows.shape[0] // peers, LANES)
    return lax.all_to_all(rows.reshape(shape), GROUP, 0, 0, tiled=True).reshape(rows.shape)


def swap(values):
    side = lax.axis_size("sec")
    pairs = [(i * side + j, j * side + i) for i in range(side) for j in range(side)]
    return lax.ppermute(values, ("sec", "far"), pairs)


def shards(
    gas_field,
    parcel_state,
    parcel_mass,
    base_time,
    evap_rate,
    slot_blocks,
    parcel_block_slot,
    parcel_cell,
    parcel_count,
):
    along_x, pencils, along_z = gas_field.shape[1:]
    per_pencil = along_z // LANES
    blocks = along_x * pencils * per_pencil
    peers, per_peer = slot_blocks.shape[1:]
    slots = peers * per_peer
    lines = parcel_mass.shape[0] // LANES
    rows = 2 * slots

    def shape(dims, kind=F32):
        return jax.ShapeDtypeStruct(dims, kind)

    lists = swap(slot_blocks)
    own_gas = gas_field.reshape(along_x, pencils, per_pencil, LANES)
    own_gas = jnp.swapaxes(own_gas, 1, 2).reshape(blocks, LANES)
    own_drop = parcel_state.reshape(lines, LANES)
    together = lax.all_gather(
        jnp.concatenate([own_gas, own_drop], axis=0), "sec", axis=0, tiled=True
    )
    lists, together = lax.optimization_barrier((lists, together))
    wanted = call(
        functools.partial(order_kernel, per_peer, pencils, per_pencil, blocks),
        shape((rows, LANES), BF16),
        lists,
    )
    wanted = exchange(wanted, peers)
    pack = call(
        functools.partial(pack_kernel, slots),
        shape((2 * blocks + 7 * lines, LANES)),
        parcel_count,
        together,
        own_gas,
        own_drop,
        *(
            part.reshape(lines, LANES)
            for part in (parcel_mass, base_time, evap_rate, parcel_block_slot, parcel_cell)
        ),
        scalars=1,
    )
    pack = swap(pack)

    gas_shape = shape((2 * blocks, LANES))
    send_shape = shape((rows, LANES), BF16)
    pick, place, send = call(
        pick_kernel,
        (shape((rows, 2 * blocks), BF16), shape((2 * blocks, rows), BF16), send_shape),
        wanted,
        pack,
    )
    gas, state = pack, ()
    for substep in range(ITERS):
        last = substep == ITERS - 1
        recv = exchange(send, peers)
        state, source = call(
            functools.partial(parcel_kernel, 4, substep == 0),
            (shape((2 if last else 3, lines, LANES)), shape((rows, LANES))),
            recv,
            pack,
            *state,
            scratch=[pltpu.VMEM((2, lines, LANES), F32), pltpu.VMEM((4, lines, LANES), F32)],
        )
        source = exchange(source, peers)
        update = functools.partial(gas_kernel, pencils, per_pencil)
        if last:
            gas = call(update, shape((blocks, LANES)), source, gas, pick, place)
        else:
            gas, send = call(update, (gas_shape, send_shape), source, gas, pick, place)
            state = (state,)
    state = swap(state)
    gas = swap(gas).reshape(along_x, per_pencil, pencils, LANES)
    return (
        jnp.swapaxes(gas, 1, 2).reshape(gas_field.shape),
        state[OWN].reshape(parcel_state.shape),
        state[MASS].reshape(parcel_mass.shape),
    )


def solution(mesh):
    sec, row, col = (mesh.shape[name] for name in ("sec", "row", "col"))
    split = Mesh(mesh.devices.reshape(sec, row, sec, col // sec), ("sec", "row", "far", "near"))
    place = P(("row", "far", "near"))
    return jax.shard_map(
        shards,
        mesh=split,
        in_specs=(
            P("sec", "row", ("far", "near"), None),
            P("sec", ("row", "far", "near")),
            place,
            place,
            place,
            P(("row", "far", "near"), None, None),
            place,
            place,
            place,
        ),
        out_specs=(
            P("sec", "row", ("far", "near"), None),
            P("sec", ("row", "far", "near")),
            place,
        ),
        check_vma=False,
    )
```

time: 174 us -> 158 us (0.908)
  the two profiles are of different devices: /device:TPU:16 before, /device:TPU:22 now
where the time goes in v3:
time: 158 us
  blocking collectives  115 us (73%)
  starting transfers between devices  25.1 us (16%)
  Pallas kernels  7.79 us (5%)
  waiting for transfers between devices  5.52 us (3%)
  local copies, waits for them, and re-layouts  2.03 us (1%)
    all_to_all x8, blocking collectives, exchange(): lax.all_to_all(rows.reshape(shape), GROUP, 0, 0, tiled=True)  109 us
    ppermute x4, starting transfers between devices, swap(): return lax.ppermute(values, ('sec', 'far'), pairs)  20.6 us
    pallas_call x11, Pallas kernels, call(): pl.pallas_call(body, out_shape=out_shape, in_specs=[smem] * scalars + [vm...  7.79 us
    all_gather x1, blocking collectives, shards(): lax.all_gather(jnp.concatenate([own_gas, own_drop], axis=0), 'sec', axis=...  5.74 us
    all_to_all x1, starting transfers between devices, exchange(): lax.all_to_all(rows.reshape(shape), GROUP, 0, 0, tiled=True)  4.51 us
    all_to_all x1, waiting for transfers between devices, exchange(): lax.all_to_all(rows.reshape(shape), GROUP, 0, 0, tiled=True)  3.28 us
  transfers between devices with their start and end apart: 5, of which 2 were waited for; matrix products, arithmetic and copies ran while one was open for 1% of the time, Pallas kernels for 0%

profile of v3, /device:TPU:22, one launch (start us, length us, event | category | flops | bytes accessed | tf_op | source)
XLA Modules:
  0.0 157.6 jit_solution(6017798461595550528)
XLA Ops:
  0.6 0.8 copy.12
  1.4 7.0 %collective-permute-start = (s32[1,32,4]{2,1,0:T(8,128)S(1)}, s32[1,32,4]{2,1,0:T(8,128)S(1)}, u32[]{:S(2)}, u32[]{:S(2)}) collective-permute-start(s32[1,32,4]{2,1,0:T(8,128)S(1)} %copy.12), channel_id=1, source_target_pairs={{0,0},{8,256},{16,512},{24,768},{256,8},{264,264},{272,520},{280,7... | collective-permute-start | bytes 1544 | tf_op jit(solution)/shard_map/ppermute | solution.py:245
  8.5 0.8 pad_maximum_fusion
  9.3 0.0 copy-start.4
  9.3 0.0 copy-start.6
  9.3 5.7 %all_gather.3.temp_ref = f32[384,128]{1,0:T(8,128)S(1)} all-gather(f32[96,128]{1,0:T(8,128)S(1)} %pad_maximum_fusion), channel_id=1, replica_groups=mesh['sec'=4,'row'=8,'far'=4,'near'=8] {'sec'}, dimensions={0}, use_global_device_ids=true | all-gather | bytes 245760 | tf_op jit(solution)/shard_map/all_gather | solution.py:274
  15.8 1.9 %collective-permute-start.1 = (f32[352,128]{1,0:T(8,128)S(1)}, f32[352,128]{1,0:T(8,128)S(1)}, u32[]{:S(2)}, u32[]{:S(2)}) collective-permute-start(f32[352,128]{1,0:T(8,128)S(1)} %shard_map.113), channel_id=1, source_target_pairs={{0,0},{8,256},{16,512},{24,768},{256,8},{264,264},{272,520},{280,7... | collective-permute-start | bytes 540680 | tf_op jit(solution)/shard_map/ppermute | solution.py:245
  17.7 0.3 shard_map.112
  18.0 25.9 %all_to_all.45 = bf16[32,8,128]{2,1,0:T(8,128)(2,1)S(1)} all-to-all(bf16[32,8,128]{2,1,0:T(8,128)(2,1)S(1)} %bitcast.41), channel_id=1, replica_groups=mesh['sec'=4,'row'=8,'far'=4,'near'=8] {'sec','near'}, dimensions={0} | all-to-all | bytes 131072 | tf_op jit(solution)/shard_map/all_to_all | solution.py:239
  43.8 0.2 shard_map.114
  44.0 11.5 %all_to_all.46 = bf16[32,8,128]{2,1,0:T(8,128)(2,1)S(1)} all-to-all(bf16[32,8,128]{2,1,0:T(8,128)(2,1)S(1)} %bitcast.52), channel_id=1, replica_groups=mesh['sec'=4,'row'=8,'far'=4,'near'=8] {'sec','near'}, dimensions={0} | all-to-all | bytes 131072 | tf_op jit(solution)/shard_map/all_to_all | solution.py:239
  55.5 1.4 shard_map.115
  56.9 12.5 %all_to_all.47 = f32[32,8,128]{2,1,0:T(8,128)S(1)} all-to-all(f32[32,8,128]{2,1,0:T(8,128)S(1)} %bitcast.51), channel_id=1, replica_groups=mesh['sec'=4,'row'=8,'far'=4,'near'=8] {'sec','near'}, dimensions={0} | all-to-all | bytes 262144 | tf_op jit(solution)/shard_map/all_to_all | solution.py:239
  69.4 0.3 shard_map.116
  69.8 11.4 %all_to_all.48 = bf16[32,8,128]{2,1,0:T(8,128)(2,1)S(1)} all-to-all(bf16[32,8,128]{2,1,0:T(8,128)(2,1)S(1)} %bitcast.55), channel_id=1, replica_groups=mesh['sec'=4,'row'=8,'far'=4,'near'=8] {'sec','near'}, dimensions={0} | all-to-all | bytes 131072 | tf_op jit(solution)/shard_map/all_to_all | solution.py:239
  81.2 1.4 shard_map.117
  82.6 12.5 %all_to_all.49 = f32[32,8,128]{2,1,0:T(8,128)S(1)} all-to-all(f32[32,8,128]{2,1,0:T(8,128)S(1)} %bitcast.49), channel_id=1, replica_groups=mesh['sec'=4,'row'=8,'far'=4,'near'=8] {'sec','near'}, dimensions={0} | all-to-all | bytes 262144 | tf_op jit(solution)/shard_map/all_to_all | solution.py:239
  95.1 0.3 shard_map.118
  95.5 11.4 %all_to_all.50 = bf16[32,8,128]{2,1,0:T(8,128)(2,1)S(1)} all-to-all(bf16[32,8,128]{2,1,0:T(8,128)(2,1)S(1)} %bitcast.53), channel_id=1, replica_groups=mesh['sec'=4,'row'=8,'far'=4,'near'=8] {'sec','near'}, dimensions={0} | all-to-all | bytes 131072 | tf_op jit(solution)/shard_map/all_to_all | solution.py:239
  106.8 1.4 shard_map.119
  108.2 12.5 %all_to_all.51 = f32[32,8,128]{2,1,0:T(8,128)S(1)} all-to-all(f32[32,8,128]{2,1,0:T(8,128)S(1)} %bitcast.50), channel_id=1, replica_groups=mesh['sec'=4,'row'=8,'far'=4,'near'=8] {'sec','near'}, dimensions={0} | all-to-all | bytes 262144 | tf_op jit(solution)/shard_map/all_to_all | solution.py:239
  120.8 0.3 shard_map.120
  121.1 11.4 %all_to_all.52 = bf16[32,8,128]{2,1,0:T(8,128)(2,1)S(1)} all-to-all(bf16[32,8,128]{2,1,0:T(8,128)(2,1)S(1)} %bitcast.54), channel_id=1, replica_groups=mesh['sec'=4,'row'=8,'far'=4,'near'=8] {'sec','near'}, dimensions={0} | all-to-all | bytes 131072 | tf_op jit(solution)/shard_map/all_to_all | solution.py:239
  132.5 2.0 %shard_map.121 = (f32[2,32,128]{2,1,0:T(8,128)S(1)}, f32[256,128]{1,0:T(8,128)}) custom-call(bf16[256,128]{1,0:T(8,128)(2,1)S(1)} %bitcast.43, f32[352,128]{1,0:T(8,128)S(1)} %collective-permute-done.1.pack_ref.gas_ref, f32[3,32,128]{2,1,0:T(8,128)S(1)} %get-tuple-element.37.refs_0_), custom_call_target="tpu_custom_call" | custom-call | tf_op jit(solution)/shard_map/pallas_call | solution.py:227
  134.5 4.5 %all-to-all-start.8 = ((f32[32,8,128]{2,1,0:T(8,128)}), f32[32,8,128]{2,1,0:T(8,128)S(1)}, u32[]{:S(2)}, u32[]{:S(2)}) async-start(f32[32,8,128]{2,1,0:T(8,128)} %bitcast.27), calls=%async_computation.8 | async-start | bytes 262144 | tf_op jit(solution)/shard_map/all_to_all | solution.py:239
  139.0 5.6 %collective-permute-start.3 = (f32[2,32,128]{2,1,0:T(8,128)S(1)}, f32[2,32,128]{2,1,0:T(8,128)S(1)}, u32[]{:S(2)}, u32[]{:S(2)}) collective-permute-start(f32[2,32,128]{2,1,0:T(8,128)S(1)} %get-tuple-element.40), channel_id=1, source_target_pairs={{0,0},{8,256},{16,512},{24,768},{256,8},{264,264},{272,520},{280,7... | collective-permute-start | bytes 98312 | tf_op jit(solution)/shard_map/ppermute | solution.py:245
  144.6 3.3 %all-to-all-done.8 = f32[32,8,128]{2,1,0:T(8,128)S(1)} async-done(((f32[32,8,128]{2,1,0:T(8,128)}), f32[32,8,128]{2,1,0:T(8,128)S(1)}, u32[]{:S(2)}, u32[]{:S(2)}) %all-to-all-start.8) | async-done | bytes 131104 | tf_op jit(solution)/shard_map/all_to_all | solution.py:239
  147.9 0.2 shard_map.122
  148.1 6.1 %collective-permute-start.2 = (f32[64,128]{1,0:T(8,128)S(1)}, f32[64,128]{1,0:T(8,128)S(1)}, u32[]{:S(2)}, u32[]{:S(2)}) collective-permute-start(f32[64,128]{1,0:T(8,128)S(1)} %shard_map.122), channel_id=1, source_target_pairs={{0,0},{8,256},{16,512},{24,768},{256,8},{264,264},{272,520},{280,7... | collective-permute-start | bytes 98312 | tf_op jit(solution)/shard_map/ppermute | solution.py:245
  154.2 0.6 slice_bitcast_fusion
  154.8 2.2 %collective-permute-done.2 = f32[64,128]{1,0:T(8,128)S(1)} collective-permute-done((f32[64,128]{1,0:T(8,128)S(1)}, f32[64,128]{1,0:T(8,128)S(1)}, u32[]{:S(2)}, u32[]{:S(2)}) %collective-permute-start.2) | collective-permute-done | bytes 32800 | tf_op jit(solution)/shard_map/ppermute | solution.py:245
  157.0 0.6 copy.17
  (16 shorter events, 0.1 us)
Async XLA Ops:
  0.6 7.8 %copy-start.1 = (f32[1,4096]{1,0:T(1,128)S(1)}, f32[1,4096]{1,0:T(1,128)}, u32[]{:S(2)}) copy-start(f32[1,4096]{1,0:T(1,128)} %param.10) | copy-start | bytes 49156
  1.4 14.3 %collective-permute-start = (s32[1,32,4]{2,1,0:T(8,128)S(1)}, s32[1,32,4]{2,1,0:T(8,128)S(1)}, u32[]{:S(2)}, u32[]{:S(2)}) collective-permute-start(s32[1,32,4]{2,1,0:T(8,128)S(1)} %copy.12), channel_id=1, source_target_pairs={{0,0},{8,256},{16,512},{24,768},{256,8},{264,264},{272,520},{280,7... | collective-permute-start | bytes 1544 | tf_op jit(solution)/shard_map/ppermute | solution.py:245
  9.2 6.5 %copy-start = (f32[1,4,2,1024]{3,2,1,0:T(2,128)S(1)}, f32[1,4,2,1024]{3,2,1,0:T(2,128)}, u32[]{:S(2)}) copy-start(f32[1,4,2,1024]{3,2,1,0:T(2,128)} %param.9) | copy-start | bytes 98308
  9.2 6.5 %copy-start.2 = (f32[4096]{0:T(1024)S(1)}, f32[4096]{0:T(1024)}, u32[]{:S(2)}) copy-start(f32[4096]{0:T(1024)} %param.11) | copy-start | bytes 49156
  9.2 6.5 %copy-start.3 = (f32[4096]{0:T(1024)S(1)}, f32[4096]{0:T(1024)}, u32[]{:S(2)}) copy-start(f32[4096]{0:T(1024)} %param.12) | copy-start | bytes 49156
  9.3 6.5 %copy-start.4 = (f32[4096]{0:T(1024)S(1)}, f32[4096]{0:T(1024)}, u32[]{:S(2)}) copy-start(f32[4096]{0:T(1024)} %param.13) | copy-start | bytes 49156
  9.3 6.5 %copy-start.5 = (s32[4096]{0:T(1024)S(1)}, s32[4096]{0:T(1024)}, u32[]{:S(2)}) copy-start(s32[4096]{0:T(1024)} %param.15) | copy-start | bytes 49156
  9.3 6.5 %copy-start.6 = (s32[4096]{0:T(1024)S(1)}, s32[4096]{0:T(1024)}, u32[]{:S(2)}) copy-start(s32[4096]{0:T(1024)} %param.16) | copy-start | bytes 49156
  15.8 28.1 %collective-permute-start.1 = (f32[352,128]{1,0:T(8,128)S(1)}, f32[352,128]{1,0:T(8,128)S(1)}, u32[]{:S(2)}, u32[]{:S(2)}) collective-permute-start(f32[352,128]{1,0:T(8,128)S(1)} %shard_map.113), channel_id=1, source_target_pairs={{0,0},{8,256},{16,512},{24,768},{256,8},{264,264},{272,520},{280,7... | collective-permute-start | bytes 540680 | tf_op jit(solution)/shard_map/ppermute | solution.py:245
  134.5 13.4 %all-to-all-start.8 = ((f32[32,8,128]{2,1,0:T(8,128)}), f32[32,8,128]{2,1,0:T(8,128)S(1)}, u32[]{:S(2)}, u32[]{:S(2)}) async-start(f32[32,8,128]{2,1,0:T(8,128)} %bitcast.27), calls=%async_computation.8 | async-start | bytes 262144 | tf_op jit(solution)/shard_map/all_to_all | solution.py:239
  139.0 15.1 %collective-permute-start.3 = (f32[2,32,128]{2,1,0:T(8,128)S(1)}, f32[2,32,128]{2,1,0:T(8,128)S(1)}, u32[]{:S(2)}, u32[]{:S(2)}) collective-permute-start(f32[2,32,128]{2,1,0:T(8,128)S(1)} %get-tuple-element.40), channel_id=1, source_target_pairs={{0,0},{8,256},{16,512},{24,768},{256,8},{264,264},{272,520},{280,7... | collective-permute-start | bytes 98312 | tf_op jit(solution)/shard_map/ppermute | solution.py:245
  148.1 8.9 %collective-permute-start.2 = (f32[64,128]{1,0:T(8,128)S(1)}, f32[64,128]{1,0:T(8,128)S(1)}, u32[]{:S(2)}, u32[]{:S(2)}) collective-permute-start(f32[64,128]{1,0:T(8,128)S(1)} %shard_map.122), channel_id=1, source_target_pairs={{0,0},{8,256},{16,512},{24,768},{256,8},{264,264},{272,520},{280,7... | collective-permute-start | bytes 98312 | tf_op jit(solution)/shard_map/ppermute | solution.py:245

commit v4 on v3

--- a/solution.py
+++ b/solution.py
@@ -36,9 +36,11 @@
     )
 
 
-def halves(values):
-    high = values.astype(BF16)
-    return high, (values - high.astype(F32)).astype(BF16)
+def thirds(values):
+    high = values.astype(BF16).astype(F32)
+    rest = values - high
+    middle = rest.astype(BF16).astype(F32)
+    return high, middle, rest - middle
 
 
 def split_pair(rows):
@@ -60,21 +62,24 @@
     return jnp.stack([even, odd], axis=1).reshape(2 * shape[0] * 8, LANES)
 
 
-def order_kernel(per_peer, pencils, per_pencil, blocks, list_ref, rows_ref):
+def list_kernel(side, pencils, per_pencil, list_ref, out_ref):
     block = list_ref[0]
     first = block // (pencils * per_pencil)
     rest = block - first * (pencils * per_pencil)
     pencil = rest // per_pencil
-    place = first * (pencils * per_pencil) + (rest - pencil * per_pencil) * pencils + pencil
-    rows, peers = rows_ref.shape[0], block.shape[0]
-    each = rows // peers
-    owner = (iota((rows, peers), 0) // each == iota((rows, peers), 1)).astype(BF16)
-    spread = dot(owner, place.astype(F32).astype(BF16))
-    within = iota(spread.shape, 0) % each
-    kept = jnp.where(within % per_peer == iota(spread.shape, 1), spread, 0.0)
-    value = jnp.sum(kept, axis=1, keepdims=True)
-    value = value + (blocks * (within[:, :1] // per_peer)).astype(F32)
-    rows_ref[...] = jnp.broadcast_to(value, rows_ref.shape).astype(BF16)
+    line = first * (pencils * per_pencil) + (rest - pencil * per_pencil) * pencils + pencil
+    peers, per_peer = block.shape
+    slots = peers * per_peer
+    owner = (iota((slots, peers), 0) // per_peer == iota((slots, peers), 1)).astype(BF16)
+    spread = dot(owner, line.astype(F32).astype(BF16))
+    mine = iota(spread.shape, 0) % per_peer == iota(spread.shape, 1)
+    value = jnp.sum(jnp.where(mine, spread, 0.0), axis=1, keepdims=True)
+    value = jnp.broadcast_to(value, (slots, LANES))
+    height = slots // side
+    for i in range(side):
+        for j in range(side):
+            at = (i * side + j) * height
+            out_ref[at : at + height] = value[i * height : (i + 1) * height]
 
 
 def pack_kernel(
@@ -101,19 +106,21 @@
     store(CELL, jnp.where(active, cell_ref[...] - HALF * upper, -1).astype(F32))
 
 
-def pick_kernel(wanted_ref, pack_ref, pick_ref, place_ref, send_ref):
-    wanted = wanted_ref[...].astype(F32).astype(jnp.int32)
-    pick = (wanted == iota(wanted.shape, 1)).astype(F32)
+def pick_kernel(list_ref, pack_ref, pick_ref, place_ref, send_ref):
+    rows, columns = pick_ref.shape
+    lines = list_ref[: rows // 2]
+    wanted = merge_pair(lines, lines + columns / 2)
+    pick = (wanted == iota((rows, columns), 1).astype(F32)).astype(F32)
     pick_ref[...] = pick.astype(BF16)
     place_ref[...] = pick.T.astype(BF16)
-    gas = pack_ref[: wanted.shape[1]]
+    gas = pack_ref[:columns]
     send_ref[...] = dot(pick.astype(BF16), gas.astype(BF16)).astype(BF16)
 
 
 def gas_kernel(stride, per_pencil, source_ref, gas_ref, pick_ref, place_ref, gas_out, send_ref=None):
-    high, low = halves(source_ref[...])
     place = place_ref[...]
-    deposit = dot(place, high) + dot(place, low)
+    high, middle, low = (dot(place, part.astype(BF16)) for part in thirds(source_ref[...]))
+    deposit = high + (middle + low)
     rows = place.shape[0]
     gas = gas_ref[:rows]
     block = iota(gas.shape, 0) // stride % per_pencil
@@ -201,19 +208,18 @@
         if which < state_out.shape[0]:
             state_out[which] = new_drop
         source = mass * drop - new_mass * new_drop - latent * (mass - new_mass)
-        high = source.astype(BF16).astype(F32)
-        part_ref[quantity] = high
-        part_ref[2 + quantity] = source - high
-
-    total = jnp.zeros((2 * slots, 4 * HALF), F32)
+        for i, part in enumerate(thirds(source)):
+            part_ref[2 * i + quantity] = part
+
+    total = jnp.zeros((2 * slots, 6 * HALF), F32)
     for start in range(0, lines, chunk):
         hot, here = masks(start)
         parts = [
             jnp.where(here, packed(part_ref.at[i], start), zero).reshape(HALF, width)
-            for i in range(4)
+            for i in range(6)
         ]
         total += dot(hot, jnp.concatenate(parts, axis=0), 1, 1)
-    total = total[:, :LANES] + total[:, LANES:]
+    total = total[:, :LANES] + (total[:, LANES : 2 * LANES] + total[:, 2 * LANES :])
     lower, upper = total[:slots], total[slots:]
     left = iota(lower.shape, 1) < HALF
     first_rows = jnp.where(left, lower, pltpu.roll(upper, HALF, 1))
@@ -267,20 +273,20 @@
     def shape(dims, kind=F32):
         return jax.ShapeDtypeStruct(dims, kind)
 
-    lists = swap(slot_blocks)
+    side = lax.axis_size("sec")
+    lists = call(
+        functools.partial(list_kernel, side, pencils, per_pencil),
+        shape((side * slots, LANES)),
+        slot_blocks,
+    ).reshape(side * peers, per_peer, LANES)
+    lists = lax.all_to_all(lists, ("sec", "far", "near"), 0, 0, tiled=True)
+    lists = lists.reshape(side * slots, LANES)
     own_gas = gas_field.reshape(along_x, pencils, per_pencil, LANES)
     own_gas = jnp.swapaxes(own_gas, 1, 2).reshape(blocks, LANES)
     own_drop = parcel_state.reshape(lines, LANES)
     together = lax.all_gather(
         jnp.concatenate([own_gas, own_drop], axis=0), "sec", axis=0, tiled=True
     )
-    lists, together = lax.optimization_barrier((lists, together))
-    wanted = call(
-        functools.partial(order_kernel, per_peer, pencils, per_pencil, blocks),
-        shape((rows, LANES), BF16),
-        lists,
-    )
-    wanted = exchange(wanted, peers)
     pack = call(
         functools.partial(pack_kernel, slots),
         shape((2 * blocks + 7 * lines, LANES)),
@@ -301,7 +307,7 @@
     pick, place, send = call(
         pick_kernel,
         (shape((rows, 2 * blocks), BF16), shape((2 * blocks, rows), BF16), send_shape),
-        wanted,
+        lists,
         pack,
     )
     gas, state = pack, ()
@@ -314,7 +320,7 @@
             recv,
             pack,
             *state,
-            scratch=[pltpu.VMEM((2, lines, LANES), F32), pltpu.VMEM((4, lines, LANES), F32)],
+            scratch=[pltpu.VMEM((2, lines, LANES), F32), pltpu.VMEM((6, lines, LANES), F32)],
         )
         source = exchange(source, peers)
         update = functools.partial(gas_kernel, pencils, per_pencil)

time: 158 us -> 169 us (1.070)
  the two profiles are of different devices: /device:TPU:22 before, /device:TPU:16 now
where the time goes in v4:
time: 169 us
  blocking collectives  94.3 us (56%)
  starting transfers between devices  42.6 us (25%)
  waiting for transfers between devices  18 us (11%)
  Pallas kernels  10.3 us (6%)
  local copies, waits for them, and re-layouts  2.03 us (1%)
    all_to_all x7, blocking collectives, exchange(): lax.all_to_all(rows.reshape(shape), GROUP, 0, 0, tiled=True)  87.6 us
    all_to_all x1, starting transfers between devices, shards(): lists = lax.all_to_all(lists, ('sec', 'far', 'near'), 0, 0, tiled=True)  24.5 us
    ppermute x3, starting transfers between devices, swap(): return lax.ppermute(values, ('sec', 'far'), pairs)  13.5 us
    ppermute x3, waiting for transfers between devices, swap(): return lax.ppermute(values, ('sec', 'far'), pairs)  11.9 us
    pallas_call x11, Pallas kernels, call(): pl.pallas_call(body, out_shape=out_shape, in_specs=[smem] * scalars + [vm...  10.3 us
    all_gather x1, blocking collectives, shards(): lax.all_gather(jnp.concatenate([own_gas, own_drop], axis=0), 'sec', axis=...  6.74 us
    all_to_all x1, waiting for transfers between devices, exchange(): lax.all_to_all(rows.reshape(shape), GROUP, 0, 0, tiled=True)  6.06 us
    all_to_all x1, starting transfers between devices, exchange(): lax.all_to_all(rows.reshape(shape), GROUP, 0, 0, tiled=True)  4.52 us
  transfers between devices with their start and end apart: 5, of which 3 were waited for; matrix products, arithmetic and copies ran while one was open for 0% of the time, Pallas kernels for 0%

profile of v4, /device:TPU:16, one launch (start us, length us, event | category | flops | bytes accessed | tf_op | source)
XLA Modules:
  0.0 168.7 jit_solution(3899633451610963084)
XLA Ops:
  0.6 0.8 copy.12.list_ref
  1.4 0.9 shard_map.112
  2.3 24.5 %all-to-all-start = ((f32[128,4,128]{2,1,0:T(4,128)}), f32[128,4,128]{2,1,0:T(4,128)S(1)}, u32[]{:S(2)}, u32[]{:S(2)}) async-start(f32[128,4,128]{2,1,0:T(4,128)} %bitcast), calls=%async_computation | async-start | bytes 524288 | tf_op jit(solution)/shard_map/all_to_all | solution.py:282
  27.5 0.0 copy-start.2
  27.6 0.0 copy-start.5
  27.6 0.0 copy-start.6
  27.6 6.7 %all_gather.3.temp_ref = f32[384,128]{1,0:T(8,128)S(1)} all-gather(f32[96,128]{1,0:T(8,128)S(1)} %pad_maximum_fusion), channel_id=1, replica_groups=mesh['sec'=4,'row'=8,'far'=4,'near'=8] {'sec'}, dimensions={0}, use_global_device_ids=true | all-gather | bytes 245760 | tf_op jit(solution)/shard_map/all_gather | solution.py:287
  34.4 7.4 %collective-permute-start = (f32[352,128]{1,0:T(8,128)S(1)}, f32[352,128]{1,0:T(8,128)S(1)}, u32[]{:S(2)}, u32[]{:S(2)}) collective-permute-start(f32[352,128]{1,0:T(8,128)S(1)} %shard_map.113), channel_id=1, source_target_pairs={{0,0},{8,256},{16,512},{24,768},{256,8},{264,264},{272,520},{280,7... | collective-permute-start | bytes 540680 | tf_op jit(solution)/shard_map/ppermute | solution.py:251
  41.9 7.0 %collective-permute-done.pack_ref.gas_ref = f32[352,128]{1,0:T(8,128)S(1)} collective-permute-done((f32[352,128]{1,0:T(8,128)S(1)}, f32[352,128]{1,0:T(8,128)S(1)}, u32[]{:S(2)}, u32[]{:S(2)}) %collective-permute-start) | collective-permute-done | bytes 180256 | tf_op jit(solution)/shard_map/ppermute | solution.py:251
  48.8 0.2 shard_map.114
  49.0 15.8 %all_to_all.45 = bf16[32,8,128]{2,1,0:T(8,128)(2,1)S(1)} all-to-all(bf16[32,8,128]{2,1,0:T(8,128)(2,1)S(1)} %bitcast.51), channel_id=1, replica_groups=mesh['sec'=4,'row'=8,'far'=4,'near'=8] {'sec','near'}, dimensions={0} | all-to-all | bytes 131072 | tf_op jit(solution)/shard_map/all_to_all | solution.py:245
  64.8 1.8 %shard_map.115 = (f32[3,32,128]{2,1,0:T(8,128)S(1)}, f32[256,128]{1,0:T(8,128)S(1)}) custom-call(bf16[256,128]{1,0:T(8,128)(2,1)S(1)} %bitcast.45, f32[352,128]{1,0:T(8,128)S(1)} %collective-permute-done.pack_ref.gas_ref), custom_call_target="tpu_custom_call" | custom-call | tf_op jit(solution)/shard_map/pallas_call | solution.py:233
  66.6 12.5 %all_to_all.46 = f32[32,8,128]{2,1,0:T(8,128)S(1)} all-to-all(f32[32,8,128]{2,1,0:T(8,128)S(1)} %bitcast.50), channel_id=1, replica_groups=mesh['sec'=4,'row'=8,'far'=4,'near'=8] {'sec','near'}, dimensions={0} | all-to-all | bytes 262144 | tf_op jit(solution)/shard_map/all_to_all | solution.py:245
  79.2 0.4 shard_map.116
  79.6 11.4 %all_to_all.47 = bf16[32,8,128]{2,1,0:T(8,128)(2,1)S(1)} all-to-all(bf16[32,8,128]{2,1,0:T(8,128)(2,1)S(1)} %bitcast.54), channel_id=1, replica_groups=mesh['sec'=4,'row'=8,'far'=4,'near'=8] {'sec','near'}, dimensions={0} | all-to-all | bytes 131072 | tf_op jit(solution)/shard_map/all_to_all | solution.py:245
  90.9 1.8 %shard_map.117 = (f32[3,32,128]{2,1,0:T(8,128)S(1)}, f32[256,128]{1,0:T(8,128)S(1)}) custom-call(bf16[256,128]{1,0:T(8,128)(2,1)S(1)} %bitcast.43, f32[352,128]{1,0:T(8,128)S(1)} %collective-permute-done.pack_ref.gas_ref, f32[3,32,128]{2,1,0:T(8,128)S(1)} %get-tuple-element.25.refs_0_), custom_call_target="tpu_custom_call" | custom-call | tf_op jit(solution)/shard_map/pallas_call | solution.py:233
  92.7 12.5 %all_to_all.48 = f32[32,8,128]{2,1,0:T(8,128)S(1)} all-to-all(f32[32,8,128]{2,1,0:T(8,128)S(1)} %bitcast.48), channel_id=1, replica_groups=mesh['sec'=4,'row'=8,'far'=4,'near'=8] {'sec','near'}, dimensions={0} | all-to-all | bytes 262144 | tf_op jit(solution)/shard_map/all_to_all | solution.py:245
  105.3 0.4 shard_map.118
  105.7 11.4 %all_to_all.49 = bf16[32,8,128]{2,1,0:T(8,128)(2,1)S(1)} all-to-all(bf16[32,8,128]{2,1,0:T(8,128)(2,1)S(1)} %bitcast.52), channel_id=1, replica_groups=mesh['sec'=4,'row'=8,'far'=4,'near'=8] {'sec','near'}, dimensions={0} | all-to-all | bytes 131072 | tf_op jit(solution)/shard_map/all_to_all | solution.py:245
  117.1 1.8 %shard_map.119 = (f32[3,32,128]{2,1,0:T(8,128)S(1)}, f32[256,128]{1,0:T(8,128)S(1)}) custom-call(bf16[256,128]{1,0:T(8,128)(2,1)S(1)} %bitcast.44, f32[352,128]{1,0:T(8,128)S(1)} %collective-permute-done.pack_ref.gas_ref, f32[3,32,128]{2,1,0:T(8,128)S(1)} %get-tuple-element.29.refs_0_), custom_call_target="tpu_custom_call" | custom-call | tf_op jit(solution)/shard_map/pallas_call | solution.py:233
  118.9 12.5 %all_to_all.50 = f32[32,8,128]{2,1,0:T(8,128)S(1)} all-to-all(f32[32,8,128]{2,1,0:T(8,128)S(1)} %bitcast.49), channel_id=1, replica_groups=mesh['sec'=4,'row'=8,'far'=4,'near'=8] {'sec','near'}, dimensions={0} | all-to-all | bytes 262144 | tf_op jit(solution)/shard_map/all_to_all | solution.py:245
  131.4 0.4 shard_map.120
  131.8 11.4 %all_to_all.51 = bf16[32,8,128]{2,1,0:T(8,128)(2,1)S(1)} all-to-all(bf16[32,8,128]{2,1,0:T(8,128)(2,1)S(1)} %bitcast.53), channel_id=1, replica_groups=mesh['sec'=4,'row'=8,'far'=4,'near'=8] {'sec','near'}, dimensions={0} | all-to-all | bytes 131072 | tf_op jit(solution)/shard_map/all_to_all | solution.py:245
  143.2 2.5 %shard_map.121 = (f32[2,32,128]{2,1,0:T(8,128)S(1)}, f32[256,128]{1,0:T(8,128)}) custom-call(bf16[256,128]{1,0:T(8,128)(2,1)S(1)} %bitcast.42, f32[352,128]{1,0:T(8,128)S(1)} %collective-permute-done.pack_ref.gas_ref, f32[3,32,128]{2,1,0:T(8,128)S(1)} %get-tuple-element.33.refs_0_), custom_call_target="tpu_custom_call" | custom-call | tf_op jit(solution)/shard_map/pallas_call | solution.py:233
  145.6 4.5 %all-to-all-start.8 = ((f32[32,8,128]{2,1,0:T(8,128)}), f32[32,8,128]{2,1,0:T(8,128)S(1)}, u32[]{:S(2)}, u32[]{:S(2)}) async-start(f32[32,8,128]{2,1,0:T(8,128)} %bitcast.25), calls=%async_computation.8 | async-start | bytes 262144 | tf_op jit(solution)/shard_map/all_to_all | solution.py:245
  150.2 2.8 %collective-permute-start.2 = (f32[2,32,128]{2,1,0:T(8,128)S(1)}, f32[2,32,128]{2,1,0:T(8,128)S(1)}, u32[]{:S(2)}, u32[]{:S(2)}) collective-permute-start(f32[2,32,128]{2,1,0:T(8,128)S(1)} %get-tuple-element.36), channel_id=1, source_target_pairs={{0,0},{8,256},{16,512},{24,768},{256,8},{264,264},{272,520},{280,7... | collective-permute-start | bytes 98312 | tf_op jit(solution)/shard_map/ppermute | solution.py:251
  153.0 6.1 %all-to-all-done.8 = f32[32,8,128]{2,1,0:T(8,128)S(1)} async-done(((f32[32,8,128]{2,1,0:T(8,128)}), f32[32,8,128]{2,1,0:T(8,128)S(1)}, u32[]{:S(2)}, u32[]{:S(2)}) %all-to-all-start.8) | async-done | bytes 131104 | tf_op jit(solution)/shard_map/all_to_all | solution.py:245
  159.1 0.2 shard_map.122
  159.3 3.3 %collective-permute-start.1 = (f32[64,128]{1,0:T(8,128)S(1)}, f32[64,128]{1,0:T(8,128)S(1)}, u32[]{:S(2)}, u32[]{:S(2)}) collective-permute-start(f32[64,128]{1,0:T(8,128)S(1)} %shard_map.122), channel_id=1, source_target_pairs={{0,0},{8,256},{16,512},{24,768},{256,8},{264,264},{272,520},{280,7... | collective-permute-start | bytes 98312 | tf_op jit(solution)/shard_map/ppermute | solution.py:251
  162.6 0.6 slice_bitcast_fusion
  163.2 4.9 %collective-permute-done.1 = f32[64,128]{1,0:T(8,128)S(1)} collective-permute-done((f32[64,128]{1,0:T(8,128)S(1)}, f32[64,128]{1,0:T(8,128)S(1)}, u32[]{:S(2)}, u32[]{:S(2)}) %collective-permute-start.1) | collective-permute-done | bytes 32800 | tf_op jit(solution)/shard_map/ppermute | solution.py:251
  168.1 0.6 copy.17
  (15 shorter events, 0.1 us)
Async XLA Ops:
  2.3 25.2 %copy-start = (f32[1,4,2,1024]{3,2,1,0:T(2,128)S(1)}, f32[1,4,2,1024]{3,2,1,0:T(2,128)}, u32[]{:S(2)}) copy-start(f32[1,4,2,1024]{3,2,1,0:T(2,128)} %param.9) | copy-start | bytes 98308
  2.3 25.2 %copy-start.1 = (f32[1,4096]{1,0:T(1,128)S(1)}, f32[1,4096]{1,0:T(1,128)}, u32[]{:S(2)}) copy-start(f32[1,4096]{1,0:T(1,128)} %param.10) | copy-start | bytes 49156
  2.3 46.5 %all-to-all-start = ((f32[128,4,128]{2,1,0:T(4,128)}), f32[128,4,128]{2,1,0:T(4,128)S(1)}, u32[]{:S(2)}, u32[]{:S(2)}) async-start(f32[128,4,128]{2,1,0:T(4,128)} %bitcast), calls=%async_computation | async-start | bytes 524288 | tf_op jit(solution)/shard_map/all_to_all | solution.py:282
  27.5 6.8 %copy-start.2 = (f32[4096]{0:T(1024)S(1)}, f32[4096]{0:T(1024)}, u32[]{:S(2)}) copy-start(f32[4096]{0:T(1024)} %param.11) | copy-start | bytes 49156
  27.6 6.8 %copy-start.3 = (f32[4096]{0:T(1024)S(1)}, f32[4096]{0:T(1024)}, u32[]{:S(2)}) copy-start(f32[4096]{0:T(1024)} %param.12) | copy-start | bytes 49156
  27.6 6.8 %copy-start.4 = (f32[4096]{0:T(1024)S(1)}, f32[4096]{0:T(1024)}, u32[]{:S(2)}) copy-start(f32[4096]{0:T(1024)} %param.13) | copy-start | bytes 49156
  27.6 6.8 %copy-start.5 = (s32[4096]{0:T(1024)S(1)}, s32[4096]{0:T(1024)}, u32[]{:S(2)}) copy-start(s32[4096]{0:T(1024)} %param.15) | copy-start | bytes 49156
  27.6 6.8 %copy-start.6 = (s32[4096]{0:T(1024)S(1)}, s32[4096]{0:T(1024)}, u32[]{:S(2)}) copy-start(s32[4096]{0:T(1024)} %param.16) | copy-start | bytes 49156
  34.4 14.4 %collective-permute-start = (f32[352,128]{1,0:T(8,128)S(1)}, f32[352,128]{1,0:T(8,128)S(1)}, u32[]{:S(2)}, u32[]{:S(2)}) collective-permute-start(f32[352,128]{1,0:T(8,128)S(1)} %shard_map.113), channel_id=1, source_target_pairs={{0,0},{8,256},{16,512},{24,768},{256,8},{264,264},{272,520},{280,7... | collective-permute-start | bytes 540680 | tf_op jit(solution)/shard_map/ppermute | solution.py:251
  145.6 13.4 %all-to-all-start.8 = ((f32[32,8,128]{2,1,0:T(8,128)}), f32[32,8,128]{2,1,0:T(8,128)S(1)}, u32[]{:S(2)}, u32[]{:S(2)}) async-start(f32[32,8,128]{2,1,0:T(8,128)} %bitcast.25), calls=%async_computation.8 | async-start | bytes 262144 | tf_op jit(solution)/shard_map/all_to_all | solution.py:245
  150.2 12.4 %collective-permute-start.2 = (f32[2,32,128]{2,1,0:T(8,128)S(1)}, f32[2,32,128]{2,1,0:T(8,128)S(1)}, u32[]{:S(2)}, u32[]{:S(2)}) collective-permute-start(f32[2,32,128]{2,1,0:T(8,128)S(1)} %get-tuple-element.36), channel_id=1, source_target_pairs={{0,0},{8,256},{16,512},{24,768},{256,8},{264,264},{272,520},{280,7... | collective-permute-start | bytes 98312 | tf_op jit(solution)/shard_map/ppermute | solution.py:251
  159.3 8.8 %collective-permute-start.1 = (f32[64,128]{1,0:T(8,128)S(1)}, f32[64,128]{1,0:T(8,128)S(1)}, u32[]{:S(2)}, u32[]{:S(2)}) collective-permute-start(f32[64,128]{1,0:T(8,128)S(1)} %shard_map.122), channel_id=1, source_target_pairs={{0,0},{8,256},{16,512},{24,768},{256,8},{264,264},{272,520},{280,7... | collective-permute-start | bytes 98312 | tf_op jit(solution)/shard_map/ppermute | solution.py:251

commit v5 on v3

--- a/solution.py
+++ b/solution.py
@@ -36,9 +36,11 @@
     )
 
 
-def halves(values):
-    high = values.astype(BF16)
-    return high, (values - high.astype(F32)).astype(BF16)
+def thirds(values):
+    high = values.astype(BF16).astype(F32)
+    rest = values - high
+    middle = rest.astype(BF16).astype(F32)
+    return high, middle, rest - middle
 
 
 def split_pair(rows):
@@ -111,9 +113,9 @@
 
 
 def gas_kernel(stride, per_pencil, source_ref, gas_ref, pick_ref, place_ref, gas_out, send_ref=None):
-    high, low = halves(source_ref[...])
     place = place_ref[...]
-    deposit = dot(place, high) + dot(place, low)
+    high, middle, low = (dot(place, part.astype(BF16)) for part in thirds(source_ref[...]))
+    deposit = high + (middle + low)
     rows = place.shape[0]
     gas = gas_ref[:rows]
     block = iota(gas.shape, 0) // stride % per_pencil
@@ -201,19 +203,18 @@
         if which < state_out.shape[0]:
             state_out[which] = new_drop
         source = mass * drop - new_mass * new_drop - latent * (mass - new_mass)
-        high = source.astype(BF16).astype(F32)
-        part_ref[quantity] = high
-        part_ref[2 + quantity] = source - high
-
-    total = jnp.zeros((2 * slots, 4 * HALF), F32)
+        for i, part in enumerate(thirds(source)):
+            part_ref[2 * i + quantity] = part
+
+    total = jnp.zeros((2 * slots, 6 * HALF), F32)
     for start in range(0, lines, chunk):
         hot, here = masks(start)
         parts = [
             jnp.where(here, packed(part_ref.at[i], start), zero).reshape(HALF, width)
-            for i in range(4)
+            for i in range(6)
         ]
         total += dot(hot, jnp.concatenate(parts, axis=0), 1, 1)
-    total = total[:, :LANES] + total[:, LANES:]
+    total = total[:, :LANES] + (total[:, LANES : 2 * LANES] + total[:, 2 * LANES :])
     lower, upper = total[:slots], total[slots:]
     left = iota(lower.shape, 1) < HALF
     first_rows = jnp.where(left, lower, pltpu.roll(upper, HALF, 1))
@@ -314,7 +315,7 @@
             recv,
             pack,
             *state,
-            scratch=[pltpu.VMEM((2, lines, LANES), F32), pltpu.VMEM((4, lines, LANES), F32)],
+            scratch=[pltpu.VMEM((2, lines, LANES), F32), pltpu.VMEM((6, lines, LANES), F32)],
         )
         source = exchange(source, peers)
         update = functools.partial(gas_kernel, pencils, per_pencil)

time: 158 us -> 160 us (1.013)
  the two profiles are of different devices: /device:TPU:22 before, /device:TPU:18 now
where the time goes in v5:
time: 160 us; the launch traced here: 159 us
  blocking collectives  115 us (72%)
  starting transfers between devices  25.1 us (16%)
  Pallas kernels  9.64 us (6%)
  waiting for transfers between devices  5.53 us (3%)
  local copies, waits for them, and re-layouts  2.03 us (1%)
    all_to_all x8, blocking collectives, exchange(): lax.all_to_all(rows.reshape(shape), GROUP, 0, 0, tiled=True)  109 us
    ppermute x4, starting transfers between devices, swap(): return lax.ppermute(values, ('sec', 'far'), pairs)  20.6 us
    pallas_call x11, Pallas kernels, call(): pl.pallas_call(body, out_shape=out_shape, in_specs=[smem] * scalars + [vm...  9.64 us
    all_gather x1, blocking collectives, shards(): lax.all_gather(jnp.concatenate([own_gas, own_drop], axis=0), 'sec', axis=...  5.74 us
    all_to_all x1, starting transfers between devices, exchange(): lax.all_to_all(rows.reshape(shape), GROUP, 0, 0, tiled=True)  4.52 us
    all_to_all x1, waiting for transfers between devices, exchange(): lax.all_to_all(rows.reshape(shape), GROUP, 0, 0, tiled=True)  3.29 us
  transfers between devices with their start and end apart: 5, of which 2 were waited for; matrix products, arithmetic and copies ran while one was open for 1% of the time, Pallas kernels for 0%

profile of v5, /device:TPU:18, one launch (start us, length us, event | category | flops | bytes accessed | tf_op | source)
XLA Modules:
  0.0 159.5 jit_solution(15352032392990571431)
XLA Ops:
  0.6 0.8 copy.12
  1.4 7.0 %collective-permute-start = (s32[1,32,4]{2,1,0:T(8,128)S(1)}, s32[1,32,4]{2,1,0:T(8,128)S(1)}, u32[]{:S(2)}, u32[]{:S(2)}) collective-permute-start(s32[1,32,4]{2,1,0:T(8,128)S(1)} %copy.12), channel_id=1, source_target_pairs={{0,0},{8,256},{16,512},{24,768},{256,8},{264,264},{272,520},{280,7... | collective-permute-start | bytes 1544 | tf_op jit(solution)/shard_map/ppermute | solution.py:246
  8.5 0.8 pad_maximum_fusion
  9.3 0.0 copy-start.4
  9.3 0.0 copy-start.5
  9.3 5.7 %all_gather.3.temp_ref = f32[384,128]{1,0:T(8,128)S(1)} all-gather(f32[96,128]{1,0:T(8,128)S(1)} %pad_maximum_fusion), channel_id=1, replica_groups=mesh['sec'=4,'row'=8,'far'=4,'near'=8] {'sec'}, dimensions={0}, use_global_device_ids=true | all-gather | bytes 245760 | tf_op jit(solution)/shard_map/all_gather | solution.py:275
  15.8 1.9 %collective-permute-start.1 = (f32[352,128]{1,0:T(8,128)S(1)}, f32[352,128]{1,0:T(8,128)S(1)}, u32[]{:S(2)}, u32[]{:S(2)}) collective-permute-start(f32[352,128]{1,0:T(8,128)S(1)} %shard_map.113), channel_id=1, source_target_pairs={{0,0},{8,256},{16,512},{24,768},{256,8},{264,264},{272,520},{280,7... | collective-permute-start | bytes 540680 | tf_op jit(solution)/shard_map/ppermute | solution.py:246
  17.7 0.3 shard_map.112
  18.0 25.9 %all_to_all.45 = bf16[32,8,128]{2,1,0:T(8,128)(2,1)S(1)} all-to-all(bf16[32,8,128]{2,1,0:T(8,128)(2,1)S(1)} %bitcast.41), channel_id=1, replica_groups=mesh['sec'=4,'row'=8,'far'=4,'near'=8] {'sec','near'}, dimensions={0} | all-to-all | bytes 131072 | tf_op jit(solution)/shard_map/all_to_all | solution.py:240
  43.8 0.2 shard_map.114
  44.0 11.5 %all_to_all.46 = bf16[32,8,128]{2,1,0:T(8,128)(2,1)S(1)} all-to-all(bf16[32,8,128]{2,1,0:T(8,128)(2,1)S(1)} %bitcast.52), channel_id=1, replica_groups=mesh['sec'=4,'row'=8,'far'=4,'near'=8] {'sec','near'}, dimensions={0} | all-to-all | bytes 131072 | tf_op jit(solution)/shard_map/all_to_all | solution.py:240
  55.5 1.8 %shard_map.115 = (f32[3,32,128]{2,1,0:T(8,128)S(1)}, f32[256,128]{1,0:T(8,128)S(1)}) custom-call(bf16[256,128]{1,0:T(8,128)(2,1)S(1)} %bitcast.46, f32[352,128]{1,0:T(8,128)S(1)} %collective-permute-done.1.pack_ref.gas_ref), custom_call_target="tpu_custom_call" | custom-call | tf_op jit(solution)/shard_map/pallas_call | solution.py:228
  57.3 12.5 %all_to_all.47 = f32[32,8,128]{2,1,0:T(8,128)S(1)} all-to-all(f32[32,8,128]{2,1,0:T(8,128)S(1)} %bitcast.51), channel_id=1, replica_groups=mesh['sec'=4,'row'=8,'far'=4,'near'=8] {'sec','near'}, dimensions={0} | all-to-all | bytes 262144 | tf_op jit(solution)/shard_map/all_to_all | solution.py:240
  69.9 0.4 shard_map.116
  70.3 11.4 %all_to_all.48 = bf16[32,8,128]{2,1,0:T(8,128)(2,1)S(1)} all-to-all(bf16[32,8,128]{2,1,0:T(8,128)(2,1)S(1)} %bitcast.55), channel_id=1, replica_groups=mesh['sec'=4,'row'=8,'far'=4,'near'=8] {'sec','near'}, dimensions={0} | all-to-all | bytes 131072 | tf_op jit(solution)/shard_map/all_to_all | solution.py:240
  81.6 1.8 %shard_map.117 = (f32[3,32,128]{2,1,0:T(8,128)S(1)}, f32[256,128]{1,0:T(8,128)S(1)}) custom-call(bf16[256,128]{1,0:T(8,128)(2,1)S(1)} %bitcast.44, f32[352,128]{1,0:T(8,128)S(1)} %collective-permute-done.1.pack_ref.gas_ref, f32[3,32,128]{2,1,0:T(8,128)S(1)} %get-tuple-element.29.refs_0_), custom_call_target="tpu_custom_call" | custom-call | tf_op jit(solution)/shard_map/pallas_call | solution.py:228
  83.5 12.5 %all_to_all.49 = f32[32,8,128]{2,1,0:T(8,128)S(1)} all-to-all(f32[32,8,128]{2,1,0:T(8,128)S(1)} %bitcast.49), channel_id=1, replica_groups=mesh['sec'=4,'row'=8,'far'=4,'near'=8] {'sec','near'}, dimensions={0} | all-to-all | bytes 262144 | tf_op jit(solution)/shard_map/all_to_all | solution.py:240
  96.0 0.4 shard_map.118
  96.4 11.4 %all_to_all.50 = bf16[32,8,128]{2,1,0:T(8,128)(2,1)S(1)} all-to-all(bf16[32,8,128]{2,1,0:T(8,128)(2,1)S(1)} %bitcast.53), channel_id=1, replica_groups=mesh['sec'=4,'row'=8,'far'=4,'near'=8] {'sec','near'}, dimensions={0} | all-to-all | bytes 131072 | tf_op jit(solution)/shard_map/all_to_all | solution.py:240
  107.8 1.8 %shard_map.119 = (f32[3,32,128]{2,1,0:T(8,128)S(1)}, f32[256,128]{1,0:T(8,128)S(1)}) custom-call(bf16[256,128]{1,0:T(8,128)(2,1)S(1)} %bitcast.45, f32[352,128]{1,0:T(8,128)S(1)} %collective-permute-done.1.pack_ref.gas_ref, f32[3,32,128]{2,1,0:T(8,128)S(1)} %get-tuple-element.33.refs_0_), custom_call_target="tpu_custom_call" | custom-call | tf_op jit(solution)/shard_map/pallas_call | solution.py:228
  109.6 12.5 %all_to_all.51 = f32[32,8,128]{2,1,0:T(8,128)S(1)} all-to-all(f32[32,8,128]{2,1,0:T(8,128)S(1)} %bitcast.50), channel_id=1, replica_groups=mesh['sec'=4,'row'=8,'far'=4,'near'=8] {'sec','near'}, dimensions={0} | all-to-all | bytes 262144 | tf_op jit(solution)/shard_map/all_to_all | solution.py:240
  122.1 0.4 shard_map.120
  122.5 11.4 %all_to_all.52 = bf16[32,8,128]{2,1,0:T(8,128)(2,1)S(1)} all-to-all(bf16[32,8,128]{2,1,0:T(8,128)(2,1)S(1)} %bitcast.54), channel_id=1, replica_groups=mesh['sec'=4,'row'=8,'far'=4,'near'=8] {'sec','near'}, dimensions={0} | all-to-all | bytes 131072 | tf_op jit(solution)/shard_map/all_to_all | solution.py:240
  133.9 2.4 %shard_map.121 = (f32[2,32,128]{2,1,0:T(8,128)S(1)}, f32[256,128]{1,0:T(8,128)}) custom-call(bf16[256,128]{1,0:T(8,128)(2,1)S(1)} %bitcast.43, f32[352,128]{1,0:T(8,128)S(1)} %collective-permute-done.1.pack_ref.gas_ref, f32[3,32,128]{2,1,0:T(8,128)S(1)} %get-tuple-element.37.refs_0_), custom_call_target="tpu_custom_call" | custom-call | tf_op jit(solution)/shard_map/pallas_call | solution.py:228
  136.3 4.5 %all-to-all-start.8 = ((f32[32,8,128]{2,1,0:T(8,128)}), f32[32,8,128]{2,1,0:T(8,128)S(1)}, u32[]{:S(2)}, u32[]{:S(2)}) async-start(f32[32,8,128]{2,1,0:T(8,128)} %bitcast.27), calls=%async_computation.8 | async-start | bytes 262144 | tf_op jit(solution)/shard_map/all_to_all | solution.py:240
  140.9 5.6 %collective-permute-start.3 = (f32[2,32,128]{2,1,0:T(8,128)S(1)}, f32[2,32,128]{2,1,0:T(8,128)S(1)}, u32[]{:S(2)}, u32[]{:S(2)}) collective-permute-start(f32[2,32,128]{2,1,0:T(8,128)S(1)} %get-tuple-element.40), channel_id=1, source_target_pairs={{0,0},{8,256},{16,512},{24,768},{256,8},{264,264},{272,520},{280,7... | collective-permute-start | bytes 98312 | tf_op jit(solution)/shard_map/ppermute | solution.py:246
  146.5 3.3 %all-to-all-done.8 = f32[32,8,128]{2,1,0:T(8,128)S(1)} async-done(((f32[32,8,128]{2,1,0:T(8,128)}), f32[32,8,128]{2,1,0:T(8,128)S(1)}, u32[]{:S(2)}, u32[]{:S(2)}) %all-to-all-start.8) | async-done | bytes 131104 | tf_op jit(solution)/shard_map/all_to_all | solution.py:240
  149.7 0.2 shard_map.122
  149.9 6.1 %collective-permute-start.2 = (f32[64,128]{1,0:T(8,128)S(1)}, f32[64,128]{1,0:T(8,128)S(1)}, u32[]{:S(2)}, u32[]{:S(2)}) collective-permute-start(f32[64,128]{1,0:T(8,128)S(1)} %shard_map.122), channel_id=1, source_target_pairs={{0,0},{8,256},{16,512},{24,768},{256,8},{264,264},{272,520},{280,7... | collective-permute-start | bytes 98312 | tf_op jit(solution)/shard_map/ppermute | solution.py:246
  156.0 0.6 slice_bitcast_fusion
  156.6 2.2 %collective-permute-done.2 = f32[64,128]{1,0:T(8,128)S(1)} collective-permute-done((f32[64,128]{1,0:T(8,128)S(1)}, f32[64,128]{1,0:T(8,128)S(1)}, u32[]{:S(2)}, u32[]{:S(2)}) %collective-permute-start.2) | collective-permute-done | bytes 32800 | tf_op jit(solution)/shard_map/ppermute | solution.py:246
  158.9 0.6 copy.17
  (16 shorter events, 0.1 us)
Async XLA Ops:
  0.6 7.8 %copy-start.1 = (f32[1,4096]{1,0:T(1,128)S(1)}, f32[1,4096]{1,0:T(1,128)}, u32[]{:S(2)}) copy-start(f32[1,4096]{1,0:T(1,128)} %param.10) | copy-start | bytes 49156
  1.4 14.3 %collective-permute-start = (s32[1,32,4]{2,1,0:T(8,128)S(1)}, s32[1,32,4]{2,1,0:T(8,128)S(1)}, u32[]{:S(2)}, u32[]{:S(2)}) collective-permute-start(s32[1,32,4]{2,1,0:T(8,128)S(1)} %copy.12), channel_id=1, source_target_pairs={{0,0},{8,256},{16,512},{24,768},{256,8},{264,264},{272,520},{280,7... | collective-permute-start | bytes 1544 | tf_op jit(solution)/shard_map/ppermute | solution.py:246
  9.2 6.5 %copy-start = (f32[1,4,2,1024]{3,2,1,0:T(2,128)S(1)}, f32[1,4,2,1024]{3,2,1,0:T(2,128)}, u32[]{:S(2)}) copy-start(f32[1,4,2,1024]{3,2,1,0:T(2,128)} %param.9) | copy-start | bytes 98308
  9.2 6.5 %copy-start.2 = (f32[4096]{0:T(1024)S(1)}, f32[4096]{0:T(1024)}, u32[]{:S(2)}) copy-start(f32[4096]{0:T(1024)} %param.11) | copy-start | bytes 49156
  9.2 6.5 %copy-start.3 = (f32[4096]{0:T(1024)S(1)}, f32[4096]{0:T(1024)}, u32[]{:S(2)}) copy-start(f32[4096]{0:T(1024)} %param.12) | copy-start | bytes 49156
  9.3 6.5 %copy-start.4 = (f32[4096]{0:T(1024)S(1)}, f32[4096]{0:T(1024)}, u32[]{:S(2)}) copy-start(f32[4096]{0:T(1024)} %param.13) | copy-start | bytes 49156
  9.3 6.5 %copy-start.5 = (s32[4096]{0:T(1024)S(1)}, s32[4096]{0:T(1024)}, u32[]{:S(2)}) copy-start(s32[4096]{0:T(1024)} %param.15) | copy-start | bytes 49156
  9.3 6.5 %copy-start.6 = (s32[4096]{0:T(1024)S(1)}, s32[4096]{0:T(1024)}, u32[]{:S(2)}) copy-start(s32[4096]{0:T(1024)} %param.16) | copy-start | bytes 49156
  15.8 28.1 %collective-permute-start.1 = (f32[352,128]{1,0:T(8,128)S(1)}, f32[352,128]{1,0:T(8,128)S(1)}, u32[]{:S(2)}, u32[]{:S(2)}) collective-permute-start(f32[352,128]{1,0:T(8,128)S(1)} %shard_map.113), channel_id=1, source_target_pairs={{0,0},{8,256},{16,512},{24,768},{256,8},{264,264},{272,520},{280,7... | collective-permute-start | bytes 540680 | tf_op jit(solution)/shard_map/ppermute | solution.py:246
  136.3 13.4 %all-to-all-start.8 = ((f32[32,8,128]{2,1,0:T(8,128)}), f32[32,8,128]{2,1,0:T(8,128)S(1)}, u32[]{:S(2)}, u32[]{:S(2)}) async-start(f32[32,8,128]{2,1,0:T(8,128)} %bitcast.27), calls=%async_computation.8 | async-start | bytes 262144 | tf_op jit(solution)/shard_map/all_to_all | solution.py:240
  140.9 15.2 %collective-permute-start.3 = (f32[2,32,128]{2,1,0:T(8,128)S(1)}, f32[2,32,128]{2,1,0:T(8,128)S(1)}, u32[]{:S(2)}, u32[]{:S(2)}) collective-permute-start(f32[2,32,128]{2,1,0:T(8,128)S(1)} %get-tuple-element.40), channel_id=1, source_target_pairs={{0,0},{8,256},{16,512},{24,768},{256,8},{264,264},{272,520},{280,7... | collective-permute-start | bytes 98312 | tf_op jit(solution)/shard_map/ppermute | solution.py:246
  149.9 8.9 %collective-permute-start.2 = (f32[64,128]{1,0:T(8,128)S(1)}, f32[64,128]{1,0:T(8,128)S(1)}, u32[]{:S(2)}, u32[]{:S(2)}) collective-permute-start(f32[64,128]{1,0:T(8,128)S(1)} %shard_map.122), channel_id=1, source_target_pairs={{0,0},{8,256},{16,512},{24,768},{256,8},{264,264},{272,520},{280,7... | collective-permute-start | bytes 98312 | tf_op jit(solution)/shard_map/ppermute | solution.py:246

commit v6 on v5

--- a/solution.py
+++ b/solution.py
@@ -103,8 +103,12 @@
     store(CELL, jnp.where(active, cell_ref[...] - HALF * upper, -1).astype(F32))
 
 
-def pick_kernel(wanted_ref, pack_ref, pick_ref, place_ref, send_ref):
-    wanted = wanted_ref[...].astype(F32).astype(jnp.int32)
+def pick_kernel(wanted_ref, pack_ref, pick_ref, place_ref, own_place_ref, send_ref):
+    wanted = wanted_ref[...].astype(F32)
+    own = split_pair(wanted)[0]
+    own = (own == iota(own.shape, 1).astype(F32)).astype(F32)
+    own_place_ref[...] = own.T[: own_place_ref.shape[0]].astype(BF16)
+    wanted = wanted.astype(jnp.int32)
     pick = (wanted == iota(wanted.shape, 1)).astype(F32)
     pick_ref[...] = pick.astype(BF16)
     place_ref[...] = pick.T.astype(BF16)
@@ -206,20 +210,24 @@
         for i, part in enumerate(thirds(source)):
             part_ref[2 * i + quantity] = part
 
-    total = jnp.zeros((2 * slots, 6 * HALF), F32)
+    sent = 2 if state_out.shape[0] > TEMP else 1
+    total = jnp.zeros((3 * sent * HALF, 2 * slots), F32)
     for start in range(0, lines, chunk):
         hot, here = masks(start)
         parts = [
-            jnp.where(here, packed(part_ref.at[i], start), zero).reshape(HALF, width)
-            for i in range(6)
+            jnp.where(here, packed(part_ref.at[2 * i + quantity], start), zero).reshape(HALF, width)
+            for i in range(3)
+            for quantity in range(sent)
         ]
-        total += dot(hot, jnp.concatenate(parts, axis=0), 1, 1)
-    total = total[:, :LANES] + (total[:, LANES : 2 * LANES] + total[:, 2 * LANES :])
-    lower, upper = total[:slots], total[slots:]
-    left = iota(lower.shape, 1) < HALF
-    first_rows = jnp.where(left, lower, pltpu.roll(upper, HALF, 1))
-    second_rows = jnp.where(left, pltpu.roll(lower, HALF, 1), upper)
-    send_ref[...] = merge_pair(first_rows, second_rows)
+        total += dot(jnp.concatenate(parts, axis=0), hot, 1, 1)
+    high, middle, low = (total[i * sent * HALF : (i + 1) * sent * HALF] for i in range(3))
+    total = high + (middle + low)
+
+    def unfold(values):
+        return jnp.concatenate([values[:, :slots], values[:, slots:]], axis=0).T
+
+    own = unfold(total[:HALF])
+    send_ref[...] = own if sent == 1 else merge_pair(own, unfold(total[HALF:]))
 
 
 def call(body, out_shape, *operands, scalars=0, scratch=()):
@@ -299,9 +307,14 @@
 
     gas_shape = shape((2 * blocks, LANES))
     send_shape = shape((rows, LANES), BF16)
-    pick, place, send = call(
+    pick, place, own_place, send = call(
         pick_kernel,
-        (shape((rows, 2 * blocks), BF16), shape((2 * blocks, rows), BF16), send_shape),
+        (
+            shape((rows, 2 * blocks), BF16),
+            shape((2 * blocks, rows), BF16),
+            shape((blocks, slots), BF16),
+            send_shape,
+        ),
         wanted,
         pack,
     )
@@ -311,7 +324,10 @@
         recv = exchange(send, peers)
         state, source = call(
             functools.partial(parcel_kernel, 4, substep == 0),
-            (shape((2 if last else 3, lines, LANES)), shape((rows, LANES))),
+            (
+                shape((2 if last else 3, lines, LANES)),
+                shape((slots if last else rows, LANES)),
+            ),
             recv,
             pack,
             *state,
@@ -320,7 +336,7 @@
         source = exchange(source, peers)
         update = functools.partial(gas_kernel, pencils, per_pencil)
         if last:
-            gas = call(update, shape((blocks, LANES)), source, gas, pick, place)
+            gas = call(update, shape((blocks, LANES)), source, gas, pick, own_place)
         else:
             gas, send = call(update, (gas_shape, send_shape), source, gas, pick, place)
             state = (state,)

time: 160 us -> 158 us (0.988)
  the two profiles are of different devices: /device:TPU:18 before, /device:TPU:16 now
where the time goes in v6:
time: 158 us; the launch traced here: 157 us
  blocking collectives  115 us (73%)
  starting transfers between devices  25.3 us (16%)
  Pallas kernels  8.48 us (5%)
  waiting for transfers between devices  4.41 us (3%)
  local copies, waits for them, and re-layouts  2.03 us (1%)
    all_to_all x8, blocking collectives, exchange(): lax.all_to_all(rows.reshape(shape), GROUP, 0, 0, tiled=True)  104 us
    ppermute x4, starting transfers between devices, swap(): return lax.ppermute(values, ('sec', 'far'), pairs)  20.8 us
    all_gather x1, blocking collectives, shards(): lax.all_gather(jnp.concatenate([own_gas, own_drop], axis=0), 'sec', axis=...  10.6 us
    pallas_call x11, Pallas kernels, call(): pl.pallas_call(body, out_shape=out_shape, in_specs=[smem] * scalars + [vm...  8.48 us
    all_to_all x1, starting transfers between devices, exchange(): lax.all_to_all(rows.reshape(shape), GROUP, 0, 0, tiled=True)  4.5 us
  transfers between devices with their start and end apart: 5, of which 2 were waited for; matrix products, arithmetic and copies ran while one was open for 1% of the time, Pallas kernels for 0%

profile of v6, /device:TPU:16, one launch (start us, length us, event | category | flops | bytes accessed | tf_op | source)
XLA Modules:
  0.0 157.4 jit_solution(13974713542425709260)
XLA Ops:
  0.6 0.8 copy.12
  1.4 7.0 %collective-permute-start = (s32[1,32,4]{2,1,0:T(8,128)S(1)}, s32[1,32,4]{2,1,0:T(8,128)S(1)}, u32[]{:S(2)}, u32[]{:S(2)}) collective-permute-start(s32[1,32,4]{2,1,0:T(8,128)S(1)} %copy.12), channel_id=1, source_target_pairs={{0,0},{8,256},{16,512},{24,768},{256,8},{264,264},{272,520},{280,7... | collective-permute-start | bytes 1544 | tf_op jit(solution)/shard_map/ppermute | solution.py:254
  8.5 0.8 pad_maximum_fusion
  9.3 0.0 copy-start.4
  9.3 0.0 copy-start.5
  9.3 10.6 %all_gather.3.temp_ref = f32[384,128]{1,0:T(8,128)S(1)} all-gather(f32[96,128]{1,0:T(8,128)S(1)} %pad_maximum_fusion), channel_id=1, replica_groups=mesh['sec'=4,'row'=8,'far'=4,'near'=8] {'sec'}, dimensions={0}, use_global_device_ids=true | all-gather | bytes 245760 | tf_op jit(solution)/shard_map/all_gather | solution.py:283
  20.7 1.9 %collective-permute-start.1 = (f32[352,128]{1,0:T(8,128)S(1)}, f32[352,128]{1,0:T(8,128)S(1)}, u32[]{:S(2)}, u32[]{:S(2)}) collective-permute-start(f32[352,128]{1,0:T(8,128)S(1)} %shard_map.113), channel_id=1, source_target_pairs={{0,0},{8,256},{16,512},{24,768},{256,8},{264,264},{272,520},{280,7... | collective-permute-start | bytes 540680 | tf_op jit(solution)/shard_map/ppermute | solution.py:254
  22.6 0.3 shard_map.112
  22.9 21.0 %all_to_all.45 = bf16[32,8,128]{2,1,0:T(8,128)(2,1)S(1)} all-to-all(bf16[32,8,128]{2,1,0:T(8,128)(2,1)S(1)} %bitcast.40), channel_id=1, replica_groups=mesh['sec'=4,'row'=8,'far'=4,'near'=8] {'sec','near'}, dimensions={0} | all-to-all | bytes 131072 | tf_op jit(solution)/shard_map/all_to_all | solution.py:248
  43.8 0.2 shard_map.114
  44.0 11.5 %all_to_all.46 = bf16[32,8,128]{2,1,0:T(8,128)(2,1)S(1)} all-to-all(bf16[32,8,128]{2,1,0:T(8,128)(2,1)S(1)} %bitcast.52), channel_id=1, replica_groups=mesh['sec'=4,'row'=8,'far'=4,'near'=8] {'sec','near'}, dimensions={0} | all-to-all | bytes 131072 | tf_op jit(solution)/shard_map/all_to_all | solution.py:248
  55.5 1.6 %shard_map.115 = (f32[3,32,128]{2,1,0:T(8,128)S(1)}, f32[256,128]{1,0:T(8,128)S(1)}) custom-call(bf16[256,128]{1,0:T(8,128)(2,1)S(1)} %bitcast.46, f32[352,128]{1,0:T(8,128)S(1)} %collective-permute-done.1.pack_ref.gas_ref), custom_call_target="tpu_custom_call" | custom-call | tf_op jit(solution)/shard_map/pallas_call | solution.py:236
  57.1 12.5 %all_to_all.47 = f32[32,8,128]{2,1,0:T(8,128)S(1)} all-to-all(f32[32,8,128]{2,1,0:T(8,128)S(1)} %bitcast.51), channel_id=1, replica_groups=mesh['sec'=4,'row'=8,'far'=4,'near'=8] {'sec','near'}, dimensions={0} | all-to-all | bytes 262144 | tf_op jit(solution)/shard_map/all_to_all | solution.py:248
  69.7 0.4 shard_map.116
  70.1 11.4 %all_to_all.48 = bf16[32,8,128]{2,1,0:T(8,128)(2,1)S(1)} all-to-all(bf16[32,8,128]{2,1,0:T(8,128)(2,1)S(1)} %bitcast.55), channel_id=1, replica_groups=mesh['sec'=4,'row'=8,'far'=4,'near'=8] {'sec','near'}, dimensions={0} | all-to-all | bytes 131072 | tf_op jit(solution)/shard_map/all_to_all | solution.py:248
  81.4 1.6 %shard_map.117 = (f32[3,32,128]{2,1,0:T(8,128)S(1)}, f32[256,128]{1,0:T(8,128)S(1)}) custom-call(bf16[256,128]{1,0:T(8,128)(2,1)S(1)} %bitcast.44, f32[352,128]{1,0:T(8,128)S(1)} %collective-permute-done.1.pack_ref.gas_ref, f32[3,32,128]{2,1,0:T(8,128)S(1)} %get-tuple-element.30.refs_0_), custom_call_target="tpu_custom_call" | custom-call | tf_op jit(solution)/shard_map/pallas_call | solution.py:236
  83.0 12.5 %all_to_all.49 = f32[32,8,128]{2,1,0:T(8,128)S(1)} all-to-all(f32[32,8,128]{2,1,0:T(8,128)S(1)} %bitcast.49), channel_id=1, replica_groups=mesh['sec'=4,'row'=8,'far'=4,'near'=8] {'sec','near'}, dimensions={0} | all-to-all | bytes 262144 | tf_op jit(solution)/shard_map/all_to_all | solution.py:248
  95.6 0.4 shard_map.118
  96.0 11.4 %all_to_all.50 = bf16[32,8,128]{2,1,0:T(8,128)(2,1)S(1)} all-to-all(bf16[32,8,128]{2,1,0:T(8,128)(2,1)S(1)} %bitcast.54), channel_id=1, replica_groups=mesh['sec'=4,'row'=8,'far'=4,'near'=8] {'sec','near'}, dimensions={0} | all-to-all | bytes 131072 | tf_op jit(solution)/shard_map/all_to_all | solution.py:248
  107.3 1.6 %shard_map.119 = (f32[3,32,128]{2,1,0:T(8,128)S(1)}, f32[256,128]{1,0:T(8,128)S(1)}) custom-call(bf16[256,128]{1,0:T(8,128)(2,1)S(1)} %bitcast.45, f32[352,128]{1,0:T(8,128)S(1)} %collective-permute-done.1.pack_ref.gas_ref, f32[3,32,128]{2,1,0:T(8,128)S(1)} %get-tuple-element.34.refs_0_), custom_call_target="tpu_custom_call" | custom-call | tf_op jit(solution)/shard_map/pallas_call | solution.py:236
  108.9 12.5 %all_to_all.51 = f32[32,8,128]{2,1,0:T(8,128)S(1)} all-to-all(f32[32,8,128]{2,1,0:T(8,128)S(1)} %bitcast.50), channel_id=1, replica_groups=mesh['sec'=4,'row'=8,'far'=4,'near'=8] {'sec','near'}, dimensions={0} | all-to-all | bytes 262144 | tf_op jit(solution)/shard_map/all_to_all | solution.py:248
  121.5 0.4 shard_map.120
  121.9 11.4 %all_to_all.52 = bf16[32,8,128]{2,1,0:T(8,128)(2,1)S(1)} all-to-all(bf16[32,8,128]{2,1,0:T(8,128)(2,1)S(1)} %bitcast.53), channel_id=1, replica_groups=mesh['sec'=4,'row'=8,'far'=4,'near'=8] {'sec','near'}, dimensions={0} | all-to-all | bytes 131072 | tf_op jit(solution)/shard_map/all_to_all | solution.py:248
  133.2 2.0 %shard_map.121 = (f32[2,32,128]{2,1,0:T(8,128)S(1)}, f32[128,128]{1,0:T(8,128)}) custom-call(bf16[256,128]{1,0:T(8,128)(2,1)S(1)} %bitcast.43, f32[352,128]{1,0:T(8,128)S(1)} %collective-permute-done.1.pack_ref.gas_ref, f32[3,32,128]{2,1,0:T(8,128)S(1)} %get-tuple-element.38.refs_0_), custom_call_target="tpu_custom_call" | custom-call | tf_op jit(solution)/shard_map/pallas_call | solution.py:236
  135.2 4.5 %all-to-all-start.8 = ((f32[32,4,128]{2,1,0:T(4,128)}), f32[32,4,128]{2,1,0:T(4,128)S(1)}, u32[]{:S(2)}, u32[]{:S(2)}) async-start(f32[32,4,128]{2,1,0:T(4,128)} %bitcast.27), calls=%async_computation.8 | async-start | bytes 131072 | tf_op jit(solution)/shard_map/all_to_all | solution.py:248
  139.7 5.6 %collective-permute-start.3 = (f32[2,32,128]{2,1,0:T(8,128)S(1)}, f32[2,32,128]{2,1,0:T(8,128)S(1)}, u32[]{:S(2)}, u32[]{:S(2)}) collective-permute-start(f32[2,32,128]{2,1,0:T(8,128)S(1)} %get-tuple-element.42), channel_id=1, source_target_pairs={{0,0},{8,256},{16,512},{24,768},{256,8},{264,264},{272,520},{280,7... | collective-permute-start | bytes 98312 | tf_op jit(solution)/shard_map/ppermute | solution.py:254
  145.3 2.1 %all-to-all-done.8 = f32[32,4,128]{2,1,0:T(4,128)S(1)} async-done(((f32[32,4,128]{2,1,0:T(4,128)}), f32[32,4,128]{2,1,0:T(4,128)S(1)}, u32[]{:S(2)}, u32[]{:S(2)}) %all-to-all-start.8) | async-done | bytes 65568 | tf_op jit(solution)/shard_map/all_to_all | solution.py:248
  147.5 0.2 shard_map.122
  147.6 6.3 %collective-permute-start.2 = (f32[64,128]{1,0:T(8,128)S(1)}, f32[64,128]{1,0:T(8,128)S(1)}, u32[]{:S(2)}, u32[]{:S(2)}) collective-permute-start(f32[64,128]{1,0:T(8,128)S(1)} %shard_map.122), channel_id=1, source_target_pairs={{0,0},{8,256},{16,512},{24,768},{256,8},{264,264},{272,520},{280,7... | collective-permute-start | bytes 98312 | tf_op jit(solution)/shard_map/ppermute | solution.py:254
  153.9 0.6 slice_bitcast_fusion
  154.5 2.3 %collective-permute-done.2 = f32[64,128]{1,0:T(8,128)S(1)} collective-permute-done((f32[64,128]{1,0:T(8,128)S(1)}, f32[64,128]{1,0:T(8,128)S(1)}, u32[]{:S(2)}, u32[]{:S(2)}) %collective-permute-start.2) | collective-permute-done | bytes 32800 | tf_op jit(solution)/shard_map/ppermute | solution.py:254
  156.8 0.6 copy.17
  (16 shorter events, 0.1 us)
Async XLA Ops:
  0.6 7.8 %copy-start.1 = (f32[1,4096]{1,0:T(1,128)S(1)}, f32[1,4096]{1,0:T(1,128)}, u32[]{:S(2)}) copy-start(f32[1,4096]{1,0:T(1,128)} %param.10) | copy-start | bytes 49156
  1.4 19.2 %collective-permute-start = (s32[1,32,4]{2,1,0:T(8,128)S(1)}, s32[1,32,4]{2,1,0:T(8,128)S(1)}, u32[]{:S(2)}, u32[]{:S(2)}) collective-permute-start(s32[1,32,4]{2,1,0:T(8,128)S(1)} %copy.12), channel_id=1, source_target_pairs={{0,0},{8,256},{16,512},{24,768},{256,8},{264,264},{272,520},{280,7... | collective-permute-start | bytes 1544 | tf_op jit(solution)/shard_map/ppermute | solution.py:254
  9.2 11.3 %copy-start = (f32[1,4,2,1024]{3,2,1,0:T(2,128)S(1)}, f32[1,4,2,1024]{3,2,1,0:T(2,128)}, u32[]{:S(2)}) copy-start(f32[1,4,2,1024]{3,2,1,0:T(2,128)} %param.9) | copy-start | bytes 98308
  9.2 11.3 %copy-start.2 = (f32[4096]{0:T(1024)S(1)}, f32[4096]{0:T(1024)}, u32[]{:S(2)}) copy-start(f32[4096]{0:T(1024)} %param.11) | copy-start | bytes 49156
  9.2 11.3 %copy-start.3 = (f32[4096]{0:T(1024)S(1)}, f32[4096]{0:T(1024)}, u32[]{:S(2)}) copy-start(f32[4096]{0:T(1024)} %param.12) | copy-start | bytes 49156
  9.3 11.3 %copy-start.4 = (f32[4096]{0:T(1024)S(1)}, f32[4096]{0:T(1024)}, u32[]{:S(2)}) copy-start(f32[4096]{0:T(1024)} %param.13) | copy-start | bytes 49156
  9.3 11.3 %copy-start.5 = (s32[4096]{0:T(1024)S(1)}, s32[4096]{0:T(1024)}, u32[]{:S(2)}) copy-start(s32[4096]{0:T(1024)} %param.15) | copy-start | bytes 49156
  9.3 11.3 %copy-start.6 = (s32[4096]{0:T(1024)S(1)}, s32[4096]{0:T(1024)}, u32[]{:S(2)}) copy-start(s32[4096]{0:T(1024)} %param.16) | copy-start | bytes 49156
  20.7 23.2 %collective-permute-start.1 = (f32[352,128]{1,0:T(8,128)S(1)}, f32[352,128]{1,0:T(8,128)S(1)}, u32[]{:S(2)}, u32[]{:S(2)}) collective-permute-start(f32[352,128]{1,0:T(8,128)S(1)} %shard_map.113), channel_id=1, source_target_pairs={{0,0},{8,256},{16,512},{24,768},{256,8},{264,264},{272,520},{280,7... | collective-permute-start | bytes 540680 | tf_op jit(solution)/shard_map/ppermute | solution.py:254
  135.2 12.3 %all-to-all-start.8 = ((f32[32,4,128]{2,1,0:T(4,128)}), f32[32,4,128]{2,1,0:T(4,128)S(1)}, u32[]{:S(2)}, u32[]{:S(2)}) async-start(f32[32,4,128]{2,1,0:T(4,128)} %bitcast.27), calls=%async_computation.8 | async-start | bytes 131072 | tf_op jit(solution)/shard_map/all_to_all | solution.py:248
  139.7 14.2 %collective-permute-start.3 = (f32[2,32,128]{2,1,0:T(8,128)S(1)}, f32[2,32,128]{2,1,0:T(8,128)S(1)}, u32[]{:S(2)}, u32[]{:S(2)}) collective-permute-start(f32[2,32,128]{2,1,0:T(8,128)S(1)} %get-tuple-element.42), channel_id=1, source_target_pairs={{0,0},{8,256},{16,512},{24,768},{256,8},{264,264},{272,520},{280,7... | collective-permute-start | bytes 98312 | tf_op jit(solution)/shard_map/ppermute | solution.py:254
  147.6 9.2 %collective-permute-start.2 = (f32[64,128]{1,0:T(8,128)S(1)}, f32[64,128]{1,0:T(8,128)S(1)}, u32[]{:S(2)}, u32[]{:S(2)}) collective-permute-start(f32[64,128]{1,0:T(8,128)S(1)} %shard_map.122), channel_id=1, source_target_pairs={{0,0},{8,256},{16,512},{24,768},{256,8},{264,264},{272,520},{280,7... | collective-permute-start | bytes 98312 | tf_op jit(solution)/shard_map/ppermute | solution.py:254

commit v7 on v6

--- a/solution.py
+++ b/solution.py
@@ -62,20 +62,18 @@
     return jnp.stack([even, odd], axis=1).reshape(2 * shape[0] * 8, LANES)
 
 
-def order_kernel(per_peer, pencils, per_pencil, blocks, list_ref, rows_ref):
+def order_kernel(pencils, per_pencil, list_ref, rows_ref):
     block = list_ref[0]
+    peers, per_peer = block.shape
     first = block // (pencils * per_pencil)
     rest = block - first * (pencils * per_pencil)
     pencil = rest // per_pencil
-    place = first * (pencils * per_pencil) + (rest - pencil * per_pencil) * pencils + pencil
-    rows, peers = rows_ref.shape[0], block.shape[0]
-    each = rows // peers
-    owner = (iota((rows, peers), 0) // each == iota((rows, peers), 1)).astype(BF16)
-    spread = dot(owner, place.astype(F32).astype(BF16))
-    within = iota(spread.shape, 0) % each
-    kept = jnp.where(within % per_peer == iota(spread.shape, 1), spread, 0.0)
-    value = jnp.sum(kept, axis=1, keepdims=True)
-    value = value + (blocks * (within[:, :1] // per_peer)).astype(F32)
+    line = first * (pencils * per_pencil) + (rest - pencil * per_pencil) * pencils + pencil
+    slots = rows_ref.shape[0]
+    owner = (iota((slots, peers), 0) // per_peer == iota((slots, peers), 1)).astype(BF16)
+    spread = dot(owner, line.astype(F32).astype(BF16))
+    mine = iota(spread.shape, 0) % per_peer == iota(spread.shape, 1)
+    value = jnp.sum(jnp.where(mine, spread, 0.0), axis=1, keepdims=True)
     rows_ref[...] = jnp.broadcast_to(value, rows_ref.shape).astype(BF16)
 
 
@@ -104,15 +102,14 @@
 
 
 def pick_kernel(wanted_ref, pack_ref, pick_ref, place_ref, own_place_ref, send_ref):
-    wanted = wanted_ref[...].astype(F32)
-    own = split_pair(wanted)[0]
-    own = (own == iota(own.shape, 1).astype(F32)).astype(F32)
+    lines = wanted_ref[...].astype(F32)
+    own = (lines == iota(lines.shape, 1).astype(F32)).astype(F32)
     own_place_ref[...] = own.T[: own_place_ref.shape[0]].astype(BF16)
-    wanted = wanted.astype(jnp.int32)
-    pick = (wanted == iota(wanted.shape, 1)).astype(F32)
+    wanted = merge_pair(lines, lines + pick_ref.shape[1] / 2)
+    pick = (wanted == iota(pick_ref.shape, 1).astype(F32)).astype(F32)
     pick_ref[...] = pick.astype(BF16)
     place_ref[...] = pick.T.astype(BF16)
-    gas = pack_ref[: wanted.shape[1]]
+    gas = pack_ref[: pick_ref.shape[1]]
     send_ref[...] = dot(pick.astype(BF16), gas.astype(BF16)).astype(BF16)
 
 
@@ -285,8 +282,8 @@
     )
     lists, together = lax.optimization_barrier((lists, together))
     wanted = call(
-        functools.partial(order_kernel, per_peer, pencils, per_pencil, blocks),
-        shape((rows, LANES), BF16),
+        functools.partial(order_kernel, pencils, per_pencil),
+        shape((slots, LANES), BF16),
         lists,
     )
     wanted = exchange(wanted, peers)

time: 158 us -> 158 us (level)
  the two profiles are of different devices: /device:TPU:16 before, /device:TPU:30 now
where the time goes in v7:
time: 158 us; the launch traced here: 157 us
  blocking collectives  115 us (73%)
  starting transfers between devices  25.6 us (16%)
  Pallas kernels  8.44 us (5%)
  waiting for transfers between devices  4.09 us (3%)
  local copies, waits for them, and re-layouts  2.03 us (1%)
    all_to_all x8, blocking collectives, exchange(): lax.all_to_all(rows.reshape(shape), GROUP, 0, 0, tiled=True)  109 us
    ppermute x4, starting transfers between devices, swap(): return lax.ppermute(values, ('sec', 'far'), pairs)  21.1 us
    pallas_call x11, Pallas kernels, call(): pl.pallas_call(body, out_shape=out_shape, in_specs=[smem] * scalars + [vm...  8.44 us
    all_gather x1, blocking collectives, shards(): lax.all_gather(jnp.concatenate([own_gas, own_drop], axis=0), 'sec', axis=...  5.74 us
    all_to_all x1, starting transfers between devices, exchange(): lax.all_to_all(rows.reshape(shape), GROUP, 0, 0, tiled=True)  4.5 us
  transfers between devices with their start and end apart: 5, of which 2 were waited for; matrix products, arithmetic and copies ran while one was open for 1% of the time, Pallas kernels for 0%

profile of v7, /device:TPU:30, one launch (start us, length us, event | category | flops | bytes accessed | tf_op | source)
XLA Modules:
  0.0 157.1 jit_solution(9915583097986112004)
XLA Ops:
  0.6 0.8 copy.12
  1.4 7.0 %collective-permute-start = (s32[1,32,4]{2,1,0:T(8,128)S(1)}, s32[1,32,4]{2,1,0:T(8,128)S(1)}, u32[]{:S(2)}, u32[]{:S(2)}) collective-permute-start(s32[1,32,4]{2,1,0:T(8,128)S(1)} %copy.12), channel_id=1, source_target_pairs={{0,0},{8,256},{16,512},{24,768},{256,8},{264,264},{272,520},{280,7... | collective-permute-start | bytes 1544 | tf_op jit(solution)/shard_map/ppermute | solution.py:251
  8.5 0.8 pad_maximum_fusion
  9.3 0.0 copy-start.4
  9.3 0.0 copy-start.6
  9.3 5.7 %all_gather.3.temp_ref = f32[384,128]{1,0:T(8,128)S(1)} all-gather(f32[96,128]{1,0:T(8,128)S(1)} %pad_maximum_fusion), channel_id=1, replica_groups=mesh['sec'=4,'row'=8,'far'=4,'near'=8] {'sec'}, dimensions={0}, use_global_device_ids=true | all-gather | bytes 245760 | tf_op jit(solution)/shard_map/all_gather | solution.py:280
  15.8 1.9 %collective-permute-start.1 = (f32[352,128]{1,0:T(8,128)S(1)}, f32[352,128]{1,0:T(8,128)S(1)}, u32[]{:S(2)}, u32[]{:S(2)}) collective-permute-start(f32[352,128]{1,0:T(8,128)S(1)} %shard_map.113), channel_id=1, source_target_pairs={{0,0},{8,256},{16,512},{24,768},{256,8},{264,264},{272,520},{280,7... | collective-permute-start | bytes 540680 | tf_op jit(solution)/shard_map/ppermute | solution.py:251
  17.7 0.2 shard_map.112
  18.0 25.4 %all_to_all.45 = bf16[32,4,128]{2,1,0:T(4,128)(2,1)S(1)} all-to-all(bf16[32,4,128]{2,1,0:T(4,128)(2,1)S(1)} %bitcast.50), channel_id=1, replica_groups=mesh['sec'=4,'row'=8,'far'=4,'near'=8] {'sec','near'}, dimensions={0} | all-to-all | bytes 65536 | tf_op jit(solution)/shard_map/all_to_all | solution.py:245
  43.4 0.2 shard_map.114
  43.5 11.7 %all_to_all.46 = bf16[32,8,128]{2,1,0:T(8,128)(2,1)S(1)} all-to-all(bf16[32,8,128]{2,1,0:T(8,128)(2,1)S(1)} %bitcast.52), channel_id=1, replica_groups=mesh['sec'=4,'row'=8,'far'=4,'near'=8] {'sec','near'}, dimensions={0} | all-to-all | bytes 131072 | tf_op jit(solution)/shard_map/all_to_all | solution.py:245
  55.3 1.6 %shard_map.115 = (f32[3,32,128]{2,1,0:T(8,128)S(1)}, f32[256,128]{1,0:T(8,128)S(1)}) custom-call(bf16[256,128]{1,0:T(8,128)(2,1)S(1)} %bitcast.44, f32[352,128]{1,0:T(8,128)S(1)} %collective-permute-done.1.pack_ref.gas_ref), custom_call_target="tpu_custom_call" | custom-call | tf_op jit(solution)/shard_map/pallas_call | solution.py:233
  56.9 12.6 %all_to_all.47 = f32[32,8,128]{2,1,0:T(8,128)S(1)} all-to-all(f32[32,8,128]{2,1,0:T(8,128)S(1)} %bitcast.49), channel_id=1, replica_groups=mesh['sec'=4,'row'=8,'far'=4,'near'=8] {'sec','near'}, dimensions={0} | all-to-all | bytes 262144 | tf_op jit(solution)/shard_map/all_to_all | solution.py:245
  69.4 0.4 shard_map.116
  69.8 11.4 %all_to_all.48 = bf16[32,8,128]{2,1,0:T(8,128)(2,1)S(1)} all-to-all(bf16[32,8,128]{2,1,0:T(8,128)(2,1)S(1)} %bitcast.55), channel_id=1, replica_groups=mesh['sec'=4,'row'=8,'far'=4,'near'=8] {'sec','near'}, dimensions={0} | all-to-all | bytes 131072 | tf_op jit(solution)/shard_map/all_to_all | solution.py:245
  81.2 1.6 %shard_map.117 = (f32[3,32,128]{2,1,0:T(8,128)S(1)}, f32[256,128]{1,0:T(8,128)S(1)}) custom-call(bf16[256,128]{1,0:T(8,128)(2,1)S(1)} %bitcast.42, f32[352,128]{1,0:T(8,128)S(1)} %collective-permute-done.1.pack_ref.gas_ref, f32[3,32,128]{2,1,0:T(8,128)S(1)} %get-tuple-element.30.refs_0_), custom_call_target="tpu_custom_call" | custom-call | tf_op jit(solution)/shard_map/pallas_call | solution.py:233
  82.8 12.5 %all_to_all.49 = f32[32,8,128]{2,1,0:T(8,128)S(1)} all-to-all(f32[32,8,128]{2,1,0:T(8,128)S(1)} %bitcast.47), channel_id=1, replica_groups=mesh['sec'=4,'row'=8,'far'=4,'near'=8] {'sec','near'}, dimensions={0} | all-to-all | bytes 262144 | tf_op jit(solution)/shard_map/all_to_all | solution.py:245
  95.3 0.4 shard_map.118
  95.7 11.4 %all_to_all.50 = bf16[32,8,128]{2,1,0:T(8,128)(2,1)S(1)} all-to-all(bf16[32,8,128]{2,1,0:T(8,128)(2,1)S(1)} %bitcast.54), channel_id=1, replica_groups=mesh['sec'=4,'row'=8,'far'=4,'near'=8] {'sec','near'}, dimensions={0} | all-to-all | bytes 131072 | tf_op jit(solution)/shard_map/all_to_all | solution.py:245
  107.1 1.6 %shard_map.119 = (f32[3,32,128]{2,1,0:T(8,128)S(1)}, f32[256,128]{1,0:T(8,128)S(1)}) custom-call(bf16[256,128]{1,0:T(8,128)(2,1)S(1)} %bitcast.43, f32[352,128]{1,0:T(8,128)S(1)} %collective-permute-done.1.pack_ref.gas_ref, f32[3,32,128]{2,1,0:T(8,128)S(1)} %get-tuple-element.34.refs_0_), custom_call_target="tpu_custom_call" | custom-call | tf_op jit(solution)/shard_map/pallas_call | solution.py:233
  108.7 12.5 %all_to_all.51 = f32[32,8,128]{2,1,0:T(8,128)S(1)} all-to-all(f32[32,8,128]{2,1,0:T(8,128)S(1)} %bitcast.48), channel_id=1, replica_groups=mesh['sec'=4,'row'=8,'far'=4,'near'=8] {'sec','near'}, dimensions={0} | all-to-all | bytes 262144 | tf_op jit(solution)/shard_map/all_to_all | solution.py:245
  121.2 0.4 shard_map.120
  121.6 11.4 %all_to_all.52 = bf16[32,8,128]{2,1,0:T(8,128)(2,1)S(1)} all-to-all(bf16[32,8,128]{2,1,0:T(8,128)(2,1)S(1)} %bitcast.53), channel_id=1, replica_groups=mesh['sec'=4,'row'=8,'far'=4,'near'=8] {'sec','near'}, dimensions={0} | all-to-all | bytes 131072 | tf_op jit(solution)/shard_map/all_to_all | solution.py:245
  133.0 2.0 %shard_map.121 = (f32[2,32,128]{2,1,0:T(8,128)S(1)}, f32[128,128]{1,0:T(8,128)}) custom-call(bf16[256,128]{1,0:T(8,128)(2,1)S(1)} %bitcast.41, f32[352,128]{1,0:T(8,128)S(1)} %collective-permute-done.1.pack_ref.gas_ref, f32[3,32,128]{2,1,0:T(8,128)S(1)} %get-tuple-element.38.refs_0_), custom_call_target="tpu_custom_call" | custom-call | tf_op jit(solution)/shard_map/pallas_call | solution.py:233
  134.9 4.5 %all-to-all-start.8 = ((f32[32,4,128]{2,1,0:T(4,128)}), f32[32,4,128]{2,1,0:T(4,128)S(1)}, u32[]{:S(2)}, u32[]{:S(2)}) async-start(f32[32,4,128]{2,1,0:T(4,128)} %bitcast.27), calls=%async_computation.8 | async-start | bytes 131072 | tf_op jit(solution)/shard_map/all_to_all | solution.py:245
  139.4 5.7 %collective-permute-start.3 = (f32[2,32,128]{2,1,0:T(8,128)S(1)}, f32[2,32,128]{2,1,0:T(8,128)S(1)}, u32[]{:S(2)}, u32[]{:S(2)}) collective-permute-start(f32[2,32,128]{2,1,0:T(8,128)S(1)} %get-tuple-element.42), channel_id=1, source_target_pairs={{0,0},{8,256},{16,512},{24,768},{256,8},{264,264},{272,520},{280,7... | collective-permute-start | bytes 98312 | tf_op jit(solution)/shard_map/ppermute | solution.py:251
  145.2 2.0 %all-to-all-done.8 = f32[32,4,128]{2,1,0:T(4,128)S(1)} async-done(((f32[32,4,128]{2,1,0:T(4,128)}), f32[32,4,128]{2,1,0:T(4,128)S(1)}, u32[]{:S(2)}, u32[]{:S(2)}) %all-to-all-start.8) | async-done | bytes 65568 | tf_op jit(solution)/shard_map/all_to_all | solution.py:245
  147.2 0.2 shard_map.122
  147.4 6.4 %collective-permute-start.2 = (f32[64,128]{1,0:T(8,128)S(1)}, f32[64,128]{1,0:T(8,128)S(1)}, u32[]{:S(2)}, u32[]{:S(2)}) collective-permute-start(f32[64,128]{1,0:T(8,128)S(1)} %shard_map.122), channel_id=1, source_target_pairs={{0,0},{8,256},{16,512},{24,768},{256,8},{264,264},{272,520},{280,7... | collective-permute-start | bytes 98312 | tf_op jit(solution)/shard_map/ppermute | solution.py:251
  153.8 0.6 slice_bitcast_fusion
  154.4 2.1 %collective-permute-done.2 = f32[64,128]{1,0:T(8,128)S(1)} collective-permute-done((f32[64,128]{1,0:T(8,128)S(1)}, f32[64,128]{1,0:T(8,128)S(1)}, u32[]{:S(2)}, u32[]{:S(2)}) %collective-permute-start.2) | collective-permute-done | bytes 32800 | tf_op jit(solution)/shard_map/ppermute | solution.py:251
  156.5 0.6 copy.17
  (16 shorter events, 0.1 us)
Async XLA Ops:
  0.6 7.8 %copy-start.1 = (f32[1,4096]{1,0:T(1,128)S(1)}, f32[1,4096]{1,0:T(1,128)}, u32[]{:S(2)}) copy-start(f32[1,4096]{1,0:T(1,128)} %param.10) | copy-start | bytes 49156
  1.4 14.3 %collective-permute-start = (s32[1,32,4]{2,1,0:T(8,128)S(1)}, s32[1,32,4]{2,1,0:T(8,128)S(1)}, u32[]{:S(2)}, u32[]{:S(2)}) collective-permute-start(s32[1,32,4]{2,1,0:T(8,128)S(1)} %copy.12), channel_id=1, source_target_pairs={{0,0},{8,256},{16,512},{24,768},{256,8},{264,264},{272,520},{280,7... | collective-permute-start | bytes 1544 | tf_op jit(solution)/shard_map/ppermute | solution.py:251
  9.2 6.5 %copy-start = (f32[1,4,2,1024]{3,2,1,0:T(2,128)S(1)}, f32[1,4,2,1024]{3,2,1,0:T(2,128)}, u32[]{:S(2)}) copy-start(f32[1,4,2,1024]{3,2,1,0:T(2,128)} %param.9) | copy-start | bytes 98308
  9.2 6.5 %copy-start.2 = (f32[4096]{0:T(1024)S(1)}, f32[4096]{0:T(1024)}, u32[]{:S(2)}) copy-start(f32[4096]{0:T(1024)} %param.11) | copy-start | bytes 49156
  9.2 6.5 %copy-start.3 = (f32[4096]{0:T(1024)S(1)}, f32[4096]{0:T(1024)}, u32[]{:S(2)}) copy-start(f32[4096]{0:T(1024)} %param.12) | copy-start | bytes 49156
  9.3 6.5 %copy-start.4 = (f32[4096]{0:T(1024)S(1)}, f32[4096]{0:T(1024)}, u32[]{:S(2)}) copy-start(f32[4096]{0:T(1024)} %param.13) | copy-start | bytes 49156
  9.3 6.5 %copy-start.5 = (s32[4096]{0:T(1024)S(1)}, s32[4096]{0:T(1024)}, u32[]{:S(2)}) copy-start(s32[4096]{0:T(1024)} %param.15) | copy-start | bytes 49156
  9.3 6.5 %copy-start.6 = (s32[4096]{0:T(1024)S(1)}, s32[4096]{0:T(1024)}, u32[]{:S(2)}) copy-start(s32[4096]{0:T(1024)} %param.16) | copy-start | bytes 49156
  15.8 27.6 %collective-permute-start.1 = (f32[352,128]{1,0:T(8,128)S(1)}, f32[352,128]{1,0:T(8,128)S(1)}, u32[]{:S(2)}, u32[]{:S(2)}) collective-permute-start(f32[352,128]{1,0:T(8,128)S(1)} %shard_map.113), channel_id=1, source_target_pairs={{0,0},{8,256},{16,512},{24,768},{256,8},{264,264},{272,520},{280,7... | collective-permute-start | bytes 540680 | tf_op jit(solution)/shard_map/ppermute | solution.py:251
  134.9 12.3 %all-to-all-start.8 = ((f32[32,4,128]{2,1,0:T(4,128)}), f32[32,4,128]{2,1,0:T(4,128)S(1)}, u32[]{:S(2)}, u32[]{:S(2)}) async-start(f32[32,4,128]{2,1,0:T(4,128)} %bitcast.27), calls=%async_computation.8 | async-start | bytes 131072 | tf_op jit(solution)/shard_map/all_to_all | solution.py:245
  139.4 14.3 %collective-permute-start.3 = (f32[2,32,128]{2,1,0:T(8,128)S(1)}, f32[2,32,128]{2,1,0:T(8,128)S(1)}, u32[]{:S(2)}, u32[]{:S(2)}) collective-permute-start(f32[2,32,128]{2,1,0:T(8,128)S(1)} %get-tuple-element.42), channel_id=1, source_target_pairs={{0,0},{8,256},{16,512},{24,768},{256,8},{264,264},{272,520},{280,7... | collective-permute-start | bytes 98312 | tf_op jit(solution)/shard_map/ppermute | solution.py:251
  147.4 9.1 %collective-permute-start.2 = (f32[64,128]{1,0:T(8,128)S(1)}, f32[64,128]{1,0:T(8,128)S(1)}, u32[]{:S(2)}, u32[]{:S(2)}) collective-permute-start(f32[64,128]{1,0:T(8,128)S(1)} %shard_map.122), channel_id=1, source_target_pairs={{0,0},{8,256},{16,512},{24,768},{256,8},{264,264},{272,520},{280,7... | collective-permute-start | bytes 98312 | tf_op jit(solution)/shard_map/ppermute | solution.py:251

commit v8 on v7

--- a/solution.py
+++ b/solution.py
@@ -78,15 +78,16 @@
 
 
 def pack_kernel(
-    slots, count_ref, temp_ref, gas_ref, drop_ref, mass_ref, base_ref, evap_ref, slot_ref, cell_ref, out_ref
+    slots, count_ref, temp_ref, gas_ref, drop_ref, mass_ref, base_ref, evap_ref, slot_ref, cell_ref,
+    gas_out, out_ref,
 ):
     blocks, lines = gas_ref.shape[0], mass_ref.shape[0]
     start = temp_ref.shape[0] - blocks - lines
-    out_ref[:blocks] = gas_ref[...]
-    out_ref[blocks : 2 * blocks] = temp_ref[start : start + blocks]
+    gas_out[:blocks] = gas_ref[...]
+    gas_out[blocks:] = temp_ref[start : start + blocks]
 
     def store(which, values):
-        at = 2 * blocks + which * lines
+        at = which * lines
         out_ref[at : at + lines] = values
 
     store(OWN, drop_ref[...])
@@ -287,9 +288,9 @@
         lists,
     )
     wanted = exchange(wanted, peers)
-    pack = call(
+    gas, pack = call(
         functools.partial(pack_kernel, slots),
-        shape((2 * blocks + 7 * lines, LANES)),
+        (shape((2 * blocks, LANES)), shape((7 * lines, LANES))),
         parcel_count,
         together,
         own_gas,
@@ -300,7 +301,7 @@
         ),
         scalars=1,
     )
-    pack = swap(pack)
+    gas = swap(gas)
 
     gas_shape = shape((2 * blocks, LANES))
     send_shape = shape((rows, LANES), BF16)
@@ -313,9 +314,11 @@
             send_shape,
         ),
         wanted,
-        pack,
-    )
-    gas, state = pack, ()
+        gas,
+    )
+    pack, send = lax.optimization_barrier((pack, send))
+    pack = swap(pack)
+    state = ()
     for substep in range(ITERS):
         last = substep == ITERS - 1
         recv = exchange(send, peers)

time: 158 us -> 167 us (1.057)
  the two profiles are of different devices: /device:TPU:30 before, /device:TPU:16 now
where the time goes in v8:
time: 167 us; the launch traced here: 166 us
  blocking collectives  107 us (64%)
  starting transfers between devices  31.9 us (19%)
  waiting for transfers between devices  13.3 us (8%)
  Pallas kernels  9.06 us (5%)
  local copies, waits for them, and re-layouts  2.03 us (1%)
    all_to_all x7, blocking collectives, exchange(): lax.all_to_all(rows.reshape(shape), GROUP, 0, 0, tiled=True)  96.8 us
    ppermute x5, starting transfers between devices, swap(): return lax.ppermute(values, ('sec', 'far'), pairs)  22.5 us
    all_gather x1, blocking collectives, shards(): lax.all_gather(jnp.concatenate([own_gas, own_drop], axis=0), 'sec', axis=...  10.6 us
    all_to_all x2, starting transfers between devices, exchange(): lax.all_to_all(rows.reshape(shape), GROUP, 0, 0, tiled=True)  9.39 us
    ppermute x5, waiting for transfers between devices, swap(): return lax.ppermute(values, ('sec', 'far'), pairs)  9.15 us
    pallas_call x11, Pallas kernels, call(): pl.pallas_call(body, out_shape=out_shape, in_specs=[smem] * scalars + [vm...  9.06 us
    all_to_all x2, waiting for transfers between devices, exchange(): lax.all_to_all(rows.reshape(shape), GROUP, 0, 0, tiled=True)  4.18 us
  transfers between devices with their start and end apart: 7, of which 3 were waited for; matrix products, arithmetic and copies ran while one was open for 1% of the time, Pallas kernels for 0%

profile of v8, /device:TPU:16, one launch (start us, length us, event | category | flops | bytes accessed | tf_op | source)
XLA Modules:
  0.0 166.0 jit_solution(2462771333079168271)
XLA Ops:
  0.6 0.8 copy.12
  1.4 7.0 %collective-permute-start = (s32[1,32,4]{2,1,0:T(8,128)S(1)}, s32[1,32,4]{2,1,0:T(8,128)S(1)}, u32[]{:S(2)}, u32[]{:S(2)}) collective-permute-start(s32[1,32,4]{2,1,0:T(8,128)S(1)} %copy.12), channel_id=1, source_target_pairs={{0,0},{8,256},{16,512},{24,768},{256,8},{264,264},{272,520},{280,7... | collective-permute-start | bytes 1544 | tf_op jit(solution)/shard_map/ppermute | solution.py:252
  8.5 0.8 pad_maximum_fusion
  9.3 10.6 %all_gather.3.temp_ref = f32[384,128]{1,0:T(8,128)S(1)} all-gather(f32[96,128]{1,0:T(8,128)S(1)} %pad_maximum_fusion), channel_id=1, replica_groups=mesh['sec'=4,'row'=8,'far'=4,'near'=8] {'sec'}, dimensions={0}, use_global_device_ids=true | all-gather | bytes 245760 | tf_op jit(solution)/shard_map/all_gather | solution.py:281
  20.7 1.9 %collective-permute-start.1 = (f32[128,128]{1,0:T(8,128)S(1)}, f32[128,128]{1,0:T(8,128)S(1)}, u32[]{:S(2)}, u32[]{:S(2)}) collective-permute-start(f32[128,128]{1,0:T(8,128)S(1)} %get-tuple-element.30), channel_id=1, source_target_pairs={{0,0},{8,256},{16,512},{24,768},{256,8},{264,264},{272,520},{280,7... | collective-permute-start | bytes 196616 | tf_op jit(solution)/shard_map/ppermute | solution.py:252
  22.6 0.2 shard_map.113
  22.8 20.5 %all_to_all.45 = bf16[32,4,128]{2,1,0:T(4,128)(2,1)S(1)} all-to-all(bf16[32,4,128]{2,1,0:T(4,128)(2,1)S(1)} %bitcast.51), channel_id=1, replica_groups=mesh['sec'=4,'row'=8,'far'=4,'near'=8] {'sec','near'}, dimensions={0} | all-to-all | bytes 65536 | tf_op jit(solution)/shard_map/all_to_all | solution.py:246
  43.4 0.8 shard_map.114
  44.1 4.9 %all-to-all-start.1 = ((bf16[32,8,128]{2,1,0:T(8,128)(2,1)}), bf16[32,8,128]{2,1,0:T(8,128)(2,1)S(1)}, u32[]{:S(2)}, u32[]{:S(2)}) async-start(bf16[32,8,128]{2,1,0:T(8,128)(2,1)} %bitcast.11), calls=%async_computation.1 | async-start | bytes 131072 | tf_op jit(solution)/shard_map/all_to_all | solution.py:246
  49.0 5.7 %collective-permute-start.2 = (f32[224,128]{1,0:T(8,128)S(1)}, f32[224,128]{1,0:T(8,128)S(1)}, u32[]{:S(2)}, u32[]{:S(2)}) collective-permute-start(f32[224,128]{1,0:T(8,128)S(1)} %get-tuple-element.33), channel_id=1, source_target_pairs={{0,0},{8,256},{16,512},{24,768},{256,8},{264,264},{272,520},{280,7... | collective-permute-start | bytes 344072 | tf_op jit(solution)/shard_map/ppermute | solution.py:252
  54.7 5.2 %collective-permute-done.2.pack_ref = f32[224,128]{1,0:T(8,128)S(1)} collective-permute-done((f32[224,128]{1,0:T(8,128)S(1)}, f32[224,128]{1,0:T(8,128)S(1)}, u32[]{:S(2)}, u32[]{:S(2)}) %collective-permute-start.2) | collective-permute-done | bytes 114720 | tf_op jit(solution)/shard_map/ppermute | solution.py:252
  60.0 1.6 shard_map.115
  61.6 17.0 %all_to_all.46 = f32[32,8,128]{2,1,0:T(8,128)S(1)} all-to-all(f32[32,8,128]{2,1,0:T(8,128)S(1)} %bitcast.50), channel_id=1, replica_groups=mesh['sec'=4,'row'=8,'far'=4,'near'=8] {'sec','near'}, dimensions={0} | all-to-all | bytes 262144 | tf_op jit(solution)/shard_map/all_to_all | solution.py:246
  78.5 0.4 shard_map.116
  78.9 11.5 %all_to_all.47 = bf16[32,8,128]{2,1,0:T(8,128)(2,1)S(1)} all-to-all(bf16[32,8,128]{2,1,0:T(8,128)(2,1)S(1)} %bitcast.53), channel_id=1, replica_groups=mesh['sec'=4,'row'=8,'far'=4,'near'=8] {'sec','near'}, dimensions={0} | all-to-all | bytes 131072 | tf_op jit(solution)/shard_map/all_to_all | solution.py:246
  90.4 1.6 shard_map.117
  92.0 12.5 %all_to_all.48 = f32[32,8,128]{2,1,0:T(8,128)S(1)} all-to-all(f32[32,8,128]{2,1,0:T(8,128)S(1)} %bitcast.48), channel_id=1, replica_groups=mesh['sec'=4,'row'=8,'far'=4,'near'=8] {'sec','near'}, dimensions={0} | all-to-all | bytes 262144 | tf_op jit(solution)/shard_map/all_to_all | solution.py:246
  104.5 0.4 shard_map.118
  104.9 11.4 %all_to_all.49 = bf16[32,8,128]{2,1,0:T(8,128)(2,1)S(1)} all-to-all(bf16[32,8,128]{2,1,0:T(8,128)(2,1)S(1)} %bitcast.54), channel_id=1, replica_groups=mesh['sec'=4,'row'=8,'far'=4,'near'=8] {'sec','near'}, dimensions={0} | all-to-all | bytes 131072 | tf_op jit(solution)/shard_map/all_to_all | solution.py:246
  116.3 1.6 shard_map.119
  117.9 12.5 %all_to_all.50 = f32[32,8,128]{2,1,0:T(8,128)S(1)} all-to-all(f32[32,8,128]{2,1,0:T(8,128)S(1)} %bitcast.49), channel_id=1, replica_groups=mesh['sec'=4,'row'=8,'far'=4,'near'=8] {'sec','near'}, dimensions={0} | all-to-all | bytes 262144 | tf_op jit(solution)/shard_map/all_to_all | solution.py:246
  130.4 0.4 shard_map.120
  130.8 11.4 %all_to_all.51 = bf16[32,8,128]{2,1,0:T(8,128)(2,1)S(1)} all-to-all(bf16[32,8,128]{2,1,0:T(8,128)(2,1)S(1)} %bitcast.52), channel_id=1, replica_groups=mesh['sec'=4,'row'=8,'far'=4,'near'=8] {'sec','near'}, dimensions={0} | all-to-all | bytes 131072 | tf_op jit(solution)/shard_map/all_to_all | solution.py:246
  142.2 1.9 %shard_map.121 = (f32[2,32,128]{2,1,0:T(8,128)S(1)}, f32[128,128]{1,0:T(8,128)}) custom-call(bf16[256,128]{1,0:T(8,128)(2,1)S(1)} %bitcast.40, f32[224,128]{1,0:T(8,128)S(1)} %collective-permute-done.2.pack_ref, f32[3,32,128]{2,1,0:T(8,128)S(1)} %get-tuple-element.46.refs_0_), custom_call_target="tpu_custom_call" | custom-call | tf_op jit(solution)/shard_map/pallas_call | solution.py:234
  144.1 4.5 %all-to-all-start.8 = ((f32[32,4,128]{2,1,0:T(4,128)}), f32[32,4,128]{2,1,0:T(4,128)S(1)}, u32[]{:S(2)}, u32[]{:S(2)}) async-start(f32[32,4,128]{2,1,0:T(4,128)} %bitcast.25), calls=%async_computation.8 | async-start | bytes 131072 | tf_op jit(solution)/shard_map/all_to_all | solution.py:246
  148.7 3.6 %collective-permute-start.4 = (f32[2,32,128]{2,1,0:T(8,128)S(1)}, f32[2,32,128]{2,1,0:T(8,128)S(1)}, u32[]{:S(2)}, u32[]{:S(2)}) collective-permute-start(f32[2,32,128]{2,1,0:T(8,128)S(1)} %get-tuple-element.50), channel_id=1, source_target_pairs={{0,0},{8,256},{16,512},{24,768},{256,8},{264,264},{272,520},{280,7... | collective-permute-start | bytes 98312 | tf_op jit(solution)/shard_map/ppermute | solution.py:252
  152.2 4.2 %all-to-all-done.8 = f32[32,4,128]{2,1,0:T(4,128)S(1)} async-done(((f32[32,4,128]{2,1,0:T(4,128)}), f32[32,4,128]{2,1,0:T(4,128)S(1)}, u32[]{:S(2)}, u32[]{:S(2)}) %all-to-all-start.8) | async-done | bytes 65568 | tf_op jit(solution)/shard_map/all_to_all | solution.py:246
  156.4 0.2 shard_map.122
  156.6 4.3 %collective-permute-start.3 = (f32[64,128]{1,0:T(8,128)S(1)}, f32[64,128]{1,0:T(8,128)S(1)}, u32[]{:S(2)}, u32[]{:S(2)}) collective-permute-start(f32[64,128]{1,0:T(8,128)S(1)} %shard_map.122), channel_id=1, source_target_pairs={{0,0},{8,256},{16,512},{24,768},{256,8},{264,264},{272,520},{280,7... | collective-permute-start | bytes 98312 | tf_op jit(solution)/shard_map/ppermute | solution.py:252
  160.8 0.6 slice_bitcast_fusion
  161.5 3.9 %collective-permute-done.3 = f32[64,128]{1,0:T(8,128)S(1)} collective-permute-done((f32[64,128]{1,0:T(8,128)S(1)}, f32[64,128]{1,0:T(8,128)S(1)}, u32[]{:S(2)}, u32[]{:S(2)}) %collective-permute-start.3) | collective-permute-done | bytes 32800 | tf_op jit(solution)/shard_map/ppermute | solution.py:252
  165.4 0.6 copy.17
  (19 shorter events, 0.1 us)
Async XLA Ops:
  0.6 7.8 %copy-start.1 = (f32[1,4096]{1,0:T(1,128)S(1)}, f32[1,4096]{1,0:T(1,128)}, u32[]{:S(2)}) copy-start(f32[1,4096]{1,0:T(1,128)} %param.10) | copy-start | bytes 49156
  1.4 19.2 %collective-permute-start = (s32[1,32,4]{2,1,0:T(8,128)S(1)}, s32[1,32,4]{2,1,0:T(8,128)S(1)}, u32[]{:S(2)}, u32[]{:S(2)}) collective-permute-start(s32[1,32,4]{2,1,0:T(8,128)S(1)} %copy.12), channel_id=1, source_target_pairs={{0,0},{8,256},{16,512},{24,768},{256,8},{264,264},{272,520},{280,7... | collective-permute-start | bytes 1544 | tf_op jit(solution)/shard_map/ppermute | solution.py:252
  9.2 11.3 %copy-start = (f32[1,4,2,1024]{3,2,1,0:T(2,128)S(1)}, f32[1,4,2,1024]{3,2,1,0:T(2,128)}, u32[]{:S(2)}) copy-start(f32[1,4,2,1024]{3,2,1,0:T(2,128)} %param.9) | copy-start | bytes 98308
  9.2 11.3 %copy-start.2 = (f32[4096]{0:T(1024)S(1)}, f32[4096]{0:T(1024)}, u32[]{:S(2)}) copy-start(f32[4096]{0:T(1024)} %param.11) | copy-start | bytes 49156
  9.2 11.3 %copy-start.3 = (f32[4096]{0:T(1024)S(1)}, f32[4096]{0:T(1024)}, u32[]{:S(2)}) copy-start(f32[4096]{0:T(1024)} %param.12) | copy-start | bytes 49156
  9.3 11.3 %copy-start.4 = (f32[4096]{0:T(1024)S(1)}, f32[4096]{0:T(1024)}, u32[]{:S(2)}) copy-start(f32[4096]{0:T(1024)} %param.13) | copy-start | bytes 49156
  9.3 11.3 %copy-start.5 = (s32[4096]{0:T(1024)S(1)}, s32[4096]{0:T(1024)}, u32[]{:S(2)}) copy-start(s32[4096]{0:T(1024)} %param.15) | copy-start | bytes 49156
  9.3 11.3 %copy-start.6 = (s32[4096]{0:T(1024)S(1)}, s32[4096]{0:T(1024)}, u32[]{:S(2)}) copy-start(s32[4096]{0:T(1024)} %param.16) | copy-start | bytes 49156
  20.7 22.7 %collective-permute-start.1 = (f32[128,128]{1,0:T(8,128)S(1)}, f32[128,128]{1,0:T(8,128)S(1)}, u32[]{:S(2)}, u32[]{:S(2)}) collective-permute-start(f32[128,128]{1,0:T(8,128)S(1)} %get-tuple-element.30), channel_id=1, source_target_pairs={{0,0},{8,256},{16,512},{24,768},{256,8},{264,264},{272,520},{280,7... | collective-permute-start | bytes 196616 | tf_op jit(solution)/shard_map/ppermute | solution.py:252
  44.1 15.8 %all-to-all-start.1 = ((bf16[32,8,128]{2,1,0:T(8,128)(2,1)}), bf16[32,8,128]{2,1,0:T(8,128)(2,1)S(1)}, u32[]{:S(2)}, u32[]{:S(2)}) async-start(bf16[32,8,128]{2,1,0:T(8,128)(2,1)} %bitcast.11), calls=%async_computation.1 | async-start | bytes 131072 | tf_op jit(solution)/shard_map/all_to_all | solution.py:246
  49.0 10.9 %collective-permute-start.2 = (f32[224,128]{1,0:T(8,128)S(1)}, f32[224,128]{1,0:T(8,128)S(1)}, u32[]{:S(2)}, u32[]{:S(2)}) collective-permute-start(f32[224,128]{1,0:T(8,128)S(1)} %get-tuple-element.33), channel_id=1, source_target_pairs={{0,0},{8,256},{16,512},{24,768},{256,8},{264,264},{272,520},{280,7... | collective-permute-start | bytes 344072 | tf_op jit(solution)/shard_map/ppermute | solution.py:252
  144.1 12.3 %all-to-all-start.8 = ((f32[32,4,128]{2,1,0:T(4,128)}), f32[32,4,128]{2,1,0:T(4,128)S(1)}, u32[]{:S(2)}, u32[]{:S(2)}) async-start(f32[32,4,128]{2,1,0:T(4,128)} %bitcast.25), calls=%async_computation.8 | async-start | bytes 131072 | tf_op jit(solution)/shard_map/all_to_all | solution.py:246
  148.7 12.2 %collective-permute-start.4 = (f32[2,32,128]{2,1,0:T(8,128)S(1)}, f32[2,32,128]{2,1,0:T(8,128)S(1)}, u32[]{:S(2)}, u32[]{:S(2)}) collective-permute-start(f32[2,32,128]{2,1,0:T(8,128)S(1)} %get-tuple-element.50), channel_id=1, source_target_pairs={{0,0},{8,256},{16,512},{24,768},{256,8},{264,264},{272,520},{280,7... | collective-permute-start | bytes 98312 | tf_op jit(solution)/shard_map/ppermute | solution.py:252
  156.6 8.8 %collective-permute-start.3 = (f32[64,128]{1,0:T(8,128)S(1)}, f32[64,128]{1,0:T(8,128)S(1)}, u32[]{:S(2)}, u32[]{:S(2)}) collective-permute-start(f32[64,128]{1,0:T(8,128)S(1)} %shard_map.122), channel_id=1, source_target_pairs={{0,0},{8,256},{16,512},{24,768},{256,8},{264,264},{272,520},{280,7... | collective-permute-start | bytes 98312 | tf_op jit(solution)/shard_map/ppermute | solution.py:252

commit v9 on v7

--- a/solution.py
+++ b/solution.py
@@ -337,8 +337,10 @@
         else:
             gas, send = call(update, (gas_shape, send_shape), source, gas, pick, place)
             state = (state,)
-    state = swap(state)
-    gas = swap(gas).reshape(along_x, per_pencil, pencils, LANES)
+    gas, state = lax.optimization_barrier((gas, state))
+    both = swap(jnp.concatenate([gas, state.reshape(2 * lines, LANES)], axis=0))
+    gas, state = both[:blocks], both[blocks:].reshape(2, lines, LANES)
+    gas = gas.reshape(along_x, per_pencil, pencils, LANES)
     return (
         jnp.swapaxes(gas, 1, 2).reshape(gas_field.shape),
         state[OWN].reshape(parcel_state.shape),

time: 158 us -> 158 us (level)
  blocking collectives: 115 us -> 126 us
  starting transfers between devices: 25.6 us -> 15.4 us
    all_to_all x8 -> x9, blocking collectives: 109 us -> 120 us  [exchange(): lax.all_to_all(rows.reshape(shape), GROUP, 0, 0, tiled=True)]
    ppermute x4 -> x3, starting transfers between devices: 21.1 us -> 15.4 us  [swap(): return lax.ppermute(values, ('sec', 'far'), pairs)]
    all_to_all x1 -> x0, starting transfers between devices: 4.5 us -> none  [exchange(): lax.all_to_all(rows.reshape(shape), GROUP, 0, 0, tiled=True)]
    all_to_all x1 -> x0, waiting for transfers between devices: 2.03 us -> none  [exchange(): lax.all_to_all(rows.reshape(shape), GROUP, 0, 0, tiled=True)]
    ppermute x4 -> x3, waiting for transfers between devices: 2.06 us -> 3.39 us  [swap(): return lax.ppermute(values, ('sec', 'far'), pairs)]
  transfers between devices with their start and end apart: 5 -> 3, of which waited for: 2 -> 1; matrix products, arithmetic and copies ran while one was open for 1% -> 0% of each run, Pallas kernels for 0% -> 0%
where the time goes in v9:
time: 158 us; the launch traced here: 157 us
  blocking collectives  126 us (80%)
  starting transfers between devices  15.4 us (10%)
  Pallas kernels  7.81 us (5%)
  waiting for transfers between devices  3.39 us (2%)
  local copies, waits for them, and re-layouts  2.03 us (1%)
    all_to_all x9, blocking collectives, exchange(): lax.all_to_all(rows.reshape(shape), GROUP, 0, 0, tiled=True)  120 us
    ppermute x3, starting transfers between devices, swap(): return lax.ppermute(values, ('sec', 'far'), pairs)  15.4 us
    pallas_call x11, Pallas kernels, call(): pl.pallas_call(body, out_shape=out_shape, in_specs=[smem] * scalars + [vm...  7.81 us
    all_gather x1, blocking collectives, shards(): lax.all_gather(jnp.concatenate([own_gas, own_drop], axis=0), 'sec', axis=...  5.74 us
    ppermute x3, waiting for transfers between devices, swap(): return lax.ppermute(values, ('sec', 'far'), pairs)  3.39 us
  transfers between devices with their start and end apart: 3, of which 1 were waited for; matrix products, arithmetic and copies ran while one was open for 0% of the time, Pallas kernels for 0%

profile of v9, /device:TPU:30, one launch (start us, length us, event | category | flops | bytes accessed | tf_op | source)
XLA Modules:
  0.0 156.9 jit_solution(13887995825605455614)
XLA Ops:
  0.6 0.8 copy.12
  1.4 7.0 %collective-permute-start = (s32[1,32,4]{2,1,0:T(8,128)S(1)}, s32[1,32,4]{2,1,0:T(8,128)S(1)}, u32[]{:S(2)}, u32[]{:S(2)}) collective-permute-start(s32[1,32,4]{2,1,0:T(8,128)S(1)} %copy.12), channel_id=1, source_target_pairs={{0,0},{8,256},{16,512},{24,768},{256,8},{264,264},{272,520},{280,7... | collective-permute-start | bytes 1544 | tf_op jit(solution)/shard_map/ppermute | solution.py:251
  8.5 0.8 pad_maximum_fusion.1
  9.3 0.0 copy-start.4
  9.3 0.0 copy-start.5
  9.3 0.0 copy-start.6
  9.3 5.7 %all_gather.3.temp_ref = f32[384,128]{1,0:T(8,128)S(1)} all-gather(f32[96,128]{1,0:T(8,128)S(1)} %pad_maximum_fusion.1), channel_id=1, replica_groups=mesh['sec'=4,'row'=8,'far'=4,'near'=8] {'sec'}, dimensions={0}, use_global_device_ids=true | all-gather | bytes 245760 | tf_op jit(solution)/shard_map/all_gather | solution.py:280
  15.7 0.0 collective-permute-done.list_ref
  15.8 1.9 %collective-permute-start.1 = (f32[352,128]{1,0:T(8,128)S(1)}, f32[352,128]{1,0:T(8,128)S(1)}, u32[]{:S(2)}, u32[]{:S(2)}) collective-permute-start(f32[352,128]{1,0:T(8,128)S(1)} %shard_map.113), channel_id=1, source_target_pairs={{0,0},{8,256},{16,512},{24,768},{256,8},{264,264},{272,520},{280,7... | collective-permute-start | bytes 540680 | tf_op jit(solution)/shard_map/ppermute | solution.py:251
  17.7 0.2 shard_map.112
  18.0 25.4 %all_to_all.45 = bf16[32,4,128]{2,1,0:T(4,128)(2,1)S(1)} all-to-all(bf16[32,4,128]{2,1,0:T(4,128)(2,1)S(1)} %bitcast.51), channel_id=1, replica_groups=mesh['sec'=4,'row'=8,'far'=4,'near'=8] {'sec','near'}, dimensions={0} | all-to-all | bytes 65536 | tf_op jit(solution)/shard_map/all_to_all | solution.py:245
  43.4 0.2 shard_map.114
  43.5 11.7 %all_to_all.46 = bf16[32,8,128]{2,1,0:T(8,128)(2,1)S(1)} all-to-all(bf16[32,8,128]{2,1,0:T(8,128)(2,1)S(1)} %bitcast.53), channel_id=1, replica_groups=mesh['sec'=4,'row'=8,'far'=4,'near'=8] {'sec','near'}, dimensions={0} | all-to-all | bytes 131072 | tf_op jit(solution)/shard_map/all_to_all | solution.py:245
  55.3 1.6 %shard_map.115 = (f32[3,32,128]{2,1,0:T(8,128)S(1)}, f32[256,128]{1,0:T(8,128)S(1)}) custom-call(bf16[256,128]{1,0:T(8,128)(2,1)S(1)} %bitcast.45, f32[352,128]{1,0:T(8,128)S(1)} %collective-permute-done.1.pack_ref.gas_ref), custom_call_target="tpu_custom_call" | custom-call | tf_op jit(solution)/shard_map/pallas_call | solution.py:233
  56.9 12.6 %all_to_all.47 = f32[32,8,128]{2,1,0:T(8,128)S(1)} all-to-all(f32[32,8,128]{2,1,0:T(8,128)S(1)} %bitcast.50), channel_id=1, replica_groups=mesh['sec'=4,'row'=8,'far'=4,'near'=8] {'sec','near'}, dimensions={0} | all-to-all | bytes 262144 | tf_op jit(solution)/shard_map/all_to_all | solution.py:245
  69.4 0.4 shard_map.116
  69.8 11.4 %all_to_all.48 = bf16[32,8,128]{2,1,0:T(8,128)(2,1)S(1)} all-to-all(bf16[32,8,128]{2,1,0:T(8,128)(2,1)S(1)} %bitcast.57), channel_id=1, replica_groups=mesh['sec'=4,'row'=8,'far'=4,'near'=8] {'sec','near'}, dimensions={0} | all-to-all | bytes 131072 | tf_op jit(solution)/shard_map/all_to_all | solution.py:245
  81.2 1.6 %shard_map.117 = (f32[3,32,128]{2,1,0:T(8,128)S(1)}, f32[256,128]{1,0:T(8,128)S(1)}) custom-call(bf16[256,128]{1,0:T(8,128)(2,1)S(1)} %bitcast.43, f32[352,128]{1,0:T(8,128)S(1)} %collective-permute-done.1.pack_ref.gas_ref, f32[3,32,128]{2,1,0:T(8,128)S(1)} %get-tuple-element.32.refs_0_), custom_call_target="tpu_custom_call" | custom-call | tf_op jit(solution)/shard_map/pallas_call | solution.py:233
  82.8 12.5 %all_to_all.49 = f32[32,8,128]{2,1,0:T(8,128)S(1)} all-to-all(f32[32,8,128]{2,1,0:T(8,128)S(1)} %bitcast.48), channel_id=1, replica_groups=mesh['sec'=4,'row'=8,'far'=4,'near'=8] {'sec','near'}, dimensions={0} | all-to-all | bytes 262144 | tf_op jit(solution)/shard_map/all_to_all | solution.py:245
  95.3 0.4 shard_map.118
  95.7 11.4 %all_to_all.50 = bf16[32,8,128]{2,1,0:T(8,128)(2,1)S(1)} all-to-all(bf16[32,8,128]{2,1,0:T(8,128)(2,1)S(1)} %bitcast.56), channel_id=1, replica_groups=mesh['sec'=4,'row'=8,'far'=4,'near'=8] {'sec','near'}, dimensions={0} | all-to-all | bytes 131072 | tf_op jit(solution)/shard_map/all_to_all | solution.py:245
  107.1 1.6 %shard_map.119 = (f32[3,32,128]{2,1,0:T(8,128)S(1)}, f32[256,128]{1,0:T(8,128)S(1)}) custom-call(bf16[256,128]{1,0:T(8,128)(2,1)S(1)} %bitcast.44, f32[352,128]{1,0:T(8,128)S(1)} %collective-permute-done.1.pack_ref.gas_ref, f32[3,32,128]{2,1,0:T(8,128)S(1)} %get-tuple-element.36.refs_0_), custom_call_target="tpu_custom_call" | custom-call | tf_op jit(solution)/shard_map/pallas_call | solution.py:233
  108.7 12.5 %all_to_all.51 = f32[32,8,128]{2,1,0:T(8,128)S(1)} all-to-all(f32[32,8,128]{2,1,0:T(8,128)S(1)} %bitcast.49), channel_id=1, replica_groups=mesh['sec'=4,'row'=8,'far'=4,'near'=8] {'sec','near'}, dimensions={0} | all-to-all | bytes 262144 | tf_op jit(solution)/shard_map/all_to_all | solution.py:245
  121.2 0.4 shard_map.120
  121.6 11.4 %all_to_all.52 = bf16[32,8,128]{2,1,0:T(8,128)(2,1)S(1)} all-to-all(bf16[32,8,128]{2,1,0:T(8,128)(2,1)S(1)} %bitcast.54), channel_id=1, replica_groups=mesh['sec'=4,'row'=8,'far'=4,'near'=8] {'sec','near'}, dimensions={0} | all-to-all | bytes 131072 | tf_op jit(solution)/shard_map/all_to_all | solution.py:245
  133.0 1.3 shard_map.121
  134.3 11.4 %all_to_all.53 = f32[32,4,128]{2,1,0:T(4,128)S(1)} all-to-all(f32[32,4,128]{2,1,0:T(4,128)S(1)} %bitcast.55), channel_id=1, replica_groups=mesh['sec'=4,'row'=8,'far'=4,'near'=8] {'sec','near'}, dimensions={0} | all-to-all | bytes 131072 | tf_op jit(solution)/shard_map/all_to_all | solution.py:245
  145.7 0.2 shard_map.122
  145.9 6.4 %collective-permute-start.2 = (f32[128,128]{1,0:T(8,128)S(1)}, f32[128,128]{1,0:T(8,128)S(1)}, u32[]{:S(2)}, u32[]{:S(2)}) collective-permute-start(f32[128,128]{1,0:T(8,128)S(1)} %pad_maximum_fusion), channel_id=1, source_target_pairs={{0,0},{8,256},{16,512},{24,768},{256,8},{264,264},{272,520},{280,7... | collective-permute-start | bytes 196616 | tf_op jit(solution)/shard_map/ppermute | solution.py:251
  152.3 3.4 %collective-permute-done.2 = f32[128,128]{1,0:T(8,128)S(1)} collective-permute-done((f32[128,128]{1,0:T(8,128)S(1)}, f32[128,128]{1,0:T(8,128)S(1)}, u32[]{:S(2)}, u32[]{:S(2)}) %collective-permute-start.2) | collective-permute-done | bytes 65568 | tf_op jit(solution)/shard_map/ppermute | solution.py:251
  155.7 0.6 slice.17
  156.3 0.6 slice_bitcast_fusion
  (14 shorter events, 0.1 us)
Async XLA Ops:
  0.6 7.8 %copy-start.1 = (f32[1,4096]{1,0:T(1,128)S(1)}, f32[1,4096]{1,0:T(1,128)}, u32[]{:S(2)}) copy-start(f32[1,4096]{1,0:T(1,128)} %param.10) | copy-start | bytes 49156
  1.4 14.3 %collective-permute-start = (s32[1,32,4]{2,1,0:T(8,128)S(1)}, s32[1,32,4]{2,1,0:T(8,128)S(1)}, u32[]{:S(2)}, u32[]{:S(2)}) collective-permute-start(s32[1,32,4]{2,1,0:T(8,128)S(1)} %copy.12), channel_id=1, source_target_pairs={{0,0},{8,256},{16,512},{24,768},{256,8},{264,264},{272,520},{280,7... | collective-permute-start | bytes 1544 | tf_op jit(solution)/shard_map/ppermute | solution.py:251
  9.2 6.5 %copy-start = (f32[1,4,2,1024]{3,2,1,0:T(2,128)S(1)}, f32[1,4,2,1024]{3,2,1,0:T(2,128)}, u32[]{:S(2)}) copy-start(f32[1,4,2,1024]{3,2,1,0:T(2,128)} %param.9) | copy-start | bytes 98308
  9.2 6.5 %copy-start.2 = (f32[4096]{0:T(1024)S(1)}, f32[4096]{0:T(1024)}, u32[]{:S(2)}) copy-start(f32[4096]{0:T(1024)} %param.11) | copy-start | bytes 49156
  9.2 6.5 %copy-start.3 = (f32[4096]{0:T(1024)S(1)}, f32[4096]{0:T(1024)}, u32[]{:S(2)}) copy-start(f32[4096]{0:T(1024)} %param.12) | copy-start | bytes 49156
  9.3 6.5 %copy-start.4 = (f32[4096]{0:T(1024)S(1)}, f32[4096]{0:T(1024)}, u32[]{:S(2)}) copy-start(f32[4096]{0:T(1024)} %param.13) | copy-start | bytes 49156
  9.3 6.5 %copy-start.5 = (s32[4096]{0:T(1024)S(1)}, s32[4096]{0:T(1024)}, u32[]{:S(2)}) copy-start(s32[4096]{0:T(1024)} %param.15) | copy-start | bytes 49156
  9.3 6.5 %copy-start.6 = (s32[4096]{0:T(1024)S(1)}, s32[4096]{0:T(1024)}, u32[]{:S(2)}) copy-start(s32[4096]{0:T(1024)} %param.16) | copy-start | bytes 49156
  15.8 27.6 %collective-permute-start.1 = (f32[352,128]{1,0:T(8,128)S(1)}, f32[352,128]{1,0:T(8,128)S(1)}, u32[]{:S(2)}, u32[]{:S(2)}) collective-permute-start(f32[352,128]{1,0:T(8,128)S(1)} %shard_map.113), channel_id=1, source_target_pairs={{0,0},{8,256},{16,512},{24,768},{256,8},{264,264},{272,520},{280,7... | collective-permute-start | bytes 540680 | tf_op jit(solution)/shard_map/ppermute | solution.py:251
  145.9 9.8 %collective-permute-start.2 = (f32[128,128]{1,0:T(8,128)S(1)}, f32[128,128]{1,0:T(8,128)S(1)}, u32[]{:S(2)}, u32[]{:S(2)}) collective-permute-start(f32[128,128]{1,0:T(8,128)S(1)} %pad_maximum_fusion), channel_id=1, source_target_pairs={{0,0},{8,256},{16,512},{24,768},{256,8},{264,264},{272,520},{280,7... | collective-permute-start | bytes 196616 | tf_op jit(solution)/shard_map/ppermute | solution.py:251
